TPU v7x, 32 devices: a whole 2x2x4 slice. The times are simulated.
32 devices in a mesh: groups: 2 (over y), page: 8 (over z, core), head: 2 (over x), sub: 1.
Axes of the slice: x: 2, y: 2, z: 4, core: 2. Of those that a mesh axis runs over, the one named last changes fastest.
Arguments:
- queries: bfloat16 [128, 3, 16384], P(('groups', 'page', 'sub'), None, 'head'), parts along dimension 0, may hold values from -400 to 400
- page_keys: bfloat16 [128, 128, 1024], P(('groups', 'page'), None, 'head'), parts along dimension 0, may hold values from -6 to 6
- page_values: bfloat16 [128, 128, 1024], P(('groups', 'page'), None, 'head'), parts along dimension 0, may hold values from -6 to 6
- page_count: int32 [128], P(('groups', 'page')), parts along dimension 0, may hold values from 1 to 128
- leaf_keys: bfloat16 [128, 128, 1024], P(('groups', 'page', 'sub'), None, 'head'), parts along dimension 0, may hold values from -6 to 6
- leaf_values: bfloat16 [128, 128, 1024], P(('groups', 'page', 'sub'), None, 'head'), parts along dimension 0, may hold values from -6 to 6
- leaf_count: int32 [128], P(('groups', 'page', 'sub')), parts along dimension 0, may hold values from 1 to 128
- new_keys: bfloat16 [128, 3, 1024], P(('groups', 'page', 'sub'), None, 'head'), parts along dimension 0, may hold values from -6 to 6
- new_values: bfloat16 [128, 3, 1024], P(('groups', 'page', 'sub'), None, 'head'), parts along dimension 0, may hold values from -6 to 6
- path_owner: int32 [128, 3], P(('groups', 'page', 'sub')), parts along dimension 0, may hold values from 0 to 7, all different within a row; in each aligned block of 8 rows (0 to 7, 8 to 15, ...) at most 6 rows name the same one
- path_slot: int32 [128, 3], P(('groups', 'page', 'sub')), parts along dimension 0, may hold values from 0 to 7
Outputs:
- attended: bfloat16 [128, 3, 16384], P(('groups', 'page', 'sub'), None, 'head'), parts along dimension 0
There are 2 independent parts, one for each index of `groups`. A program takes and returns all parts, laid end to end along the dimension named above; each array names one. Nothing has to cross between parts.
Inputs may be any that keep to these rules, and one draw needn't show every extreme that they name: `path_owner`: each request names 3 different owners; the requests of one device (aligned blocks of 8 requests) name one owner at most 6 times.
All inputs are finite; a program needn't handle non-finite values.
Results may differ from a plain program's by a relative error of at most 0.0047.
Values may be sent and summed in bfloat16 or wider, within the bound.
No kernel may reach another device: no remote copies, remote signals or barrier semaphores. Data moves between devices by JAX's collectives and lax.ppermute only.
A program may use at most 64 MiB of HBM per device.

v0:
```python
import math

import jax
import jax.numpy as jnp
from jax import lax
from jax.sharding import PartitionSpec as P

HD = 128
QH = 128
KVH = 8


def page_states(query_rows, keys, values, counts):
    slot_rows = query_rows.shape[0]
    kv_local = keys.shape[2] // HD
    group_size = QH // KVH
    step_count = query_rows.shape[1] // (kv_local * group_size * HD)
    page_tok = keys.shape[1]
    query_five = query_rows.reshape(slot_rows, step_count, kv_local, group_size, HD)
    key_heads = keys.reshape(slot_rows, page_tok, kv_local, HD)
    value_heads = values.reshape(slot_rows, page_tok, kv_local, HD)
    scores = jnp.einsum(
        "nskgd,ntkd->nskgt", query_five, key_heads, preferred_element_type=jnp.float32
    ) * (1.0 / math.sqrt(HD))
    allowed = jnp.arange(page_tok, dtype=jnp.int32)[None, :] < counts[:, None]
    scores = jnp.where(allowed[:, None, None, None, :], scores, -jnp.inf)
    item_max = jnp.max(scores, axis=-1)
    weights = jnp.exp(scores - item_max[..., None])
    item_total = jnp.sum(weights, axis=-1)
    mixed = jnp.einsum(
        "nskgt,ntkd->nskgd",
        weights.astype(jnp.bfloat16),
        value_heads,
        preferred_element_type=jnp.float32,
    )
    item_out = (mixed / item_total[..., None]).astype(jnp.bfloat16)
    return (
        item_out.reshape(slot_rows, -1),
        item_max.reshape(slot_rows, -1),
        item_total.reshape(slot_rows, -1),
    )


def in_blocks(step_fn, arrays, rows_per_slot):
    owner_count = arrays[0].shape[0]
    slot_width = arrays[0].shape[1]
    wanted_slots = -(-512 // max(1, slot_width * rows_per_slot))
    divisors = [
        candidate
        for candidate in range(1, owner_count + 1)
        if owner_count % candidate == 0 and candidate >= wanted_slots
    ]
    merge_count = min(divisors)
    merged = tuple(
        (
            member.reshape(
                (owner_count // merge_count, merge_count * slot_width) + member.shape[2:]
            )
            for member in arrays
        )
    )
    results = lax.map(step_fn, merged)
    return tuple(
        (member.reshape((owner_count, slot_width) + member.shape[2:]) for member in results)
    )


def shards(
    queries,
    page_keys,
    page_values,
    page_count,
    leaf_keys,
    leaf_values,
    leaf_count,
    new_keys,
    new_values,
    path_owner,
    path_slot,
):
    request_rows, step_count, head_width = queries.shape
    kv_local = page_keys.shape[2] // HD
    group_size = QH // KVH
    page_tok = page_keys.shape[1]
    level_count = path_owner.shape[1]
    owner_count = lax.axis_size("page")
    capacity = max(
        2, min(request_rows, (2 * request_rows * level_count + owner_count - 1) // owner_count)
    )
    score_scale = 1.0 / math.sqrt(HD)
    rows_per_slot = step_count * kv_local * group_size
    item_count = request_rows * level_count
    slot_count = owner_count * capacity
    flat_owner = path_owner.reshape(item_count)
    flat_slot = path_slot.reshape(item_count)
    owner_hot = (flat_owner[:, None] == jnp.arange(owner_count, dtype=jnp.int32)[None, :]).astype(
        jnp.int32
    )
    earlier = jnp.cumsum(owner_hot, axis=0) - owner_hot
    owner_rank = jnp.sum(earlier * owner_hot, axis=1)
    position = flat_owner * capacity + owner_rank
    slot_match = (position[None, :] == jnp.arange(slot_count, dtype=jnp.int32)[:, None]).astype(
        jnp.int32
    )
    item_of_slot = jnp.sum(slot_match * jnp.arange(item_count, dtype=jnp.int32)[None, :], axis=1)
    slot_used = jnp.sum(slot_match, axis=1) > 0
    page_ids = jnp.where(slot_used, jnp.take(flat_slot, item_of_slot, axis=0), 0).reshape(
        owner_count, capacity
    )
    outgoing = jnp.take(queries, item_of_slot // level_count, axis=0).reshape(
        owner_count, capacity, step_count * head_width
    )

    def remote_block(packed):
        block_ids = packed[1]
        return page_states(
            packed[0],
            jnp.take(page_keys, block_ids, axis=0),
            jnp.take(page_values, block_ids, axis=0),
            jnp.take(page_count, block_ids, axis=0),
        )

    states = in_blocks(
        remote_block,
        (
            lax.all_to_all(outgoing, "page", split_axis=0, concat_axis=0, tiled=True),
            lax.all_to_all(page_ids, "page", split_axis=0, concat_axis=0, tiled=True),
        ),
        rows_per_slot,
    )
    out_back = lax.all_to_all(states[0], "page", split_axis=0, concat_axis=0, tiled=True)
    max_back = lax.all_to_all(states[1], "page", split_axis=0, concat_axis=0, tiled=True)
    total_back = lax.all_to_all(states[2], "page", split_axis=0, concat_axis=0, tiled=True)
    item_out = jnp.take(out_back.reshape(slot_count, step_count * head_width), position, axis=0)
    item_out = item_out.astype(jnp.float32).reshape(
        request_rows, level_count, step_count, kv_local, group_size, HD
    )
    item_max = jnp.take(max_back.reshape(slot_count, rows_per_slot), position, axis=0)
    item_max = item_max.reshape(request_rows, level_count, step_count, kv_local, group_size)
    item_total = jnp.take(total_back.reshape(slot_count, rows_per_slot), position, axis=0)
    item_total = item_total.reshape(request_rows, level_count, step_count, kv_local, group_size)
    query_five = queries.reshape(request_rows, step_count, kv_local, group_size, HD)
    leaf_heads = leaf_keys.reshape(request_rows, page_tok, kv_local, HD)
    leaf_value_heads = leaf_values.reshape(request_rows, page_tok, kv_local, HD)
    fresh_heads = new_keys.reshape(request_rows, step_count, kv_local, HD)
    fresh_value_heads = new_values.reshape(request_rows, step_count, kv_local, HD)
    leaf_scores = (
        jnp.einsum("rskgd,rtkd->rskgt", query_five, leaf_heads, preferred_element_type=jnp.float32)
        * score_scale
    )
    leaf_allowed = jnp.arange(page_tok, dtype=jnp.int32)[None, :] < leaf_count[:, None]
    leaf_scores = jnp.where(leaf_allowed[:, None, None, None, :], leaf_scores, -jnp.inf)
    fresh_scores = (
        jnp.einsum("rskgd,rukd->rskgu", query_five, fresh_heads, preferred_element_type=jnp.float32)
        * score_scale
    )
    causal = (
        jnp.arange(step_count, dtype=jnp.int32)[None, :]
        <= jnp.arange(step_count, dtype=jnp.int32)[:, None]
    )
    fresh_scores = jnp.where(causal[None, :, None, None, :], fresh_scores, -jnp.inf)
    local_max = jnp.maximum(jnp.max(leaf_scores, axis=-1), jnp.max(fresh_scores, axis=-1))
    leaf_weights = jnp.exp(leaf_scores - local_max[..., None])
    fresh_weights = jnp.exp(fresh_scores - local_max[..., None])
    local_total = jnp.sum(leaf_weights, axis=-1) + jnp.sum(fresh_weights, axis=-1)
    local_sum = jnp.einsum(
        "rskgt,rtkd->rskgd",
        leaf_weights.astype(jnp.bfloat16),
        leaf_value_heads,
        preferred_element_type=jnp.float32,
    )
    local_sum = local_sum + jnp.einsum(
        "rskgu,rukd->rskgd",
        fresh_weights.astype(jnp.bfloat16),
        fresh_value_heads,
        preferred_element_type=jnp.float32,
    )
    local_out = local_sum / local_total[..., None]
    top_score = jnp.maximum(local_max, jnp.max(item_max, axis=1))
    local_mass = local_total * jnp.exp(local_max - top_score)
    item_mass = item_total * jnp.exp(item_max - top_score[:, None])
    numerator = local_mass[..., None] * local_out + jnp.sum(item_mass[..., None] * item_out, axis=1)
    denominator = local_mass + jnp.sum(item_mass, axis=1)
    return (
        (numerator / denominator[..., None])
        .astype(jnp.bfloat16)
        .reshape(request_rows, step_count, head_width)
    )


def solution(mesh):
    return jax.shard_map(
        shards,
        mesh=mesh,
        in_specs=(
            P(("groups", "page", "sub"), None, "head"),
            P(("groups", "page"), None, "head"),
            P(("groups", "page"), None, "head"),
            P(("groups", "page")),
            P(("groups", "page", "sub"), None, "head"),
            P(("groups", "page", "sub"), None, "head"),
            P(("groups", "page", "sub")),
            P(("groups", "page", "sub"), None, "head"),
            P(("groups", "page", "sub"), None, "head"),
            P(("groups", "page", "sub"), None),
            P(("groups", "page", "sub"), None),
        ),
        out_specs=P(("groups", "page", "sub"), None, "head"),
        check_vma=False,
    )
```

profile of v0, /device:TPU:0, one launch (start us, length us, event | category | flops | bytes accessed | tf_op | source)
XLA Modules:
  0.0 292.9 jit_solution(1077446260876932401)
XLA Ops:
  4.8 6.3 %all-to-all-start = ((s32[8,1,6]{2,1,0:T(1,128)}), s32[8,1,6]{2,1,0:T(1,128)S(1)}, u32[]{:S(2)}, u32[]{:S(2)}) async-start(s32[8,1,6]{2,1,0:T(1,128)} %bitcast.15), calls=%async_computation | async-start | bytes 8192 | tf_op jit(solution)/shard_map/all_to_all | solution.py:127
  11.9 8.4 %gather_fusion.4 = bf16[48,3,8192]{2,0,1:T(8,128)(2,1)S(1)} fusion(bf16[8,3,8192]{2,0,1:T(8,128)(2,1)S(1)} %copy-done, s32[1024]{0:T(1024)S(1)} %get-tuple-element.106), kind=kCustom, calls=%fused_computation.6 | custom fusion | bytes 4718784 | tf_op jit(solution)/shard_map/jit(_take)/gather | solution.py:110
  20.3 3.7 %copy.104 = bf16[48,3,8192]{2,1,0:T(4,128)(2,1)} copy(bf16[48,3,8192]{2,0,1:T(8,128)(2,1)S(1)} %gather_fusion.4) | data formatting | bytes 4718592 | tf_op jit(solution)/shard_map/jit(_take)/gather | solution.py:110
  24.0 6.2 %gather.31 = bf16[8,6,24576]{2,1,0:T(8,128)(2,1)S(1)} reshape(bf16[48,3,8192]{2,1,0:T(4,128)(2,1)} %copy.104) | data formatting | bytes 4718592 | tf_op jit(solution)/shard_map/jit(_take)/gather | solution.py:110
  30.9 2.2 broadcast_select_fusion.3
  33.1 5.2 %all-to-all-start.1 = ((bf16[8,6,24576]{2,1,0:T(8,128)(2,1)}), bf16[8,6,24576]{2,1,0:T(8,128)(2,1)}, u32[]{:S(2)}, u32[]{:S(2)}) async-start(bf16[8,6,24576]{2,1,0:T(8,128)(2,1)} %broadcast_select_fusion.3), calls=%async_computation.1 | async-start | bytes 6291456 | tf_op jit(solution)/shard_map/all_to_all | solution.py:126
  38.4 71.6 %all-to-all-done.1 = bf16[8,6,24576]{2,1,0:T(8,128)(2,1)} async-done(((bf16[8,6,24576]{2,1,0:T(8,128)(2,1)}), bf16[8,6,24576]{2,1,0:T(8,128)(2,1)}, u32[]{:S(2)}, u32[]{:S(2)}) %all-to-all-start.1) | async-done | bytes 2359328 | tf_op jit(solution)/shard_map/all_to_all | solution.py:126
  110.0 77.9 %while.14 = (s32[]{:T(128)}, bf16[8,6,24576]{2,1,0:T(8,128)(2,1)}, f32[8,6,192]{2,1,0:T(8,128)}, f32[8,6,192]{2,1,0:T(8,128)}, s32[8,6]{1,0:T(8,128)S(1)}, /*ind...) while((s32[]{:T(128)}, bf16[8,6,24576]{2,1,0:T(8,128)(2,1)}, ...), condition=%wide.region_11.13_spmd, body=%wide.region_8.12_spmd.sunk | while | flops 77611600 | bytes 16513509 | solution.py:62
  110.7 1.8 gather_fusion.1
  112.5 1.8 gather_fusion.2
  120.4 1.8 gather_fusion.1
  122.2 1.8 gather_fusion.2
  130.1 1.8 gather_fusion.1
  131.9 1.8 gather_fusion.2
  139.8 1.8 gather_fusion.1
  141.7 1.8 gather_fusion.2
  149.6 1.8 gather_fusion.1
  151.4 1.8 gather_fusion.2
  159.3 1.8 gather_fusion.1
  161.1 1.8 gather_fusion.2
  169.0 1.8 gather_fusion.1
  170.9 1.8 gather_fusion.2
  178.8 1.8 gather_fusion.1
  180.6 1.8 gather_fusion.2
  187.8 9.9 %all_to_all.29 = f32[8,6,192]{2,1,0:T(8,128)} all-to-all(f32[8,6,192]{2,1,0:T(8,128)} %get-tuple-element.56), channel_id=1, replica_groups=mesh['groups'=2,'page'=8,'head'=2,'sub'=1] {'page'}, dimensions={0} | all-to-all | bytes 73728 | tf_op jit(solution)/shard_map/all_to_all | solution.py:132
  197.7 9.9 %all_to_all.30 = f32[8,6,192]{2,1,0:T(8,128)} all-to-all(f32[8,6,192]{2,1,0:T(8,128)} %get-tuple-element.57), channel_id=1, replica_groups=mesh['groups'=2,'page'=8,'head'=2,'sub'=1] {'page'}, dimensions={0} | all-to-all | bytes 73728 | tf_op jit(solution)/shard_map/all_to_all | solution.py:133
  207.6 4.6 %all-to-all-start.4 = ((bf16[8,6,24576]{2,1,0:T(8,128)(2,1)}), bf16[8,6,24576]{2,1,0:T(8,128)(2,1)}, u32[]{:S(2)}, u32[]{:S(2)}) async-start(bf16[8,6,24576]{2,1,0:T(8,128)(2,1)} %get-tuple-element.58), calls=%async_computation.4 | async-start | bytes 6291456 | tf_op jit(solution)/shard_map/all_to_all | solution.py:131
  214.4 2.8 fusion.44
  224.6 59.1 %all-to-all-done.4 = bf16[8,6,24576]{2,1,0:T(8,128)(2,1)} async-done(((bf16[8,6,24576]{2,1,0:T(8,128)(2,1)}), bf16[8,6,24576]{2,1,0:T(8,128)(2,1)}, u32[]{:S(2)}, u32[]{:S(2)}) %all-to-all-start.4) | async-done | bytes 2359328 | tf_op jit(solution)/shard_map/all_to_all | solution.py:131
  283.7 2.3 reshape.420
  286.0 2.3 gather_fusion.5
  288.4 1.6 copy.132
  (267 shorter events, 66.4 us)
Async XLA Ops:
  0.0 11.9 %copy-start = (bf16[8,3,8192]{2,0,1:T(8,128)(2,1)S(1)}, bf16[8,3,8192]{2,0,1:T(8,128)(2,1)}, u32[]{:S(2)}) copy-start(bf16[8,3,8192]{2,0,1:T(8,128)(2,1)} %param.17) | copy-start | bytes 1179652
  1.2 10.7 %copy-start.8 = (s32[24]{0:T(128)}, s32[24]{0:T(128)S(1)}, u32[]{:S(2)}) copy-start(s32[24]{0:T(128)S(1)} %select_reduce_fusion.1) | copy-start | bytes 292
  1.8 0.5 copy-start.11
  4.8 28.3 %all-to-all-start = ((s32[8,1,6]{2,1,0:T(1,128)}), s32[8,1,6]{2,1,0:T(1,128)S(1)}, u32[]{:S(2)}, u32[]{:S(2)}) async-start(s32[8,1,6]{2,1,0:T(1,128)} %bitcast.15), calls=%async_computation | async-start | bytes 8192 | tf_op jit(solution)/shard_map/all_to_all | solution.py:127
  33.1 76.9 %copy-start.1 = (s32[8]{0:T(128)S(1)}, s32[8]{0:T(128)}, u32[]{:S(2)}) copy-start(s32[8]{0:T(128)} %param.20) | copy-start | bytes 100
  33.1 76.9 %all-to-all-start.1 = ((bf16[8,6,24576]{2,1,0:T(8,128)(2,1)}), bf16[8,6,24576]{2,1,0:T(8,128)(2,1)}, u32[]{:S(2)}, u32[]{:S(2)}) async-start(bf16[8,6,24576]{2,1,0:T(8,128)(2,1)} %broadcast_select_fusion.3), calls=%async_computation.1 | async-start | bytes 6291456 | tf_op jit(solution)/shard_map/all_to_all | solution.py:126
  207.6 4.6 %copy-start.9 = (s32[24]{0:T(128)S(1)}, s32[24]{0:T(128)}, u32[]{:S(2)}) copy-start(s32[24]{0:T(128)} %copy-done.8) | copy-start | bytes 292
  207.6 4.7 %copy-start.2 = (bf16[8,128,512]{2,1,0:T(8,128)(2,1)S(1)}, bf16[8,128,512]{2,1,0:T(8,128)(2,1)}, u32[]{:S(2)}) copy-start(bf16[8,128,512]{2,1,0:T(8,128)(2,1)} %param.21) | copy-start | bytes 3145732
  207.6 5.0 %copy-start.3 = (bf16[8,128,512]{2,1,0:T(8,128)(2,1)S(1)}, bf16[8,128,512]{2,1,0:T(8,128)(2,1)}, u32[]{:S(2)}) copy-start(bf16[8,128,512]{2,1,0:T(8,128)(2,1)} %param.22) | copy-start | bytes 3145732
  207.6 76.1 %all-to-all-start.4 = ((bf16[8,6,24576]{2,1,0:T(8,128)(2,1)}), bf16[8,6,24576]{2,1,0:T(8,128)(2,1)}, u32[]{:S(2)}, u32[]{:S(2)}) async-start(bf16[8,6,24576]{2,1,0:T(8,128)(2,1)} %get-tuple-element.58), calls=%async_computation.4 | async-start | bytes 6291456 | tf_op jit(solution)/shard_map/all_to_all | solution.py:131
  212.9 5.8 %copy-start.6 = (f32[8,6,192]{2,1,0:T(8,128)S(1)}, f32[8,6,192]{2,1,0:T(8,128)}, u32[]{:S(2)}) copy-start(f32[8,6,192]{2,1,0:T(8,128)} %all_to_all.29) | copy-start | bytes 110596
  212.9 6.4 %copy-start.5 = (f32[8,6,192]{2,1,0:T(8,128)S(1)}, f32[8,6,192]{2,1,0:T(8,128)}, u32[]{:S(2)}) copy-start(f32[8,6,192]{2,1,0:T(8,128)} %all_to_all.30) | copy-start | bytes 110596
  212.9 7.1 %copy-start.10 = (pred[24]{0:T(512)(128)(4,1)S(1)}, pred[24]{0:T(512)(128)(4,1)}, u32[]{:S(2)}) copy-start(pred[24]{0:T(512)(128)(4,1)} %get-tuple-element.88) | copy-start | bytes 76
  288.4 2.5 copy-start.4
  288.4 2.5 copy-start.7
  288.4 2.5 copy-start.12
where the time goes:
time: 295 us; the launch traced here: 293 us
  waiting for transfers between devices  131 us (44%)
  local copies, waits for them, and re-layouts  93.2 us (32%)
  blocking collectives  19.7 us (7%)
  starting transfers between devices  16.1 us (5%)
  other arithmetic  16 us (5%)
  matrix products  16 us (5%)
    all_to_all x1, waiting for transfers between devices, shards(): lax.all_to_all(outgoing, 'page', split_axis=0, concat_axis=0, tiled=True)  71.6 us
    all_to_all x1, waiting for transfers between devices, shards(): lax.all_to_all(states[0], 'page', split_axis=0, concat_axis=0, tiled=True)  59.1 us
    gather x3, local copies, waits for them, and re-layouts, shards(): jnp.take(queries, item_of_slot // level_count, axis=0)  18.3 us
    gather x8, local copies, waits for them, and re-layouts, remote_block(): jnp.take(page_values, block_ids, axis=0)  14.6 us
    gather x8, local copies, waits for them, and re-layouts, remote_block(): jnp.take(page_keys, block_ids, axis=0)  14.6 us
    dynamic_update_slice x16, local copies, waits for them, and re-layouts, in_blocks(): results = lax.map(step_fn, merged)  11.1 us
    all_to_all x1, blocking collectives, shards(): lax.all_to_all(states[2], 'page', split_axis=0, concat_axis=0, tiled=True)  9.87 us
    all_to_all x1, blocking collectives, shards(): lax.all_to_all(states[1], 'page', split_axis=0, concat_axis=0, tiled=True)  9.87 us
  transfers between devices with their start and end apart: 3, of which 2 were waited for; matrix products, arithmetic and copies ran while one was open for 12% of the time, Pallas kernels for 0%

commit v1 on v0

--- a/solution.py
+++ b/solution.py
@@ -1,8 +1,11 @@
+import functools
 import math
 
 import jax
 import jax.numpy as jnp
 from jax import lax
+from jax.experimental import pallas as pl
+from jax.experimental.pallas import tpu as pltpu
 from jax.sharding import PartitionSpec as P
 
 HD = 128
@@ -188,9 +191,338 @@
     )
 
 
+NEG = -3e38
+CORES = 2
+
+
+def packed_stats(tile):
+    return tile + pltpu.roll(tile, tile.shape[1] - 1, 1)
+
+
+def put_lane(tile, lane_ids, lane, column):
+    return jnp.where(lane_ids == lane, column, tile)
+
+
+def two_pieces(column):
+    high = column.astype(jnp.bfloat16).astype(jnp.float32)
+    low = (column - high).astype(jnp.bfloat16).astype(jnp.float32)
+    return high, low
+
+
+def dot_nt(a, b):
+    return lax.dot_general(a, b, (((1,), (1,)), ((), ())), preferred_element_type=jnp.float32)
+
+
+def dot_nn(a, b):
+    return lax.dot_general(a, b, (((1,), (0,)), ((), ())), preferred_element_type=jnp.float32)
+
+
+def plain_call(kernel, out_shape, in_memory, scratch=(), flops=0, num_bytes=0, exps=0):
+    return pl.pallas_call(
+        kernel,
+        out_shape=out_shape,
+        in_specs=[pl.BlockSpec(memory_space=space) for space in in_memory],
+        out_specs=jax.tree.map(lambda _: pl.BlockSpec(memory_space=pltpu.VMEM), out_shape),
+        scratch_shapes=list(scratch),
+        compiler_params=pltpu.CompilerParams(vmem_limit_bytes=32 * 1024 * 1024),
+        cost_estimate=pl.CostEstimate(flops=flops, bytes_accessed=num_bytes, transcendentals=exps),
+    )
+
+
+class Sizes:
+    def __init__(self, requests, steps, kv, group, levels, pages, page_tok, owners):
+        self.requests, self.steps, self.kv, self.group = requests, steps, kv, group
+        self.levels, self.pages, self.page_tok, self.owners = levels, pages, page_tok, owners
+        self.rows = steps * group
+        self.step_rows = kv * group
+        self.all_rows = requests * steps * kv * group
+        self.tile_count = -(-requests * kv * 4 // HD)
+        self.stat_rows = self.tile_count * self.rows
+        self.table = pages + 2 * requests * levels
+        self.scale = 1.0 / math.sqrt(HD)
+
+    def head_rows(self, ref, request, head):
+        base = request * (self.steps * self.step_rows) + head * self.group
+        return jnp.concatenate(
+            [ref[pl.ds(base + step * self.step_rows, self.group), :] for step in range(self.steps)],
+            axis=0,
+        )
+
+    def put_rows(self, ref, request, head, value):
+        base = request * (self.steps * self.step_rows) + head * self.group
+        for step in range(self.steps):
+            ref[pl.ds(base + step * self.step_rows, self.group), :] = value[
+                step * self.group : (step + 1) * self.group
+            ].astype(ref.dtype)
+
+    def find(self, table_ref, source, owner, request):
+        base = source * self.table + self.pages + request * self.levels
+        slot = jnp.int32(0)
+        used = jnp.int32(0)
+        for level in range(self.levels):
+            hit = table_ref[base + level] == owner
+            slot = jnp.where(hit, table_ref[base + self.requests * self.levels + level], slot)
+            used = jnp.where(hit, 1, used)
+        return slot, used * table_ref[owner * self.table + slot]
+
+
+def shared_kernel(sz, hop, exact, table_ref, q_ref, k0, v0, k1, v1, *outs):
+    num_ref, stat_ref = outs if exact else (outs[0], None)
+    me = lax.axis_index("page")
+    source = jnp.bitwise_xor(me, hop)
+    mate = jnp.bitwise_xor(me, 1)
+    lane_ids = lax.broadcasted_iota(jnp.int32, (sz.rows, HD), 1)
+    token_ids = lax.broadcasted_iota(jnp.int32, (sz.rows, sz.page_tok), 1)
+    per_tile = HD // (4 * sz.kv)
+    empty = jnp.where(lane_ids % 4 == 0, NEG, 0.0).astype(jnp.bfloat16).astype(jnp.float32)
+    for tile_at in range(sz.tile_count):
+
+        def one(request, tile):
+            slot0, count0 = sz.find(table_ref, source, me, request)
+            slot1, count1 = sz.find(table_ref, source, mate, request)
+
+            def work(tile):
+                for head in range(sz.kv):
+                    cols = slice(head * HD, (head + 1) * HD)
+                    q = sz.head_rows(q_ref, request, head)
+                    s0 = dot_nt(q, k0[slot0, :, cols]) * sz.scale
+                    s1 = dot_nt(q, k1[slot1, :, cols]) * sz.scale
+                    s0 = jnp.where(token_ids < count0, s0, NEG)
+                    s1 = jnp.where(token_ids < count1, s1, NEG)
+                    top = jnp.max(jnp.maximum(s0, s1), axis=1, keepdims=True)
+                    high, low = two_pieces(top)
+                    point = high + low
+                    w0 = jnp.exp(s0 - point)
+                    w1 = jnp.exp(s1 - point)
+                    total = jnp.sum(w0 + w1, axis=1, keepdims=True)
+                    num = dot_nn(w0.astype(jnp.bfloat16), v0[slot0, :, cols]) + dot_nn(
+                        w1.astype(jnp.bfloat16), v1[slot1, :, cols]
+                    )
+                    sz.put_rows(num_ref, request, head, num)
+                    total_high, total_low = two_pieces(total)
+                    lane = ((request - tile_at * per_tile) * sz.kv + head) * 4
+                    for piece_at, piece in enumerate((high, low, total_high, total_low)):
+                        tile = put_lane(tile, lane_ids, lane + piece_at, piece)
+                return tile
+
+            def skip(tile):
+                for head in range(sz.kv):
+                    sz.put_rows(num_ref, request, head, jnp.zeros((sz.rows, HD), jnp.float32))
+                return tile
+
+            return lax.cond(count0 + count1 > 0, work, skip, tile)
+
+        last = min(sz.requests, (tile_at + 1) * per_tile)
+        tile = lax.fori_loop(tile_at * per_tile, last, one, empty)
+        span = pl.ds(tile_at * sz.rows, sz.rows)
+        if exact:
+            stat_ref[span, :] = tile
+        else:
+            num_ref[pl.ds(sz.all_rows + tile_at * sz.rows, sz.rows), :] = tile.astype(jnp.bfloat16)
+
+
+def local_kernel(
+    sz, table_ref, leaf_count_ref, q_ref, k0, v0, k1, v1, leaf_k, leaf_v, new_k, new_v, num_ref, stat_ref
+):
+    me = lax.axis_index("page")
+    mate = jnp.bitwise_xor(me, 1)
+    lane_ids = lax.broadcasted_iota(jnp.int32, (sz.rows, HD), 1)
+    token_ids = lax.broadcasted_iota(jnp.int32, (sz.rows, sz.page_tok), 1)
+    fresh = new_k.shape[0]
+    fresh_ids = lax.broadcasted_iota(jnp.int32, (sz.rows, fresh), 1)
+    step_ids = lax.broadcasted_iota(jnp.int32, (sz.rows, fresh), 0) // sz.group
+    per_tile = HD // (4 * sz.kv)
+    for tile_at in range(sz.tile_count):
+
+        def one(request, tile):
+            slot0, count0 = sz.find(table_ref, me, me, request)
+            slot1, count1 = sz.find(table_ref, me, mate, request)
+            count2 = leaf_count_ref[request]
+            first = request * sz.steps
+            for head in range(sz.kv):
+                cols = slice(head * HD, (head + 1) * HD)
+                q = sz.head_rows(q_ref, request, head)
+                keys = (k0[slot0, :, cols], k1[slot1, :, cols], leaf_k[request, :, cols])
+                values = (
+                    v0[slot0, :, cols],
+                    v1[slot1, :, cols],
+                    leaf_v[request, :, cols],
+                    new_v[:, cols],
+                )
+                scores = [
+                    jnp.where(token_ids < count, dot_nt(q, key) * sz.scale, NEG)
+                    for key, count in zip(keys, (count0, count1, count2))
+                ]
+                allowed = (fresh_ids >= first) & (fresh_ids <= first + step_ids)
+                scores.append(jnp.where(allowed, dot_nt(q, new_k[:, cols]) * sz.scale, NEG))
+                top = jnp.maximum(scores[0], scores[1])
+                top = jnp.max(jnp.maximum(top, scores[2]), axis=1, keepdims=True)
+                top = jnp.maximum(top, jnp.max(scores[3], axis=1, keepdims=True))
+                weights = [jnp.exp(score - top) for score in scores]
+                total = jnp.sum(weights[0] + weights[1] + weights[2], axis=1, keepdims=True)
+                total = total + jnp.sum(weights[3], axis=1, keepdims=True)
+                num = sum(
+                    dot_nn(weight.astype(jnp.bfloat16), value)
+                    for weight, value in zip(weights, values)
+                )
+                sz.put_rows(num_ref, request, head, num)
+                lane = ((request - tile_at * per_tile) * sz.kv + head) * 4
+                tile = put_lane(tile, lane_ids, lane, top)
+                tile = put_lane(tile, lane_ids, lane + 2, total)
+            return tile
+
+        last = min(sz.requests, (tile_at + 1) * per_tile)
+        tile = lax.fori_loop(
+            tile_at * per_tile, last, one, jnp.zeros((sz.rows, HD), jnp.float32)
+        )
+        stat_ref[pl.ds(tile_at * sz.rows, sz.rows), :] = tile
+
+
+def merge_kernel(sz, num_ref, stat_ref, came_ref, out_ref):
+    lane_ids = lax.broadcasted_iota(jnp.int32, (sz.rows, HD), 1)
+    per_tile = HD // (4 * sz.kv)
+    for tile_at in range(sz.tile_count):
+        span = pl.ds(tile_at * sz.rows, sz.rows)
+        came_span = pl.ds(sz.all_rows + tile_at * sz.rows, sz.rows)
+        mine = packed_stats(stat_ref[span, :])
+        came = packed_stats(came_ref[came_span, :].astype(jnp.float32))
+        top = jnp.maximum(mine, came)
+        keep, add = jnp.exp(mine - top), jnp.exp(came - top)
+        total = mine * pltpu.roll(keep, 2, 1) + came * pltpu.roll(add, 2, 1)
+        high, low = two_pieces(top)
+        total_high, total_low = two_pieces(total)
+        kind = lane_ids % 4
+        tile = jnp.where(kind == 0, high, pltpu.roll(low, 1, 1))
+        tile = jnp.where(kind == 2, total_high, tile)
+        tile = jnp.where(kind == 3, pltpu.roll(total_low, 1, 1), tile)
+        out_ref[came_span, :] = tile.astype(jnp.bfloat16)
+        for request in range(tile_at * per_tile, min(sz.requests, (tile_at + 1) * per_tile)):
+            for head in range(sz.kv):
+                lane = ((request - tile_at * per_tile) * sz.kv + head) * 4
+                joined = sz.head_rows(num_ref, request, head) * keep[:, lane : lane + 1]
+                joined = joined + (
+                    sz.head_rows(came_ref, request, head).astype(jnp.float32)
+                    * add[:, lane : lane + 1]
+                )
+                sz.put_rows(out_ref, request, head, joined)
+
+
+def final_kernel(sz, num_ref, stat_ref, near_ref, far_ref, out_ref):
+    per_tile = HD // (4 * sz.kv)
+    for tile_at in range(sz.tile_count):
+        span = pl.ds(tile_at * sz.rows, sz.rows)
+        came_span = pl.ds(sz.all_rows + tile_at * sz.rows, sz.rows)
+        mine = stat_ref[span, :]
+        near = packed_stats(near_ref[came_span, :].astype(jnp.float32))
+        far = packed_stats(far_ref[came_span, :].astype(jnp.float32))
+        top = jnp.maximum(jnp.maximum(mine, near), far)
+        parts = [jnp.exp(one - top) for one in (mine, near, far)]
+        total = sum(
+            one * pltpu.roll(part, 2, 1) for one, part in zip((mine, near, far), parts)
+        )
+        total = pltpu.roll(total, HD - 2, 1)
+        parts = [part / total for part in parts]
+        for request in range(tile_at * per_tile, min(sz.requests, (tile_at + 1) * per_tile)):
+            for head in range(sz.kv):
+                lane = ((request - tile_at * per_tile) * sz.kv + head) * 4
+                joined = sum(
+                    sz.head_rows(ref, request, head).astype(jnp.float32) * part[:, lane : lane + 1]
+                    for ref, part in zip((num_ref, near_ref, far_ref), parts)
+                )
+                sz.put_rows(out_ref, request, head, joined)
+
+
+def line_shards(
+    queries,
+    page_keys,
+    page_values,
+    page_count,
+    leaf_keys,
+    leaf_values,
+    leaf_count,
+    new_keys,
+    new_values,
+    path_owner,
+    path_slot,
+):
+    requests, steps, width = queries.shape
+    owners = lax.axis_size("page")
+    sz = Sizes(
+        requests,
+        steps,
+        page_keys.shape[2] // HD,
+        QH // KVH,
+        path_owner.shape[1],
+        page_keys.shape[0],
+        page_keys.shape[1],
+        owners,
+    )
+
+    def exchange(array, hop):
+        return lax.ppermute(array, "page", [(at, at ^ hop) for at in range(owners)])
+
+    near, far = CORES, owners - CORES
+    table = jnp.concatenate([page_count, path_owner.reshape(-1), path_slot.reshape(-1)])
+    table = lax.all_gather(table, "page", tiled=True)
+    block = queries.reshape(sz.all_rows, HD)
+    far_q = exchange(block, far)
+    near_q = exchange(block, near)
+    mate_keys = exchange(page_keys, 1)
+    mate_values = exchange(page_values, 1)
+
+    smem, vmem = pltpu.SMEM, pltpu.VMEM
+    sent = jax.ShapeDtypeStruct((sz.all_rows + sz.stat_rows, HD), jnp.bfloat16)
+    exact = (
+        jax.ShapeDtypeStruct((sz.all_rows, HD), jnp.float32),
+        jax.ShapeDtypeStruct((sz.stat_rows, HD), jnp.float32),
+    )
+    pages = (page_keys, page_values, mate_keys, mate_values)
+    flops = sz.all_rows * HD * sz.page_tok * 8
+    page_bytes = 4 * page_keys.size * 2 + sz.all_rows * HD * 4
+
+    def shared(hop, is_exact, block):
+        return plain_call(
+            functools.partial(shared_kernel, sz, hop, is_exact),
+            exact if is_exact else (sent,),
+            [smem] + [vmem] * 5,
+            flops=flops,
+            num_bytes=page_bytes,
+        )(table, block, *pages)
+
+    fresh_rows = -(-requests * steps // HD) * HD
+    pad = ((0, fresh_rows - requests * steps), (0, 0))
+    fresh_keys = jnp.pad(new_keys.reshape(requests * steps, -1), pad)
+    fresh_values = jnp.pad(new_values.reshape(requests * steps, -1), pad)
+    local_num, local_stat = plain_call(
+        functools.partial(local_kernel, sz),
+        exact,
+        [smem, smem] + [vmem] * 9,
+        flops=flops * 2,
+        num_bytes=page_bytes * 2,
+    )(table, leaf_count, block, *pages, leaf_keys, leaf_values, fresh_keys, fresh_values)
+    (near_part,) = shared(near, False, near_q)
+    far_num, far_stat = shared(far, True, far_q)
+    cross_q = exchange(far_q, near)
+    (cross_part,) = shared(near ^ far, False, cross_q)
+    cross_back = exchange(cross_part, near)
+    (far_part,) = plain_call(
+        functools.partial(merge_kernel, sz), (sent,), [vmem] * 3, num_bytes=sz.all_rows * HD * 8
+    )(far_num, far_stat, cross_back)
+    far_back = exchange(far_part, far)
+    near_back = exchange(near_part, near)
+    (out,) = plain_call(
+        functools.partial(final_kernel, sz),
+        (jax.ShapeDtypeStruct((sz.all_rows, HD), jnp.bfloat16),),
+        [vmem] * 4,
+        num_bytes=sz.all_rows * HD * 10,
+    )(local_num, local_stat, near_back, far_back)
+    return out.reshape(requests, steps, width)
+
+
 def solution(mesh):
+    on_line = mesh.shape["sub"] == 1 and mesh.shape["page"] == 4 * CORES
     return jax.shard_map(
-        shards,
+        line_shards if on_line else shards,
         mesh=mesh,
         in_specs=(
             P(("groups", "page", "sub"), None, "head"),

time: 295 us -> 108 us (0.37)
  the two profiles are of different devices: /device:TPU:0 before, /device:TPU:4 now
where the time goes in v1:
time: 108 us; the launch traced here: 109 us
  Pallas kernels  44.3 us (41%)
  local copies, waits for them, and re-layouts  18.8 us (17%)
  blocking collectives  18 us (17%)
  starting transfers between devices  17.1 us (16%)
  waiting for transfers between devices  9.57 us (9%)
    pallas_call x3, Pallas kernels, shared(): plain_call(functools.partial(shared_kernel, sz, hop, is_exact), exact if...  29.2 us
    unnamed x1, blocking collectives  18 us
    ppermute x8, starting transfers between devices, exchange(): return lax.ppermute(array, 'page', [(at, at ^ hop) for at in range(owners)])  17.1 us
    unnamed x35, local copies, waits for them, and re-layouts  12.3 us
    pallas_call x1, Pallas kernels, line_shards(): plain_call(functools.partial(local_kernel, sz), exact, [smem, smem] + [vm...  11.6 us
    ppermute x8, waiting for transfers between devices, exchange(): return lax.ppermute(array, 'page', [(at, at ^ hop) for at in range(owners)])  9.57 us
  transfers between devices with their start and end apart: 8, of which 1 were waited for; matrix products, arithmetic and copies ran while one was open for 9% of the time, Pallas kernels for 39%

profile of v1, /device:TPU:4, one launch (start us, length us, event | category | flops | bytes accessed | tf_op | source)
XLA Modules:
  0.0 108.8 jit_solution(9078254531181048112)
XLA Ops:
  0.0 0.5 collective-permute-start.1
  0.5 2.1 %copy.20 = bf16[8,3,8192]{2,1,0:T(4,128)(2,1)} copy(bf16[8,3,8192]{2,0,1:T(8,128)(2,1)} %param.11) | data formatting | bytes 786432 | tf_op args[0]
  2.7 1.6 %reshape.20.q_ref = bf16[1536,128]{1,0:T(8,128)(2,1)S(1)} reshape(bf16[8,3,8192]{2,1,0:T(4,128)(2,1)} %copy.20) | data formatting | bytes 786432 | tf_op jit(solution)/shard_map/reshape | solution.py:467
  4.3 3.7 %collective-permute-start.4 = (bf16[1536,128]{1,0:T(8,128)(2,1)S(1)}, bf16[1536,128]{1,0:T(8,128)(2,1)}, u32[]{:S(2)}, u32[]{:S(2)}) collective-permute-start(bf16[1536,128]{1,0:T(8,128)(2,1)S(1)} %reshape.20.q_ref), channel_id=1, source_target_pairs={{0,12},{2,14},{4,8},{6,10},{8,4},{10,6},{12,0},{14,2},{1,13},{3,15... | collective-permute-start | bytes 1179656 | tf_op jit(solution)/shard_map/ppermute | solution.py:462
  7.9 9.6 %collective-permute-done.4.q_ref = bf16[1536,128]{1,0:T(8,128)(2,1)} collective-permute-done((bf16[1536,128]{1,0:T(8,128)(2,1)S(1)}, bf16[1536,128]{1,0:T(8,128)(2,1)}, u32[]{:S(2)}, u32[]{:S(2)}) %collective-permute-start.4) | collective-permute-done | bytes 393248 | tf_op jit(solution)/shard_map/ppermute | solution.py:462
  17.5 8.0 %collective-permute-start.5 = (bf16[1536,128]{1,0:T(8,128)(2,1)}, bf16[1536,128]{1,0:T(8,128)(2,1)}, u32[]{:S(2)}, u32[]{:S(2)}) collective-permute-start(bf16[1536,128]{1,0:T(8,128)(2,1)} %collective-permute-done.4.q_ref), channel_id=1, source_target_pairs={{0,4},{2,6},{4,0},{6,2},{8,12},{10,14},{12,8},{14,10},{1,5},{3,7},... | collective-permute-start | bytes 1179656 | tf_op jit(solution)/shard_map/ppermute | solution.py:462
  25.7 0.6 copy-done.11
  26.4 0.1 reshape.19
  26.5 0.7 copy-done.13
  27.1 0.6 dynamic-slice
  28.4 0.6 copy-done.12
  29.0 0.2 add_dynamic-update-slice_fusion
  29.2 18.0 %all-reduce.2.table_ref = s32[448]{0:T(512)S(1)} all-reduce(s32[448]{0:T(512)S(1)} %add_dynamic-update-slice_fusion), channel_id=1, replica_groups=mesh['groups'=2,'page'=8,'head'=2,'sub'=1] {'page'}, use_global_device_ids=true, to_apply=%add.2 | all-reduce | flops 448 | bytes 3584
  47.2 1.2 %copy-done.1 = bf16[8,128,512]{2,1,0:T(8,128)(2,1)S(1)} copy-done((bf16[8,128,512]{2,1,0:T(8,128)(2,1)S(1)}, bf16[8,128,512]{2,1,0:T(8,128)(2,1)}, u32[]{:S(2)}) %copy-start.1) | copy-done | bytes 1048600
  48.4 9.7 %shard_map.112 = bf16[1584,128]{1,0:T(8,128)(2,1)S(1)} custom-call(s32[448]{0:T(512)S(1)} %all-reduce.2.table_ref, bf16[1536,128]{1,0:T(8,128)(2,1)} %collective-permute-done.5.q_ref, bf16[8,128,512]{2,1,0:T(8,128)(2,1)S(1)} %copy-done, bf16[8,128,512]{2,1,0:T(8,128)(2,1)S(1)} %copy-done.1, bf16[8,128,512]{2,1,0:T(8,128)(2,1)S(1)} %collective-permute-done.k1, ...), custom_call_target="tpu_custom_call" | custom-call | flops 201326592 | bytes 4980736 | tf_op jit(solution)/shard_map/pallas_call | solution.py:484
  58.2 10.2 %shard_map.110 = bf16[1584,128]{1,0:T(8,128)(2,1)} custom-call(s32[448]{0:T(512)S(1)} %all-reduce.2.table_ref, bf16[1536,128]{1,0:T(8,128)(2,1)} %collective-permute-done.2.q_ref, bf16[8,128,512]{2,1,0:T(8,128)(2,1)S(1)} %copy-done, bf16[8,128,512]{2,1,0:T(8,128)(2,1)S(1)} %copy-done.1, bf16[8,128,512]{2,1,0:T(8,128)(2,1)S(1)} %collective-permute-done.k1, ...), custom_call_target="tpu_custom_call" | custom-call | flops 201326592 | bytes 4980736 | tf_op jit(solution)/shard_map/pallas_call | solution.py:484
  68.4 9.4 %shard_map.111 = (f32[1536,128]{1,0:T(8,128)S(1)}, f32[48,128]{1,0:T(8,128)S(1)}) custom-call(s32[448]{0:T(512)S(1)} %all-reduce.2.table_ref, bf16[1536,128]{1,0:T(8,128)(2,1)} %collective-permute-done.4.q_ref, bf16[8,128,512]{2,1,0:T(8,128)(2,1)S(1)} %copy-done, bf16[8,128,512]{2,1,0:T(8,128)(2,1)S(1)} %copy-done.1, ...), custom_call_target="tpu_custom_call" | custom-call | flops 201326592 | bytes 4980736 | tf_op jit(solution)/shard_map/pallas_call | solution.py:484
  77.8 1.4 %shard_map.113 = bf16[1584,128]{1,0:T(8,128)(2,1)} custom-call(f32[1536,128]{1,0:T(8,128)S(1)} %get-tuple-element.11.num_ref, f32[48,128]{1,0:T(8,128)S(1)} %get-tuple-element.12.stat_ref, bf16[1584,128]{1,0:T(8,128)(2,1)S(1)} %collective-permute-done.6.came_ref), custom_call_target="tpu_custom_call" | custom-call | bytes 1572864 | tf_op jit(solution)/shard_map/pallas_call | solution.py:508
  79.2 4.8 %collective-permute-start.7 = (bf16[1584,128]{1,0:T(8,128)(2,1)}, bf16[1584,128]{1,0:T(8,128)(2,1)}, u32[]{:S(2)}, u32[]{:S(2)}) collective-permute-start(bf16[1584,128]{1,0:T(8,128)(2,1)} %shard_map.113), channel_id=1, source_target_pairs={{0,12},{2,14},{4,8},{6,10},{8,4},{10,6},{12,0},{14,2},{1,13},{3,15... | collective-permute-start | bytes 1216520 | tf_op jit(solution)/shard_map/ppermute | solution.py:462
  84.0 0.6 copy.21
  84.7 1.4 %reshape.21 = bf16[24,512]{1,0:T(8,128)(2,1)} reshape(bf16[8,3,512]{2,1,0:T(4,128)(2,1)} %copy.21) | data formatting | bytes 49152 | tf_op jit(solution)/shard_map/reshape | solution.py:494
  86.1 1.4 %copy.22 = bf16[8,3,512]{2,1,0:T(4,128)(2,1)} copy(bf16[8,3,512]{2,0,1:T(8,128)(2,1)} %param.19) | data formatting | bytes 49152 | tf_op args[8]
  87.4 1.4 %reshape.22 = bf16[24,512]{1,0:T(8,128)(2,1)} reshape(bf16[8,3,512]{2,1,0:T(4,128)(2,1)} %copy.22) | data formatting | bytes 49152 | tf_op jit(solution)/shard_map/reshape | solution.py:495
  88.8 0.8 pad.7.new_k
  89.6 0.6 copy-done.7
  90.2 1.2 %copy-done.4 = bf16[8,128,512]{2,1,0:T(8,128)(2,1)S(1)} copy-done((bf16[8,128,512]{2,1,0:T(8,128)(2,1)S(1)}, bf16[8,128,512]{2,1,0:T(8,128)(2,1)}, u32[]{:S(2)}) %copy-start.4) | copy-done | bytes 1048600
  91.5 1.2 %copy-done.5 = bf16[8,128,512]{2,1,0:T(8,128)(2,1)S(1)} copy-done((bf16[8,128,512]{2,1,0:T(8,128)(2,1)S(1)}, bf16[8,128,512]{2,1,0:T(8,128)(2,1)}, u32[]{:S(2)}) %copy-start.5) | copy-done | bytes 1048600
  92.7 1.2 %copy-done.6 = bf16[8,128,512]{2,1,0:T(8,128)(2,1)S(1)} copy-done((bf16[8,128,512]{2,1,0:T(8,128)(2,1)S(1)}, bf16[8,128,512]{2,1,0:T(8,128)(2,1)}, u32[]{:S(2)}) %copy-start.6) | copy-done | bytes 1048600
  93.9 11.6 %shard_map.109 = (f32[1536,128]{1,0:T(8,128)S(1)}, f32[48,128]{1,0:T(8,128)S(1)}) custom-call(s32[448]{0:T(512)S(1)} %all-reduce.2.table_ref, s32[8]{0:T(128)S(1)} %copy-done.7, bf16[1536,128]{1,0:T(8,128)(2,1)S(1)} %reshape.20.q_ref, bf16[8,128,512]{2,1,0:T(8,128)(2,1)S(1)} %copy-done, bf16[8,128,512]{2,1,0:T(8,128)(2,1)S(1)} %copy-done.2, ...), custom_call_target="tpu_custom_call" | custom-call | flops 402653184 | bytes 9961472 | tf_op jit(solution)/shard_map/pallas_call | solution.py:496
  105.5 2.1 %shard_map.114 = bf16[1536,128]{1,0:T(8,128)(2,1)S(1)} custom-call(f32[1536,128]{1,0:T(8,128)S(1)} %get-tuple-element.9.num_ref, f32[48,128]{1,0:T(8,128)S(1)} %get-tuple-element.10.stat_ref, bf16[1584,128]{1,0:T(8,128)(2,1)} %collective-permute-done.3.near_ref, bf16[1584,128]{1,0:T(8,128)(2,1)} %collective-permute-done.7.far_ref), custom_call_target="tpu_custom_call" | custom-call | bytes 1966080 | tf_op jit(solution)/shard_map/pallas_call | solution.py:513
  107.6 0.1 reshape.23
  107.7 1.0 copy.23
  (36 shorter events, 0.4 us)
Async XLA Ops:
  0.0 47.2 %copy-start = (bf16[8,128,512]{2,1,0:T(8,128)(2,1)S(1)}, bf16[8,128,512]{2,1,0:T(8,128)(2,1)}, u32[]{:S(2)}) copy-start(bf16[8,128,512]{2,1,0:T(8,128)(2,1)} %k0.7) | copy-start | bytes 3145732
  0.0 47.2 %collective-permute-start = (bf16[8,128,512]{2,1,0:T(8,128)(2,1)}, bf16[8,128,512]{2,1,0:T(8,128)(2,1)S(1)}, u32[]{:S(2)}, u32[]{:S(2)}) collective-permute-start(bf16[8,128,512]{2,1,0:T(8,128)(2,1)} %k0.7), channel_id=1, source_target_pairs={{0,2},{2,0},{4,6},{6,4},{8,10},{10,8},{12,14},{14,12},{1,3},{3,1},... | collective-permute-start | bytes 3145736 | tf_op jit(solution)/shard_map/ppermute | solution.py:462
  0.0 47.2 %collective-permute-start.1 = (bf16[8,128,512]{2,1,0:T(8,128)(2,1)}, bf16[8,128,512]{2,1,0:T(8,128)(2,1)S(1)}, u32[]{:S(2)}, u32[]{:S(2)}) collective-permute-start(bf16[8,128,512]{2,1,0:T(8,128)(2,1)} %v0.7), channel_id=1, source_target_pairs={{0,2},{2,0},{4,6},{6,4},{8,10},{10,8},{12,14},{14,12},{1,3},{3,1},... | collective-permute-start | bytes 3145736 | tf_op jit(solution)/shard_map/ppermute | solution.py:462
  4.2 21.3 %copy-start.10 = (s32[8,3]{0,1:T(4,128)S(1)}, s32[8,3]{0,1:T(4,128)}, u32[]{:S(2)}) copy-start(s32[8,3]{0,1:T(4,128)} %param.20) | copy-start | bytes 292
  4.3 13.2 %collective-permute-start.4 = (bf16[1536,128]{1,0:T(8,128)(2,1)S(1)}, bf16[1536,128]{1,0:T(8,128)(2,1)}, u32[]{:S(2)}, u32[]{:S(2)}) collective-permute-start(bf16[1536,128]{1,0:T(8,128)(2,1)S(1)} %reshape.20.q_ref), channel_id=1, source_target_pairs={{0,12},{2,14},{4,8},{6,10},{8,4},{10,6},{12,0},{14,2},{1,13},{3,15... | collective-permute-start | bytes 1179656 | tf_op jit(solution)/shard_map/ppermute | solution.py:462
  17.5 29.7 %collective-permute-start.5 = (bf16[1536,128]{1,0:T(8,128)(2,1)}, bf16[1536,128]{1,0:T(8,128)(2,1)}, u32[]{:S(2)}, u32[]{:S(2)}) collective-permute-start(bf16[1536,128]{1,0:T(8,128)(2,1)} %collective-permute-done.4.q_ref), channel_id=1, source_target_pairs={{0,4},{2,6},{4,0},{6,2},{8,12},{10,14},{12,8},{14,10},{1,5},{3,7},... | collective-permute-start | bytes 1179656 | tf_op jit(solution)/shard_map/ppermute | solution.py:462
  25.5 32.7 %collective-permute-start.2 = (bf16[1536,128]{1,0:T(8,128)(2,1)S(1)}, bf16[1536,128]{1,0:T(8,128)(2,1)}, u32[]{:S(2)}, u32[]{:S(2)}) collective-permute-start(bf16[1536,128]{1,0:T(8,128)(2,1)S(1)} %reshape.20.q_ref), channel_id=1, source_target_pairs={{0,4},{2,6},{4,0},{6,2},{8,12},{10,14},{12,8},{14,10},{1,5},{3,7},... | collective-permute-start | bytes 1179656 | tf_op jit(solution)/shard_map/ppermute | solution.py:462
  25.6 0.7 copy-start.11
  26.5 0.7 copy-start.13
  28.4 0.7 copy-start.12
  47.2 1.2 %copy-start.1 = (bf16[8,128,512]{2,1,0:T(8,128)(2,1)S(1)}, bf16[8,128,512]{2,1,0:T(8,128)(2,1)}, u32[]{:S(2)}) copy-start(bf16[8,128,512]{2,1,0:T(8,128)(2,1)} %v0.7) | copy-start | bytes 3145732
  48.4 19.9 %copy-start.3 = (bf16[8,128,512]{2,1,0:T(8,128)(2,1)}, bf16[8,128,512]{2,1,0:T(8,128)(2,1)S(1)}, u32[]{:S(2)}) copy-start(bf16[8,128,512]{2,1,0:T(8,128)(2,1)S(1)} %collective-permute-done.1.v1) | copy-start | bytes 3145732
  58.1 19.7 %collective-permute-start.6 = (bf16[1584,128]{1,0:T(8,128)(2,1)S(1)}, bf16[1584,128]{1,0:T(8,128)(2,1)S(1)}, u32[]{:S(2)}, u32[]{:S(2)}) collective-permute-start(bf16[1584,128]{1,0:T(8,128)(2,1)S(1)} %shard_map.112), channel_id=1, source_target_pairs={{0,4},{2,6},{4,0},{6,2},{8,12},{10,14},{12,8},{14,10},{1,5},{3,7},... | collective-permute-start | bytes 1216520 | tf_op jit(solution)/shard_map/ppermute | solution.py:462
  68.4 37.1 %collective-permute-start.3 = (bf16[1584,128]{1,0:T(8,128)(2,1)}, bf16[1584,128]{1,0:T(8,128)(2,1)}, u32[]{:S(2)}, u32[]{:S(2)}) collective-permute-start(bf16[1584,128]{1,0:T(8,128)(2,1)} %shard_map.110), channel_id=1, source_target_pairs={{0,4},{2,6},{4,0},{6,2},{8,12},{10,14},{12,8},{14,10},{1,5},{3,7},... | collective-permute-start | bytes 1216520 | tf_op jit(solution)/shard_map/ppermute | solution.py:462
  77.8 6.2 %copy-start.9 = (bf16[8,3,512]{2,0,1:T(8,128)(2,1)S(1)}, bf16[8,3,512]{2,0,1:T(8,128)(2,1)}, u32[]{:S(2)}) copy-start(bf16[8,3,512]{2,0,1:T(8,128)(2,1)} %param.18) | copy-start | bytes 73732
  77.8 11.8 %copy-start.2 = (bf16[8,128,512]{2,1,0:T(8,128)(2,1)S(1)}, bf16[8,128,512]{2,1,0:T(8,128)(2,1)}, u32[]{:S(2)}) copy-start(bf16[8,128,512]{2,1,0:T(8,128)(2,1)} %v0.7) | copy-start | bytes 3145732
  79.2 26.3 %collective-permute-start.7 = (bf16[1584,128]{1,0:T(8,128)(2,1)}, bf16[1584,128]{1,0:T(8,128)(2,1)}, u32[]{:S(2)}, u32[]{:S(2)}) collective-permute-start(bf16[1584,128]{1,0:T(8,128)(2,1)} %shard_map.113), channel_id=1, source_target_pairs={{0,12},{2,14},{4,8},{6,10},{8,4},{10,6},{12,0},{14,2},{1,13},{3,15... | collective-permute-start | bytes 1216520 | tf_op jit(solution)/shard_map/ppermute | solution.py:462
  88.8 0.8 copy-start.8
  89.6 0.7 copy-start.7
  90.2 1.2 %copy-start.4 = (bf16[8,128,512]{2,1,0:T(8,128)(2,1)S(1)}, bf16[8,128,512]{2,1,0:T(8,128)(2,1)}, u32[]{:S(2)}) copy-start(bf16[8,128,512]{2,1,0:T(8,128)(2,1)} %copy-done.3) | copy-start | bytes 3145732
  91.5 1.2 %copy-start.5 = (bf16[8,128,512]{2,1,0:T(8,128)(2,1)S(1)}, bf16[8,128,512]{2,1,0:T(8,128)(2,1)}, u32[]{:S(2)}) copy-start(bf16[8,128,512]{2,1,0:T(8,128)(2,1)} %leaf_k.1) | copy-start | bytes 3145732
  92.7 1.2 %copy-start.6 = (bf16[8,128,512]{2,1,0:T(8,128)(2,1)S(1)}, bf16[8,128,512]{2,1,0:T(8,128)(2,1)}, u32[]{:S(2)}) copy-start(bf16[8,128,512]{2,1,0:T(8,128)(2,1)} %leaf_v.1) | copy-start | bytes 3145732

commit v2 on v0

--- a/solution.py
+++ b/solution.py
@@ -1,8 +1,11 @@
+import functools
 import math
 
 import jax
 import jax.numpy as jnp
 from jax import lax
+from jax.experimental import pallas as pl
+from jax.experimental.pallas import tpu as pltpu
 from jax.sharding import PartitionSpec as P
 
 HD = 128
@@ -188,9 +191,398 @@
     )
 
 
+NEG = -3e38
+CORES = 2
+
+
+def pair_sums(tile):
+    return tile + pltpu.roll(tile, tile.shape[1] - 1, 1)
+
+
+def two_pieces(values):
+    high = values.astype(jnp.bfloat16).astype(jnp.float32)
+    low = (values - high).astype(jnp.bfloat16).astype(jnp.float32)
+    return high, low
+
+
+def dot_nt(a, b):
+    return lax.dot_general(a, b, (((1,), (1,)), ((), ())), preferred_element_type=jnp.float32)
+
+
+def dot_nn(a, b):
+    return lax.dot_general(a, b, (((1,), (0,)), ((), ())), preferred_element_type=jnp.float32)
+
+
+def plain_call(kernel, out_shape, in_memory, scratch=(), flops=0, num_bytes=0):
+    return pl.pallas_call(
+        kernel,
+        out_shape=out_shape,
+        in_specs=[pl.BlockSpec(memory_space=space) for space in in_memory],
+        out_specs=tuple(pl.BlockSpec(memory_space=pltpu.VMEM) for _ in out_shape),
+        scratch_shapes=list(scratch),
+        compiler_params=pltpu.CompilerParams(vmem_limit_bytes=32 * 1024 * 1024),
+        cost_estimate=pl.CostEstimate(flops=flops, bytes_accessed=num_bytes, transcendentals=0),
+    )
+
+
+class Sizes:
+    def __init__(self, requests, steps, kv, group, levels, pages, page_tok):
+        self.requests, self.steps, self.kv, self.group = requests, steps, kv, group
+        self.levels, self.pages, self.page_tok = levels, pages, page_tok
+        self.rows = steps * group
+        self.step_rows = kv * group
+        self.all_rows = requests * kv * self.rows
+        self.per_tile = HD // (4 * kv)
+        self.tile_count = -(-requests // self.per_tile)
+        self.stat_rows = self.tile_count * self.rows
+        self.factor = 1.0 / math.sqrt(HD) * math.log2(math.e)
+
+    def tiles(self):
+        for tile_at in range(self.tile_count):
+            first = tile_at * self.per_tile
+            yield tile_at, first, min(self.requests, first + self.per_tile)
+
+    def read_table(self, q_ref, table_words, table_ref, sem):
+        table_words[...] = q_ref[0, :, self.step_rows * HD :].astype(jnp.float32).astype(jnp.int32)
+        copy = pltpu.make_async_copy(table_words, table_ref, sem)
+        copy.start()
+        return copy
+
+    def spread(self, q_ref, wide):
+        for step in range(self.steps):
+            for head in range(self.step_rows):
+                at = (step * self.step_rows + head) * self.requests
+                wide[at : at + self.requests, :] = q_ref[
+                    step, :, head * HD : (head + 1) * HD
+                ].astype(jnp.float32)
+
+    def pick(self, wide, request, kv_head):
+        parts = []
+        for step in range(self.steps):
+            at = (step * self.step_rows + kv_head * self.group) * self.requests
+            parts.append(wide[pl.ds(at + request, self.group, stride=self.requests), :])
+        return jnp.concatenate(parts, axis=0)
+
+    def span(self, request, kv_head):
+        return pl.ds(pl.multiple_of((request * self.kv + kv_head) * self.rows, 16), self.rows)
+
+    def find(self, table_ref, owner, request):
+        slot, used = jnp.int32(0), jnp.int32(0)
+        for level in range(self.levels):
+            hit = table_ref[request, level] == owner
+            slot = jnp.where(hit, table_ref[request, self.levels + level], slot)
+            used = jnp.where(hit, 1, used)
+        return slot, used
+
+
+def shared_kernel(
+    sz, exact, count0_ref, count1_ref, q_ref, k0, v0, k1, v1, *rest
+):
+    *outs, wide, table_words, table_ref, sem = rest
+    num_ref = outs[0]
+    me = lax.axis_index("page")
+    mate = jnp.bitwise_xor(me, 1)
+    lane_ids = lax.broadcasted_iota(jnp.int32, (sz.rows, HD), 1)
+    token_ids = lax.broadcasted_iota(jnp.int32, (sz.rows, sz.page_tok), 1)
+    heads = range(sz.kv)
+    copy = sz.read_table(q_ref, table_words, table_ref, sem)
+    sz.spread(q_ref, wide)
+    copy.wait()
+    for tile_at, first, last in sz.tiles():
+
+        def one(request, tile):
+            slot0, used0 = sz.find(table_ref, me, request)
+            slot1, used1 = sz.find(table_ref, mate, request)
+            allowed0 = token_ids < used0 * count0_ref[slot0]
+            allowed1 = token_ids < used1 * count1_ref[slot1]
+
+            def work(tile):
+                cols = [slice(head * HD, (head + 1) * HD) for head in heads]
+                q = [sz.pick(wide, request, head).astype(jnp.bfloat16) for head in heads]
+                s0 = [dot_nt(q[h], k0[slot0, :, cols[h]]) for h in heads]
+                s1 = [dot_nt(q[h], k1[slot1, :, cols[h]]) for h in heads]
+                s0 = [jnp.where(allowed0, s, NEG) for s in s0]
+                s1 = [jnp.where(allowed1, s, NEG) for s in s1]
+                top = [jnp.max(jnp.maximum(a, b), axis=1, keepdims=True) for a, b in zip(s0, s1)]
+                point = [sum(two_pieces(t)) for t in top]
+                w0 = [jnp.exp2((s - p) * sz.factor) for s, p in zip(s0, point)]
+                w1 = [jnp.exp2((s - p) * sz.factor) for s, p in zip(s1, point)]
+                total = [jnp.sum(a + b, axis=1, keepdims=True) for a, b in zip(w0, w1)]
+                num = [
+                    dot_nn(w0[h].astype(jnp.bfloat16), v0[slot0, :, cols[h]])
+                    + dot_nn(w1[h].astype(jnp.bfloat16), v1[slot1, :, cols[h]])
+                    for h in heads
+                ]
+                for h in heads:
+                    num_ref[sz.span(request, h), :] = num[h].astype(num_ref.dtype)
+                    lane = ((request - first) * sz.kv + h) * 4
+                    tile = jnp.where(lane_ids == lane, point[h], tile)
+                    tile = jnp.where(lane_ids == lane + 2, total[h], tile)
+                return tile
+
+            def skip(tile):
+                for h in heads:
+                    num_ref[sz.span(request, h), :] = jnp.zeros((sz.rows, HD), num_ref.dtype)
+                return tile
+
+            return lax.cond(used0 + used1 > 0, work, skip, tile)
+
+        empty = jnp.where(lane_ids % 4 == 0, NEG, 0.0)
+        tile = lax.fori_loop(first, last, one, empty)
+        if exact:
+            outs[1][pl.ds(tile_at * sz.rows, sz.rows), :] = tile
+        else:
+            put_stats(sz, num_ref, tile_at, tile)
+
+
+def put_stats(sz, out_ref, tile_at, tile):
+    kind = lax.broadcasted_iota(jnp.int32, tile.shape, 1) % 4
+    high, low = two_pieces(tile)
+    tile = jnp.where(kind % 2 == 0, high, pltpu.roll(low, 1, 1))
+    out_ref[pl.ds(sz.all_rows + tile_at * sz.rows, sz.rows), :] = tile.astype(jnp.bfloat16)
+
+
+def local_kernel(
+    sz,
+    count0_ref,
+    count1_ref,
+    leaf_count_ref,
+    q_ref,
+    k0,
+    v0,
+    k1,
+    v1,
+    leaf_k,
+    leaf_v,
+    new_k,
+    new_v,
+    num_ref,
+    stat_ref,
+    wide,
+    table_words,
+    table_ref,
+    sem,
+    fresh_k,
+    fresh_v,
+):
+    me = lax.axis_index("page")
+    mate = jnp.bitwise_xor(me, 1)
+    lane_ids = lax.broadcasted_iota(jnp.int32, (sz.rows, HD), 1)
+    token_ids = lax.broadcasted_iota(jnp.int32, (sz.rows, sz.page_tok), 1)
+    fresh = fresh_k.shape[0]
+    fresh_ids = lax.broadcasted_iota(jnp.int32, (sz.rows, fresh), 1)
+    step_ids = lax.broadcasted_iota(jnp.int32, (sz.rows, fresh), 0) // sz.group
+    causal = (fresh_ids // sz.requests) <= step_ids
+    fresh_request = fresh_ids % sz.requests
+    heads = range(sz.kv)
+    cols = [slice(head * HD, (head + 1) * HD) for head in heads]
+    copy = sz.read_table(q_ref, table_words, table_ref, sem)
+    sz.spread(q_ref, wide)
+    copy.wait()
+    for new_ref, full in ((new_k, fresh_k), (new_v, fresh_v)):
+        rows = [new_ref[step].astype(jnp.float32) for step in range(sz.steps)]
+        filler = fresh - sz.steps * sz.requests
+        if filler:
+            rows.append(jnp.zeros((filler, sz.kv * HD), jnp.float32))
+        full[...] = jnp.concatenate(rows, axis=0).astype(full.dtype)
+    for tile_at, first, last in sz.tiles():
+
+        def one(request, tile):
+            slot0, used0 = sz.find(table_ref, me, request)
+            slot1, used1 = sz.find(table_ref, mate, request)
+            allowed = (
+                token_ids < used0 * count0_ref[slot0],
+                token_ids < used1 * count1_ref[slot1],
+                token_ids < leaf_count_ref[request],
+                causal & (fresh_request == request),
+            )
+            places = ((k0, v0, slot0), (k1, v1, slot1), (leaf_k, leaf_v, request))
+            q = [sz.pick(wide, request, head).astype(jnp.bfloat16) for head in heads]
+            scores = []
+            for h in heads:
+                mine = [dot_nt(q[h], keys[at, :, cols[h]]) for keys, _, at in places]
+                mine.append(dot_nt(q[h], fresh_k[:, cols[h]]))
+                scores.append([jnp.where(ok, s, NEG) for ok, s in zip(allowed, mine)])
+            top = [
+                jnp.max(functools.reduce(jnp.maximum, mine), axis=1, keepdims=True)
+                for mine in scores
+            ]
+            weights = [
+                [jnp.exp2((s - t) * sz.factor) for s in mine] for mine, t in zip(scores, top)
+            ]
+            total = [jnp.sum(sum(mine), axis=1, keepdims=True) for mine in weights]
+            for h in heads:
+                w = [weight.astype(jnp.bfloat16) for weight in weights[h]]
+                num = dot_nn(w[3], fresh_v[:, cols[h]])
+                for weight, (_, values, at) in zip(w, places):
+                    num = num + dot_nn(weight, values[at, :, cols[h]])
+                num_ref[sz.span(request, h), :] = num
+                lane = ((request - first) * sz.kv + h) * 4
+                tile = jnp.where(lane_ids == lane, top[h], tile)
+                tile = jnp.where(lane_ids == lane + 2, total[h], tile)
+            return tile
+
+        tile = lax.fori_loop(first, last, one, jnp.zeros((sz.rows, HD), jnp.float32))
+        stat_ref[pl.ds(tile_at * sz.rows, sz.rows), :] = tile
+
+
+def merge_kernel(sz, num_ref, stat_ref, came_ref, out_ref):
+    for tile_at, first, last in sz.tiles():
+        came_span = pl.ds(sz.all_rows + tile_at * sz.rows, sz.rows)
+        mine = stat_ref[pl.ds(tile_at * sz.rows, sz.rows), :]
+        came = pair_sums(came_ref[came_span, :].astype(jnp.float32))
+        top = jnp.maximum(mine, came)
+        keep, add = jnp.exp2((mine - top) * sz.factor), jnp.exp2((came - top) * sz.factor)
+        total = mine * pltpu.roll(keep, 2, 1) + came * pltpu.roll(add, 2, 1)
+        kind = lax.broadcasted_iota(jnp.int32, top.shape, 1) % 4
+        put_stats(sz, out_ref, tile_at, jnp.where(kind == 0, top, total))
+        for request in range(first, last):
+            for head in range(sz.kv):
+                lane = ((request - first) * sz.kv + head) * 4
+                span = sz.span(request, head)
+                joined = num_ref[span, :] * keep[:, lane : lane + 1]
+                joined = joined + came_ref[span, :].astype(jnp.float32) * add[:, lane : lane + 1]
+                out_ref[span, :] = joined.astype(jnp.bfloat16)
+
+
+def final_kernel(sz, num_ref, stat_ref, near_ref, far_ref, out_ref, wide):
+    for tile_at, first, last in sz.tiles():
+        came_span = pl.ds(sz.all_rows + tile_at * sz.rows, sz.rows)
+        mine = stat_ref[pl.ds(tile_at * sz.rows, sz.rows), :]
+        near = pair_sums(near_ref[came_span, :].astype(jnp.float32))
+        far = pair_sums(far_ref[came_span, :].astype(jnp.float32))
+        top = jnp.maximum(jnp.maximum(mine, near), far)
+        states = (mine, near, far)
+        parts = [jnp.exp2((one - top) * sz.factor) for one in states]
+        total = sum(one * pltpu.roll(part, 2, 1) for one, part in zip(states, parts))
+        total = pltpu.roll(total, HD - 2, 1)
+        parts = [part / total for part in parts]
+        for request in range(first, last):
+            for head in range(sz.kv):
+                lane = ((request - first) * sz.kv + head) * 4
+                span = sz.span(request, head)
+                joined = sum(
+                    ref[span, :].astype(jnp.float32) * part[:, lane : lane + 1]
+                    for ref, part in zip((num_ref, near_ref, far_ref), parts)
+                )
+                for step in range(sz.steps):
+                    at = (step * sz.step_rows + head * sz.group) * sz.requests
+                    wide[pl.ds(at + request, sz.group, stride=sz.requests), :] = joined[
+                        step * sz.group : (step + 1) * sz.group
+                    ]
+    for step in range(sz.steps):
+        for head in range(sz.step_rows):
+            at = (step * sz.step_rows + head) * sz.requests
+            out_ref[step, :, head * HD : (head + 1) * HD] = wide[
+                at : at + sz.requests, :
+            ].astype(jnp.bfloat16)
+
+
+def line_shards(
+    queries,
+    page_keys,
+    page_values,
+    page_count,
+    leaf_keys,
+    leaf_values,
+    leaf_count,
+    new_keys,
+    new_values,
+    path_owner,
+    path_slot,
+):
+    requests, steps, width = queries.shape
+    owners = lax.axis_size("page")
+    kv = page_keys.shape[2] // HD
+    pages, page_tok = page_keys.shape[:2]
+    sz = Sizes(requests, steps, kv, QH // KVH, path_owner.shape[1], pages, page_tok)
+
+    def exchange(array, hop):
+        return lax.ppermute(array, "page", [(at, at ^ hop) for at in range(owners)])
+
+    near, far = CORES, owners - CORES
+    paths = jnp.concatenate([path_owner, path_slot], axis=1).astype(queries.dtype)
+    paths = jnp.pad(paths, ((0, 0), (0, HD - paths.shape[1])))
+    paths = jnp.broadcast_to(paths[None], (steps, requests, HD))
+    block = jnp.concatenate([jnp.swapaxes(queries, 0, 1), paths], axis=2)
+    far_q = exchange(block, far)
+    near_q = exchange(block, near)
+    mate_keys = exchange(page_keys, 1)
+    mate_values = exchange(page_values, 1)
+    mate_count = exchange(page_count, 1)
+
+    smem, vmem = pltpu.SMEM, pltpu.VMEM
+    sent = (jax.ShapeDtypeStruct((sz.all_rows + sz.stat_rows, HD), jnp.bfloat16),)
+    exact = (
+        jax.ShapeDtypeStruct((sz.all_rows, HD), jnp.float32),
+        jax.ShapeDtypeStruct((sz.stat_rows, HD), jnp.float32),
+    )
+    wide = pltpu.VMEM((sz.all_rows, HD), jnp.float32)
+    scratch = (
+        wide,
+        pltpu.VMEM((requests, HD), jnp.int32),
+        pltpu.SMEM((requests, HD), jnp.int32),
+        pltpu.SemaphoreType.DMA,
+    )
+    counts = (page_count, mate_count)
+    all_pages = (page_keys, page_values, mate_keys, mate_values)
+    flops = sz.all_rows * HD * sz.page_tok * 8
+    page_bytes = 4 * page_keys.size * 2 + sz.all_rows * HD * 4
+
+    def shared(is_exact, block):
+        return plain_call(
+            functools.partial(shared_kernel, sz, is_exact),
+            exact if is_exact else sent,
+            [smem] * 2 + [vmem] * 5,
+            scratch,
+            flops=flops,
+            num_bytes=page_bytes,
+        )(*counts, block, *all_pages)
+
+    fresh_rows = -(-requests * steps // page_tok) * page_tok
+    fresh = pltpu.VMEM((fresh_rows, kv * HD), jnp.bfloat16)
+    local = plain_call(
+        functools.partial(local_kernel, sz),
+        exact,
+        [smem] * 3 + [vmem] * 9,
+        [*scratch, fresh, fresh],
+        flops=flops * 2,
+        num_bytes=page_bytes * 2,
+    )(
+        *counts,
+        leaf_count,
+        block,
+        *all_pages,
+        leaf_keys,
+        leaf_values,
+        jnp.swapaxes(new_keys, 0, 1),
+        jnp.swapaxes(new_values, 0, 1),
+    )
+    far_q, local = lax.optimization_barrier((far_q, local))
+    cross_q = exchange(far_q, near)
+    far_part = shared(True, far_q)
+    near_part = shared(False, near_q)
+    cross_part = shared(False, cross_q)
+    cross_back = exchange(cross_part[0], near)
+    (joined,) = plain_call(
+        functools.partial(merge_kernel, sz), sent, [vmem] * 3, num_bytes=sz.all_rows * HD * 8
+    )(*far_part, cross_back)
+    far_back = exchange(joined, far)
+    near_back = exchange(near_part[0], near)
+    (out,) = plain_call(
+        functools.partial(final_kernel, sz),
+        (jax.ShapeDtypeStruct((steps, requests, width), jnp.bfloat16),),
+        [vmem] * 4,
+        [wide],
+        num_bytes=sz.all_rows * HD * 10,
+    )(*local, near_back, far_back)
+    return jnp.swapaxes(out, 0, 1)
+
+
 def solution(mesh):
+    on_line = mesh.shape["sub"] == 1 and mesh.shape["page"] == 4 * CORES
     return jax.shard_map(
-        shards,
+        line_shards if on_line else shards,
         mesh=mesh,
         in_specs=(
             P(("groups", "page", "sub"), None, "head"),

time: 295 us -> 73.2 us (0.25)
  waiting for transfers between devices: 131 us -> 25.3 us
  local copies, waits for them, and re-layouts: 93.2 us -> 5.67 us
  Pallas kernels: 0 us -> 22.1 us
  blocking collectives: 19.7 us -> 0 us
  matrix products: 16 us -> 0 us
  other arithmetic: 16 us -> 1.74 us
    all_to_all x3 -> x0, waiting for transfers between devices: 131 us -> none  [the longest x1 71.6 us: shards(): lax.all_to_all(outgoing, 'page', split_axis=0, concat_axis=0, tiled=True)]
    gather x32 -> x0, local copies, waits for them, and re-layouts: 57 us -> none  [the longest x3 18.3 us: shards(): jnp.take(queries, item_of_slot // level_count, axis=0)]
    ppermute x0 -> x9, waiting for transfers between devices: none -> 25.3 us  [exchange(): return lax.ppermute(array, 'page', [(at, at ^ hop) for at in range(owners)])]
    pallas_call x0 -> x6, Pallas kernels: none -> 22.1 us  [the longest x3 12.4 us: shared(): plain_call(functools.partial(shared_kernel, sz, is_exact), exact if is_ex...]
    all_to_all x2 -> x0, blocking collectives: 19.7 us -> none  [the longest x1 9.87 us: shards(): lax.all_to_all(states[2], 'page', split_axis=0, concat_axis=0, tiled=True)]
    ppermute x0 -> x9, starting transfers between devices: none -> 17.7 us  [exchange(): return lax.ppermute(array, 'page', [(at, at ^ hop) for at in range(owners)])]
    all_to_all x3 -> x0, starting transfers between devices: 16.1 us -> none  [the longest x1 6.33 us: shards(): lax.all_to_all(page_ids, 'page', split_axis=0, concat_axis=0, tiled=True)]
    dot_general x20 -> x0, matrix products: 16 us -> none  [the longest x8 5.98 us: page_states(): jnp.einsum('nskgd,ntkd->nskgt', query_five, key_heads, preferred_element_...]
  transfers between devices with their start and end apart: 3 -> 9, of which waited for: 2 -> 5; matrix products, arithmetic and copies ran while one was open for 12% -> 3% of each run, Pallas kernels for 0% -> 28%
where the time goes in v2:
time: 73.2 us; the launch traced here: 72.6 us
  waiting for transfers between devices  25.3 us (35%)
  Pallas kernels  22.1 us (30%)
  starting transfers between devices  17.7 us (24%)
  local copies, waits for them, and re-layouts  5.67 us (8%)
  other arithmetic  1.74 us (2%)
    ppermute x9, waiting for transfers between devices, exchange(): return lax.ppermute(array, 'page', [(at, at ^ hop) for at in range(owners)])  25.3 us
    ppermute x9, starting transfers between devices, exchange(): return lax.ppermute(array, 'page', [(at, at ^ hop) for at in range(owners)])  17.7 us
    pallas_call x3, Pallas kernels, shared(): plain_call(functools.partial(shared_kernel, sz, is_exact), exact if is_ex...  12.4 us
    pallas_call x1, Pallas kernels, line_shards(): plain_call(functools.partial(local_kernel, sz), exact, [smem] * 3 + [vmem...  7.24 us
    unnamed x23, local copies, waits for them, and re-layouts  5.66 us
    pallas_call x1, Pallas kernels, line_shards(): plain_call(functools.partial(final_kernel, sz), (jax.ShapeDtypeStruct((st...  1.75 us
  transfers between devices with their start and end apart: 9, of which 5 were waited for; matrix products, arithmetic and copies ran while one was open for 3% of the time, Pallas kernels for 28%

profile of v2, /device:TPU:0, one launch (start us, length us, event | category | flops | bytes accessed | tf_op | source)
XLA Modules:
  0.0 72.6 jit_solution(9811148599338129865)
XLA Ops:
  0.0 0.5 collective-permute-start.2
  0.5 0.1 collective-permute-start.3
  0.5 0.7 convert.6
  1.2 0.1 copy.13
  1.3 0.0 copy-start.6
  1.4 0.0 copy-start.7
  1.4 1.0 %pad_maximum_fusion.q_ref = bf16[3,8,8320]{2,1,0:T(8,128)(2,1)S(1)} fusion(bf16[3,8,128]{2,1,0:T(8,128)(2,1)S(1)} %broadcast_in_dim.2, bf16[3,8,8192]{2,1,0:T(8,128)(2,1)} %bitcast.6), kind=kLoop, calls=%fused_computation | loop fusion | flops 798720 | bytes 798720 | tf_op jit(solution)/shard_map/concatenate | solution.py:507
  2.4 5.1 %collective-permute-start = (bf16[3,8,8320]{2,1,0:T(8,128)(2,1)S(1)}, bf16[3,8,8320]{2,1,0:T(8,128)(2,1)S(1)}, u32[]{:S(2)}, u32[]{:S(2)}) collective-permute-start(bf16[3,8,8320]{2,1,0:T(8,128)(2,1)S(1)} %pad_maximum_fusion.q_ref), channel_id=1, source_target_pairs={{0,12},{2,14},{4,8},{6,10},{8,4},{10,6},{12,0},{14,2},{1,13},{3,15... | collective-permute-start | bytes 1198088 | tf_op jit(solution)/shard_map/ppermute | solution.py:501
  7.5 0.0 collective-permute-start.1
  7.5 1.1 %collective-permute-done.1.count1_ref = s32[8]{0:T(128)S(1)} collective-permute-done((s32[8]{0:T(128)S(1)}, s32[8]{0:T(128)S(1)}, u32[]{:S(2)}, u32[]{:S(2)}) %collective-permute-start.1) | collective-permute-done | bytes 64 | tf_op jit(solution)/shard_map/ppermute | solution.py:501
  8.6 0.0 collective-permute-done.2.k1
  8.6 0.0 collective-permute-done.3.v1
  8.7 0.6 copy-done.9
  9.3 1.2 %copy-done = bf16[8,128,512]{2,1,0:T(8,128)(2,1)S(1)} copy-done((bf16[8,128,512]{2,1,0:T(8,128)(2,1)S(1)}, bf16[8,128,512]{2,1,0:T(8,128)(2,1)}, u32[]{:S(2)}) %copy-start) | copy-done | bytes 1048600
  10.5 1.2 %copy-done.2 = bf16[8,128,512]{2,1,0:T(8,128)(2,1)S(1)} copy-done((bf16[8,128,512]{2,1,0:T(8,128)(2,1)S(1)}, bf16[8,128,512]{2,1,0:T(8,128)(2,1)}, u32[]{:S(2)}) %copy-start.2) | copy-done | bytes 1048600
  11.8 1.2 %copy-done.4 = bf16[8,128,512]{2,1,0:T(8,128)(2,1)S(1)} copy-done((bf16[8,128,512]{2,1,0:T(8,128)(2,1)S(1)}, bf16[8,128,512]{2,1,0:T(8,128)(2,1)}, u32[]{:S(2)}) %copy-start.4) | copy-done | bytes 1048600
  13.0 1.2 %copy-done.5 = bf16[8,128,512]{2,1,0:T(8,128)(2,1)S(1)} copy-done((bf16[8,128,512]{2,1,0:T(8,128)(2,1)S(1)}, bf16[8,128,512]{2,1,0:T(8,128)(2,1)}, u32[]{:S(2)}) %copy-start.5) | copy-done | bytes 1048600
  14.2 7.2 %shard_map.109 = (f32[1536,128]{1,0:T(8,128)S(1)}, f32[48,128]{1,0:T(8,128)S(1)}) custom-call(s32[8]{0:T(128)S(1)} %copy-done.8, s32[8]{0:T(128)S(1)} %collective-permute-done.1.count1_ref, s32[8]{0:T(128)S(1)} %copy-done.9, bf16[3,8,8320]{2,1,0:T(8,128)(2,1)S(1)} %pad_maximum_fusion.q_ref, bf16[8,128,512]{2,1,0:T(8,128)(2,1)S(1)} %copy-done, ...), custom_call_target="tpu_custom_call" | custom-call | flops 402653184 | bytes 9961472 | tf_op jit(solution)/shard_map/pallas_call | solution.py:544
  21.5 3.8 %collective-permute-start.6 = (bf16[3,8,8320]{2,1,0:T(8,128)(2,1)S(1)}, bf16[3,8,8320]{2,1,0:T(8,128)(2,1)S(1)}, u32[]{:S(2)}, u32[]{:S(2)}) collective-permute-start(bf16[3,8,8320]{2,1,0:T(8,128)(2,1)S(1)} %collective-permute-done.q_ref), channel_id=1, source_target_pairs={{0,4},{2,6},{4,0},{6,2},{8,12},{10,14},{12,8},{14,10},{1,5},{3,7},... | collective-permute-start | bytes 1198088 | tf_op jit(solution)/shard_map/ppermute | solution.py:501
  25.3 0.0 collective-permute-start.4
  25.3 10.1 %collective-permute-done.6.q_ref = bf16[3,8,8320]{2,1,0:T(8,128)(2,1)S(1)} collective-permute-done((bf16[3,8,8320]{2,1,0:T(8,128)(2,1)S(1)}, bf16[3,8,8320]{2,1,0:T(8,128)(2,1)S(1)}, u32[]{:S(2)}, u32[]{:S(2)}) %collective-permute-start.6) | collective-permute-done | bytes 399392 | tf_op jit(solution)/shard_map/ppermute | solution.py:501
  35.4 4.5 %shard_map.112 = bf16[1584,128]{1,0:T(8,128)(2,1)S(1)} custom-call(s32[8]{0:T(128)S(1)} %copy-done.8, s32[8]{0:T(128)S(1)} %collective-permute-done.1.count1_ref, bf16[3,8,8320]{2,1,0:T(8,128)(2,1)S(1)} %collective-permute-done.6.q_ref, bf16[8,128,512]{2,1,0:T(8,128)(2,1)S(1)} %copy-done.1, bf16[8,128,512]{2,1,0:T(8,128)(2,1)S(1)} %copy-done.3, ...), custom_call_target="tpu_custom_call" | custom-call | flops 201326592 | bytes 4980736 | tf_op jit(solution)/shard_map/pallas_call | solution.py:533
  40.0 1.1 %collective-permute-start.7 = (bf16[1584,128]{1,0:T(8,128)(2,1)S(1)}, bf16[1584,128]{1,0:T(8,128)(2,1)S(1)}, u32[]{:S(2)}, u32[]{:S(2)}) collective-permute-start(bf16[1584,128]{1,0:T(8,128)(2,1)S(1)} %shard_map.112), channel_id=1, source_target_pairs={{0,4},{2,6},{4,0},{6,2},{8,12},{10,14},{12,8},{14,10},{1,5},{3,7},... | collective-permute-start | bytes 1216520 | tf_op jit(solution)/shard_map/ppermute | solution.py:501
  41.1 2.9 %collective-permute-done.4.q_ref = bf16[3,8,8320]{2,1,0:T(8,128)(2,1)S(1)} collective-permute-done((bf16[3,8,8320]{2,1,0:T(8,128)(2,1)S(1)}, bf16[3,8,8320]{2,1,0:T(8,128)(2,1)S(1)}, u32[]{:S(2)}, u32[]{:S(2)}) %collective-permute-start.4) | collective-permute-done | bytes 399392 | tf_op jit(solution)/shard_map/ppermute | solution.py:501
  44.0 4.0 %shard_map.110 = bf16[1584,128]{1,0:T(8,128)(2,1)S(1)} custom-call(s32[8]{0:T(128)S(1)} %copy-done.8, s32[8]{0:T(128)S(1)} %collective-permute-done.1.count1_ref, bf16[3,8,8320]{2,1,0:T(8,128)(2,1)S(1)} %collective-permute-done.4.q_ref, bf16[8,128,512]{2,1,0:T(8,128)(2,1)S(1)} %copy-done.1, bf16[8,128,512]{2,1,0:T(8,128)(2,1)S(1)} %copy-done.3, ...), custom_call_target="tpu_custom_call" | custom-call | flops 201326592 | bytes 4980736 | tf_op jit(solution)/shard_map/pallas_call | solution.py:533
  48.0 1.6 %collective-permute-start.5 = (bf16[1584,128]{1,0:T(8,128)(2,1)S(1)}, bf16[1584,128]{1,0:T(8,128)(2,1)S(1)}, u32[]{:S(2)}, u32[]{:S(2)}) collective-permute-start(bf16[1584,128]{1,0:T(8,128)(2,1)S(1)} %shard_map.110), channel_id=1, source_target_pairs={{0,4},{2,6},{4,0},{6,2},{8,12},{10,14},{12,8},{14,10},{1,5},{3,7},... | collective-permute-start | bytes 1216520 | tf_op jit(solution)/shard_map/ppermute | solution.py:501
  49.6 3.9 %shard_map.111 = (f32[1536,128]{1,0:T(8,128)S(1)}, f32[48,128]{1,0:T(8,128)S(1)}) custom-call(s32[8]{0:T(128)S(1)} %copy-done.8, s32[8]{0:T(128)S(1)} %collective-permute-done.1.count1_ref, bf16[3,8,8320]{2,1,0:T(8,128)(2,1)S(1)} %collective-permute-done.q_ref, bf16[8,128,512]{2,1,0:T(8,128)(2,1)S(1)} %copy-done.1, bf16[8,128,512]{2,1,0:T(8,128)(2,1)S(1)} %copy-done.3, ...), custom_call_target="tpu_custom_call" | custom-call | flops 201326592 | bytes 4980736 | tf_op jit(solution)/shard_map/pallas_call | solution.py:533
  53.5 0.6 shard_map.113
  54.2 5.6 %collective-permute-start.8 = (bf16[1584,128]{1,0:T(8,128)(2,1)S(1)}, bf16[1584,128]{1,0:T(8,128)(2,1)S(1)}, u32[]{:S(2)}, u32[]{:S(2)}) collective-permute-start(bf16[1584,128]{1,0:T(8,128)(2,1)S(1)} %shard_map.113), channel_id=1, source_target_pairs={{0,12},{2,14},{4,8},{6,10},{8,4},{10,6},{12,0},{14,2},{1,13},{3,15... | collective-permute-start | bytes 1216520 | tf_op jit(solution)/shard_map/ppermute | solution.py:501
  59.7 1.2 %collective-permute-done.5.near_ref = bf16[1584,128]{1,0:T(8,128)(2,1)S(1)} collective-permute-done((bf16[1584,128]{1,0:T(8,128)(2,1)S(1)}, bf16[1584,128]{1,0:T(8,128)(2,1)S(1)}, u32[]{:S(2)}, u32[]{:S(2)}) %collective-permute-start.5) | collective-permute-done | bytes 405536 | tf_op jit(solution)/shard_map/ppermute | solution.py:501
  60.9 9.9 %collective-permute-done.8.far_ref = bf16[1584,128]{1,0:T(8,128)(2,1)S(1)} collective-permute-done((bf16[1584,128]{1,0:T(8,128)(2,1)S(1)}, bf16[1584,128]{1,0:T(8,128)(2,1)S(1)}, u32[]{:S(2)}, u32[]{:S(2)}) %collective-permute-start.8) | collective-permute-done | bytes 405536 | tf_op jit(solution)/shard_map/ppermute | solution.py:501
  70.8 1.8 %shard_map.114 = bf16[3,8,8192]{2,1,0:T(8,128)(2,1)} custom-call(f32[1536,128]{1,0:T(8,128)S(1)} %get-tuple-element.14.num_ref, f32[48,128]{1,0:T(8,128)S(1)} %get-tuple-element.15.stat_ref, bf16[1584,128]{1,0:T(8,128)(2,1)S(1)} %collective-permute-done.5.near_ref, bf16[1584,128]{1,0:T(8,128)(2,1)S(1)} %collective-permute-done.8.far_ref), custom_call_target="tpu_custom_call" | custom-call | bytes 1966080 | tf_op jit(solution)/shard_map/pallas_call | solution.py:572
  (21 shorter events, 0.1 us)
Async XLA Ops:
  0.0 1.2 %copy-start.10 = (s32[8,3]{0,1:T(4,128)S(1)}, s32[8,3]{0,1:T(4,128)}, u32[]{:S(2)}) copy-start(s32[8,3]{0,1:T(4,128)} %param.21) | copy-start | bytes 292
  0.0 8.6 %collective-permute-start.2 = (bf16[8,128,512]{2,1,0:T(8,128)(2,1)}, bf16[8,128,512]{2,1,0:T(8,128)(2,1)S(1)}, u32[]{:S(2)}, u32[]{:S(2)}) collective-permute-start(bf16[8,128,512]{2,1,0:T(8,128)(2,1)} %k0.7), channel_id=1, source_target_pairs={{0,2},{2,0},{4,6},{6,4},{8,10},{10,8},{12,14},{14,12},{1,3},{3,1},... | collective-permute-start | bytes 3145736 | tf_op jit(solution)/shard_map/ppermute | solution.py:501
  0.5 8.2 %collective-permute-start.3 = (bf16[8,128,512]{2,1,0:T(8,128)(2,1)}, bf16[8,128,512]{2,1,0:T(8,128)(2,1)S(1)}, u32[]{:S(2)}, u32[]{:S(2)}) collective-permute-start(bf16[8,128,512]{2,1,0:T(8,128)(2,1)} %v0.7), channel_id=1, source_target_pairs={{0,2},{2,0},{4,6},{6,4},{8,10},{10,8},{12,14},{14,12},{1,3},{3,1},... | collective-permute-start | bytes 3145736 | tf_op jit(solution)/shard_map/ppermute | solution.py:501
  1.3 6.2 %copy-start.8 = (s32[8]{0:T(128)S(1)}, s32[8]{0:T(128)}, u32[]{:S(2)}) copy-start(s32[8]{0:T(128)} %count0_ref.7) | copy-start | bytes 100
  1.3 7.3 %copy-start.6 = (bf16[8,3,512]{2,0,1:T(8,128)(2,1)S(1)}, bf16[8,3,512]{2,0,1:T(8,128)(2,1)}, u32[]{:S(2)}) copy-start(bf16[8,3,512]{2,0,1:T(8,128)(2,1)} %param.18) | copy-start | bytes 73732
  1.4 7.3 %copy-start.7 = (bf16[8,3,512]{2,0,1:T(8,128)(2,1)S(1)}, bf16[8,3,512]{2,0,1:T(8,128)(2,1)}, u32[]{:S(2)}) copy-start(bf16[8,3,512]{2,0,1:T(8,128)(2,1)} %param.19) | copy-start | bytes 73732
  2.4 19.1 %collective-permute-start = (bf16[3,8,8320]{2,1,0:T(8,128)(2,1)S(1)}, bf16[3,8,8320]{2,1,0:T(8,128)(2,1)S(1)}, u32[]{:S(2)}, u32[]{:S(2)}) collective-permute-start(bf16[3,8,8320]{2,1,0:T(8,128)(2,1)S(1)} %pad_maximum_fusion.q_ref), channel_id=1, source_target_pairs={{0,12},{2,14},{4,8},{6,10},{8,4},{10,6},{12,0},{14,2},{1,13},{3,15... | collective-permute-start | bytes 1198088 | tf_op jit(solution)/shard_map/ppermute | solution.py:501
  7.5 1.1 %collective-permute-start.1 = (s32[8]{0:T(128)S(1)}, s32[8]{0:T(128)S(1)}, u32[]{:S(2)}, u32[]{:S(2)}) collective-permute-start(s32[8]{0:T(128)S(1)} %copy-done.8), channel_id=1, source_target_pairs={{0,2},{2,0},{4,6},{6,4},{8,10},{10,8},{12,14},{14,12},{1,3},{3,1},... | collective-permute-start | bytes 104 | tf_op jit(solution)/shard_map/ppermute | solution.py:501
  8.7 0.7 copy-start.9
  9.3 1.2 %copy-start = (bf16[8,128,512]{2,1,0:T(8,128)(2,1)S(1)}, bf16[8,128,512]{2,1,0:T(8,128)(2,1)}, u32[]{:S(2)}) copy-start(bf16[8,128,512]{2,1,0:T(8,128)(2,1)} %k0.7) | copy-start | bytes 3145732
  10.5 1.2 %copy-start.2 = (bf16[8,128,512]{2,1,0:T(8,128)(2,1)S(1)}, bf16[8,128,512]{2,1,0:T(8,128)(2,1)}, u32[]{:S(2)}) copy-start(bf16[8,128,512]{2,1,0:T(8,128)(2,1)} %v0.7) | copy-start | bytes 3145732
  11.8 1.2 %copy-start.4 = (bf16[8,128,512]{2,1,0:T(8,128)(2,1)S(1)}, bf16[8,128,512]{2,1,0:T(8,128)(2,1)}, u32[]{:S(2)}) copy-start(bf16[8,128,512]{2,1,0:T(8,128)(2,1)} %leaf_k.1) | copy-start | bytes 3145732
  13.0 1.2 %copy-start.5 = (bf16[8,128,512]{2,1,0:T(8,128)(2,1)S(1)}, bf16[8,128,512]{2,1,0:T(8,128)(2,1)}, u32[]{:S(2)}) copy-start(bf16[8,128,512]{2,1,0:T(8,128)(2,1)} %leaf_v.1) | copy-start | bytes 3145732
  14.2 21.2 %copy-start.1 = (bf16[8,128,512]{2,1,0:T(8,128)(2,1)S(1)}, bf16[8,128,512]{2,1,0:T(8,128)(2,1)}, u32[]{:S(2)}) copy-start(bf16[8,128,512]{2,1,0:T(8,128)(2,1)} %k0.7) | copy-start | bytes 3145732
  14.2 21.2 %copy-start.3 = (bf16[8,128,512]{2,1,0:T(8,128)(2,1)S(1)}, bf16[8,128,512]{2,1,0:T(8,128)(2,1)}, u32[]{:S(2)}) copy-start(bf16[8,128,512]{2,1,0:T(8,128)(2,1)} %v0.7) | copy-start | bytes 3145732
  21.5 14.0 %collective-permute-start.6 = (bf16[3,8,8320]{2,1,0:T(8,128)(2,1)S(1)}, bf16[3,8,8320]{2,1,0:T(8,128)(2,1)S(1)}, u32[]{:S(2)}, u32[]{:S(2)}) collective-permute-start(bf16[3,8,8320]{2,1,0:T(8,128)(2,1)S(1)} %collective-permute-done.q_ref), channel_id=1, source_target_pairs={{0,4},{2,6},{4,0},{6,2},{8,12},{10,14},{12,8},{14,10},{1,5},{3,7},... | collective-permute-start | bytes 1198088 | tf_op jit(solution)/shard_map/ppermute | solution.py:501
  25.3 18.7 %collective-permute-start.4 = (bf16[3,8,8320]{2,1,0:T(8,128)(2,1)S(1)}, bf16[3,8,8320]{2,1,0:T(8,128)(2,1)S(1)}, u32[]{:S(2)}, u32[]{:S(2)}) collective-permute-start(bf16[3,8,8320]{2,1,0:T(8,128)(2,1)S(1)} %pad_maximum_fusion.q_ref), channel_id=1, source_target_pairs={{0,4},{2,6},{4,0},{6,2},{8,12},{10,14},{12,8},{14,10},{1,5},{3,7},... | collective-permute-start | bytes 1198088 | tf_op jit(solution)/shard_map/ppermute | solution.py:501
  40.0 13.6 %collective-permute-start.7 = (bf16[1584,128]{1,0:T(8,128)(2,1)S(1)}, bf16[1584,128]{1,0:T(8,128)(2,1)S(1)}, u32[]{:S(2)}, u32[]{:S(2)}) collective-permute-start(bf16[1584,128]{1,0:T(8,128)(2,1)S(1)} %shard_map.112), channel_id=1, source_target_pairs={{0,4},{2,6},{4,0},{6,2},{8,12},{10,14},{12,8},{14,10},{1,5},{3,7},... | collective-permute-start | bytes 1216520 | tf_op jit(solution)/shard_map/ppermute | solution.py:501
  48.0 12.9 %collective-permute-start.5 = (bf16[1584,128]{1,0:T(8,128)(2,1)S(1)}, bf16[1584,128]{1,0:T(8,128)(2,1)S(1)}, u32[]{:S(2)}, u32[]{:S(2)}) collective-permute-start(bf16[1584,128]{1,0:T(8,128)(2,1)S(1)} %shard_map.110), channel_id=1, source_target_pairs={{0,4},{2,6},{4,0},{6,2},{8,12},{10,14},{12,8},{14,10},{1,5},{3,7},... | collective-permute-start | bytes 1216520 | tf_op jit(solution)/shard_map/ppermute | solution.py:501
  54.2 16.7 %collective-permute-start.8 = (bf16[1584,128]{1,0:T(8,128)(2,1)S(1)}, bf16[1584,128]{1,0:T(8,128)(2,1)S(1)}, u32[]{:S(2)}, u32[]{:S(2)}) collective-permute-start(bf16[1584,128]{1,0:T(8,128)(2,1)S(1)} %shard_map.113), channel_id=1, source_target_pairs={{0,12},{2,14},{4,8},{6,10},{8,4},{10,6},{12,0},{14,2},{1,13},{3,15... | collective-permute-start | bytes 1216520 | tf_op jit(solution)/shard_map/ppermute | solution.py:501

commit v3 on v0

--- a/solution.py
+++ b/solution.py
@@ -1,8 +1,11 @@
+import functools
 import math
 
 import jax
 import jax.numpy as jnp
 from jax import lax
+from jax.experimental import pallas as pl
+from jax.experimental.pallas import tpu as pltpu
 from jax.sharding import PartitionSpec as P
 
 HD = 128
@@ -188,9 +191,463 @@
     )
 
 
+NEG = -(2.0**127)
+CORES = 2
+PATH_ROWS = 16
+
+
+def pair_sums(tile):
+    return tile + pltpu.roll(tile, tile.shape[1] - 1, 1)
+
+
+def two_pieces(values):
+    high = values.astype(jnp.bfloat16).astype(jnp.float32)
+    low = (values - high).astype(jnp.bfloat16).astype(jnp.float32)
+    return high, low
+
+
+def dot_nt(a, b):
+    return lax.dot_general(a, b, (((1,), (1,)), ((), ())), preferred_element_type=jnp.float32)
+
+
+def dot_nn(a, b):
+    return lax.dot_general(a, b, (((1,), (0,)), ((), ())), preferred_element_type=jnp.float32)
+
+
+def plain_call(kernel, out_shape, in_memory, scratch=(), flops=0, num_bytes=0):
+    return pl.pallas_call(
+        kernel,
+        out_shape=out_shape,
+        in_specs=[pl.BlockSpec(memory_space=space) for space in in_memory],
+        out_specs=tuple(pl.BlockSpec(memory_space=pltpu.VMEM) for _ in out_shape),
+        scratch_shapes=list(scratch),
+        compiler_params=pltpu.CompilerParams(vmem_limit_bytes=16 * 1024 * 1024),
+        cost_estimate=pl.CostEstimate(flops=flops, bytes_accessed=num_bytes, transcendentals=0),
+    )
+
+
+class Sizes:
+    def __init__(self, requests, steps, kv, group, levels, pages, page_tok):
+        self.requests, self.steps, self.kv, self.group = requests, steps, kv, group
+        self.levels, self.pages, self.page_tok = levels, pages, page_tok
+        self.rows = steps * group
+        self.step_rows = kv * group
+        self.all_rows = requests * kv * self.rows
+        self.per_tile = HD // (4 * kv)
+        self.tile_count = -(-requests // self.per_tile)
+        self.stat_rows = self.tile_count * self.rows
+        self.factor = 1.0 / math.sqrt(HD) * math.log2(math.e)
+
+    def tiles(self):
+        for tile_at in range(self.tile_count):
+            first = tile_at * self.per_tile
+            yield tile_at, first, min(self.requests, first + self.per_tile)
+
+    def read_table(self, q_ref, counts, table_words, table_ref, sem):
+        words = q_ref[self.all_rows : self.all_rows + PATH_ROWS, :]
+        table_words[:PATH_ROWS, :] = words.astype(jnp.float32).astype(jnp.int32)
+        for at, count_ref in enumerate(counts):
+            table_words[PATH_ROWS + at : PATH_ROWS + at + 1, : self.pages] = count_ref[...].reshape(1, self.pages)
+        copy = pltpu.make_async_copy(table_words, table_ref, sem)
+        copy.start()
+        return copy
+
+    def span(self, request, kv_head):
+        at = (request * self.kv + kv_head) * self.rows
+        return pl.ds(at if isinstance(at, int) else pl.multiple_of(at, 16), self.rows)
+
+    def find(self, table_ref, owner, which, request):
+        slot, used = jnp.int32(0), jnp.int32(0)
+        for level in range(self.levels):
+            hit = table_ref[level, request] == owner
+            slot = jnp.where(hit, table_ref[self.levels + level, request], slot)
+            used = jnp.where(hit, 1, used)
+        return slot, used * table_ref[PATH_ROWS + which, slot]
+
+
+def shared_kernel(
+    sz, chunk, exact, count0_ref, count1_ref, q_ref, k0, v0, k1, v1, *rest
+):
+    *outs, table_words, table_ref, sem = rest
+    num_ref = outs[0]
+    me = lax.axis_index("page")
+    mate = jnp.bitwise_xor(me, 1)
+    lane_ids = lax.broadcasted_iota(jnp.int32, (sz.rows, HD), 1)
+    token_ids = lax.broadcasted_iota(jnp.int32, (sz.rows, sz.page_tok), 1)
+    heads = range(sz.kv)
+    copy = sz.read_table(q_ref, (count0_ref, count1_ref), table_words, table_ref, sem)
+    copy.wait()
+    for tile_at, first, last in sz.tiles():
+        tile = jnp.zeros((sz.rows, HD), jnp.float32)
+        for start in range(first, last, 4):
+            items = []
+            for request in range(start, min(last, start + 4)):
+                slot0, count0 = sz.find(table_ref, me, 0, chunk * sz.requests + request)
+                slot1, count1 = sz.find(table_ref, mate, 1, chunk * sz.requests + request)
+                allowed = jnp.concatenate([token_ids < count0, token_ids < count1], axis=1)
+                items += [(request, head, slot0, slot1, allowed) for head in heads]
+            scores = []
+            for request, head, slot0, slot1, allowed in items:
+                cols = slice(head * HD, (head + 1) * HD)
+                keys = jnp.concatenate([k0[slot0, :, cols], k1[slot1, :, cols]], 0)
+                s = dot_nt(q_ref[sz.span(request, head), :], keys)
+                scores.append(jnp.where(allowed, s, NEG))
+            point = [sum(two_pieces(jnp.max(s, axis=1, keepdims=True))) for s in scores]
+            weights = [jnp.exp2((s - p) * sz.factor) for s, p in zip(scores, point)]
+            total = [jnp.sum(w, axis=1, keepdims=True) for w in weights]
+            for at, (request, head, slot0, slot1, _) in enumerate(items):
+                cols = slice(head * HD, (head + 1) * HD)
+                values = jnp.concatenate([v0[slot0, :, cols], v1[slot1, :, cols]], 0)
+                num = dot_nn(weights[at].astype(jnp.bfloat16), values)
+                num_ref[sz.span(request, head), :] = num.astype(num_ref.dtype)
+                lane = ((request - first) * sz.kv + head) * 4
+                tile = jnp.where(lane_ids == lane, point[at], tile)
+                tile = jnp.where(lane_ids == lane + 2, total[at], tile)
+        if exact:
+            outs[1][pl.ds(tile_at * sz.rows, sz.rows), :] = tile
+        else:
+            put_stats(sz, num_ref, tile_at, tile)
+
+
+def put_stats(sz, out_ref, tile_at, tile):
+    kind = lax.broadcasted_iota(jnp.int32, tile.shape, 1) % 4
+    high, low = two_pieces(tile)
+    tile = jnp.where(kind % 2 == 0, high, pltpu.roll(low, 1, 1))
+    out_ref[pl.ds(sz.all_rows + tile_at * sz.rows, sz.rows), :] = tile.astype(jnp.bfloat16)
+
+
+def local_kernel(
+    sz,
+    chunk,
+    count0_ref,
+    count1_ref,
+    leaf_count_ref,
+    q_ref,
+    k0,
+    v0,
+    k1,
+    v1,
+    leaf_k_any,
+    leaf_v_any,
+    new_k,
+    new_v,
+    num_ref,
+    stat_ref,
+    table_words,
+    table_ref,
+    sem,
+    fresh_k,
+    fresh_v,
+    leaf_k,
+    leaf_v,
+    leaf_sem,
+):
+    def leaf_copy(request, whole, part, sem_at):
+        return pltpu.make_async_copy(
+            whole.at[chunk * sz.requests + request], part.at[request], leaf_sem.at[request, sem_at]
+        )
+
+    for request in range(sz.requests):
+        leaf_copy(request, leaf_k_any, leaf_k, 0).start()
+        leaf_copy(request, leaf_v_any, leaf_v, 1).start()
+    me = lax.axis_index("page")
+    mate = jnp.bitwise_xor(me, 1)
+    lane_ids = lax.broadcasted_iota(jnp.int32, (sz.rows, HD), 1)
+    token_ids = lax.broadcasted_iota(jnp.int32, (sz.rows, sz.page_tok), 1)
+    fresh = fresh_k.shape[0]
+    fresh_ids = lax.broadcasted_iota(jnp.int32, (sz.rows, fresh), 1)
+    step_ids = lax.broadcasted_iota(jnp.int32, (sz.rows, fresh), 0) // sz.group
+    device_requests = new_k.shape[1]
+    causal = (fresh_ids // device_requests) <= step_ids
+    fresh_request = fresh_ids % device_requests
+    heads = range(sz.kv)
+    cols = [slice(head * HD, (head + 1) * HD) for head in heads]
+    copy = sz.read_table(q_ref, (count0_ref, count1_ref), table_words, table_ref, sem)
+    copy.wait()
+    for new_ref, full in ((new_k, fresh_k), (new_v, fresh_v)):
+        rows = [new_ref[step].astype(jnp.float32) for step in range(sz.steps)]
+        filler = fresh - sz.steps * device_requests
+        if filler:
+            rows.append(jnp.zeros((filler, sz.kv * HD), jnp.float32))
+        full[...] = jnp.concatenate(rows, axis=0).astype(full.dtype)
+    for tile_at, first, last in sz.tiles():
+        tile = jnp.zeros((sz.rows, HD), jnp.float32)
+        for start in range(first, last, 2):
+            items = []
+            for request in range(start, min(last, start + 2)):
+                row = chunk * sz.requests + request
+                slot0, count0 = sz.find(table_ref, me, 0, row)
+                slot1, count1 = sz.find(table_ref, mate, 1, row)
+                allowed = (
+                    token_ids < count0,
+                    token_ids < count1,
+                    token_ids < leaf_count_ref[row],
+                    causal & (fresh_request == row),
+                )
+                allowed = jnp.concatenate(allowed, axis=1)
+                places = ((k0, v0, slot0), (k1, v1, slot1), (leaf_k, leaf_v, request))
+                items += [(request, head, places, allowed) for head in heads]
+                leaf_copy(request, leaf_k_any, leaf_k, 0).wait()
+                leaf_copy(request, leaf_v_any, leaf_v, 1).wait()
+            scores = []
+            for request, head, places, allowed in items:
+                keys = [keys[at, :, cols[head]] for keys, _, at in places]
+                keys = jnp.concatenate(keys + [fresh_k[:, cols[head]]], 0)
+                s = dot_nt(q_ref[sz.span(request, head), :], keys)
+                scores.append(jnp.where(allowed, s, NEG))
+            top = [jnp.max(s, axis=1, keepdims=True) for s in scores]
+            weights = [jnp.exp2((s - t) * sz.factor) for s, t in zip(scores, top)]
+            total = [jnp.sum(w, axis=1, keepdims=True) for w in weights]
+            for at, (request, head, places, _) in enumerate(items):
+                values = [values[slot, :, cols[head]] for _, values, slot in places]
+                values = jnp.concatenate(values + [fresh_v[:, cols[head]]], 0)
+                num_ref[sz.span(request, head), :] = dot_nn(
+                    weights[at].astype(jnp.bfloat16), values
+                )
+                lane = ((request - first) * sz.kv + head) * 4
+                tile = jnp.where(lane_ids == lane, top[at], tile)
+                tile = jnp.where(lane_ids == lane + 2, total[at], tile)
+        stat_ref[pl.ds(tile_at * sz.rows, sz.rows), :] = tile
+
+
+def merge_kernel(sz, num_ref, stat_ref, came_ref, out_ref):
+    for tile_at, first, last in sz.tiles():
+        came_span = pl.ds(sz.all_rows + tile_at * sz.rows, sz.rows)
+        mine = stat_ref[pl.ds(tile_at * sz.rows, sz.rows), :]
+        came = pair_sums(came_ref[came_span, :].astype(jnp.float32))
+        top = jnp.maximum(mine, came)
+        keep, add = jnp.exp2((mine - top) * sz.factor), jnp.exp2((came - top) * sz.factor)
+        total = mine * pltpu.roll(keep, 2, 1) + came * pltpu.roll(add, 2, 1)
+        kind = lax.broadcasted_iota(jnp.int32, top.shape, 1) % 4
+        put_stats(sz, out_ref, tile_at, jnp.where(kind == 0, top, total))
+        for request in range(first, last):
+            for head in range(sz.kv):
+                lane = ((request - first) * sz.kv + head) * 4
+                span = sz.span(request, head)
+                joined = num_ref[span, :] * keep[:, lane : lane + 1]
+                joined = joined + came_ref[span, :].astype(jnp.float32) * add[:, lane : lane + 1]
+                out_ref[span, :] = joined.astype(jnp.bfloat16)
+
+
+def join_kernel(sz, num_ref, stat_ref, came_ref, out_ref, out_stat_ref):
+    mine = stat_ref[...]
+    came = pair_sums(came_ref[sz.all_rows : sz.all_rows + sz.rows, :].astype(jnp.float32))
+    top = jnp.maximum(mine, came)
+    keep, add = jnp.exp2((mine - top) * sz.factor), jnp.exp2((came - top) * sz.factor)
+    total = mine * pltpu.roll(keep, 2, 1) + came * pltpu.roll(add, 2, 1)
+    kind = lax.broadcasted_iota(jnp.int32, top.shape, 1) % 4
+    out_stat_ref[...] = jnp.where(kind == 0, top, total)
+    for request in range(sz.requests):
+        for head in range(sz.kv):
+            lane = (request * sz.kv + head) * 4
+            span = sz.span(request, head)
+            joined = num_ref[span, :] * keep[:, lane : lane + 1]
+            out_ref[span, :] = joined + came_ref[span, :].astype(jnp.float32) * add[
+                :, lane : lane + 1
+            ]
+
+
+def final_kernel(whole, sz, num_ref, stat_ref, *refs):
+    *came_refs, out_ref, wide = refs
+    lanes = sz.requests * sz.kv * 4
+    lane_ids = lax.broadcasted_iota(jnp.int32, (sz.rows, HD), 1)
+    mine = stat_ref[...]
+    came = jnp.zeros((sz.rows, HD), jnp.float32)
+    for chunk, came_ref in enumerate(came_refs):
+        tile = pair_sums(came_ref[sz.all_rows : sz.all_rows + sz.rows, :].astype(jnp.float32))
+        if chunk:
+            tile = pltpu.roll(tile, chunk * lanes, 1)
+        came = jnp.where(lane_ids // lanes == chunk, tile, came)
+    top = jnp.maximum(mine, came)
+    keep, add = jnp.exp2((mine - top) * sz.factor), jnp.exp2((came - top) * sz.factor)
+    total = mine * pltpu.roll(keep, 2, 1) + came * pltpu.roll(add, 2, 1)
+    total = pltpu.roll(total, HD - 2, 1)
+    keep, add = keep / total, add / total
+    for row in range(whole.requests):
+        chunk, request = row // sz.requests, row % sz.requests
+        for head in range(sz.kv):
+            lane = (row * sz.kv + head) * 4
+            joined = num_ref[whole.span(row, head), :] * keep[:, lane : lane + 1]
+            joined = joined + came_refs[chunk][sz.span(request, head), :].astype(
+                jnp.float32
+            ) * add[:, lane : lane + 1]
+            for step in range(sz.steps):
+                at = (step * sz.step_rows + head * sz.group) * whole.requests
+                wide[pl.ds(at + row, sz.group, stride=whole.requests), :] = joined[
+                    step * sz.group : (step + 1) * sz.group
+                ]
+    for step in range(sz.steps):
+        for head in range(sz.step_rows):
+            at = (step * sz.step_rows + head) * whole.requests
+            out_ref[step, :, head * HD : (head + 1) * HD] = wide[
+                at : at + whole.requests, :
+            ].astype(jnp.bfloat16)
+
+
+def fetch_kernel(k_any, v_any, k_ref, v_ref, sems):
+    copies = [
+        pltpu.make_async_copy(source, target, sems.at[at])
+        for at, (source, target) in enumerate(((k_any, k_ref), (v_any, v_ref)))
+    ]
+    for copy in copies:
+        copy.start()
+    for copy in copies:
+        copy.wait()
+
+
+def pack_kernel(sz, chunks, q_ref, owner_ref, slot_ref, *refs):
+    *outs, wide, words = refs
+    all_requests = chunks * sz.requests
+    words[...] = jnp.zeros(words.shape, words.dtype)
+    words[: sz.levels, :all_requests] = owner_ref[...]
+    words[sz.levels : 2 * sz.levels, :all_requests] = slot_ref[...]
+    paths = words[...].astype(jnp.float32).astype(jnp.bfloat16)
+    for out in outs:
+        out[sz.all_rows : sz.all_rows + PATH_ROWS, :] = paths
+    for step in range(sz.steps):
+        for head in range(sz.step_rows):
+            at = (step * sz.step_rows + head) * all_requests
+            wide[at : at + all_requests, :] = q_ref[
+                step, :, head * HD : (head + 1) * HD
+            ].astype(jnp.float32)
+    for chunk, out in enumerate(outs):
+        for request in range(sz.requests):
+            for head in range(sz.kv):
+                parts = []
+                for step in range(sz.steps):
+                    at = (step * sz.step_rows + head * sz.group) * all_requests
+                    at = at + chunk * sz.requests + request
+                    parts.append(wide[pl.ds(at, sz.group, stride=all_requests), :])
+                rows = jnp.concatenate(parts, axis=0).astype(out.dtype)
+                out[sz.span(request, head), :] = rows
+
+
+def line_shards(
+    queries,
+    page_keys,
+    page_values,
+    page_count,
+    leaf_keys,
+    leaf_values,
+    leaf_count,
+    new_keys,
+    new_values,
+    path_owner,
+    path_slot,
+):
+    requests, steps, width = queries.shape
+    owners = lax.axis_size("page")
+    kv = page_keys.shape[2] // HD
+    pages, page_tok = page_keys.shape[:2]
+    chunks = 1
+    line = (queries, page_keys, page_values, page_count, leaf_keys, leaf_values, leaf_count)
+    if requests % chunks or requests * kv * 4 != HD:
+        return shards(*line, new_keys, new_values, path_owner, path_slot)
+    shape_of = (steps, kv, QH // KVH, path_owner.shape[1], pages, page_tok)
+    whole, sz = Sizes(requests, *shape_of), Sizes(requests // chunks, *shape_of)
+
+    def exchange(array, hop):
+        return lax.ppermute(array, "page", [(at, at ^ hop) for at in range(owners)])
+
+    def after(array, *others):
+        return lax.optimization_barrier((array, *others))[0]
+
+    near, far = CORES, owners - CORES
+    smem, vmem, hbm = pltpu.SMEM, pltpu.VMEM, pl.ANY
+    shape = jax.ShapeDtypeStruct
+    scratch = (
+        pltpu.VMEM((PATH_ROWS + 8, HD), jnp.int32),
+        pltpu.SMEM((PATH_ROWS + 8, HD), jnp.int32),
+        pltpu.SemaphoreType.DMA,
+    )
+    wide = pltpu.VMEM((whole.all_rows, HD), jnp.float32)
+    fresh_rows = -(-requests * steps // page_tok) * page_tok
+    fresh = pltpu.VMEM((fresh_rows, kv * HD), jnp.bfloat16)
+    leaves = pltpu.VMEM((requests, page_tok, kv * HD), jnp.bfloat16)
+
+    def sent(size):
+        return (shape((size.all_rows + size.stat_rows, HD), jnp.bfloat16),)
+
+    def exact(size):
+        return (
+            shape((size.all_rows, HD), jnp.float32),
+            shape((size.stat_rows, HD), jnp.float32),
+        )
+
+    (block,) = plain_call(
+        functools.partial(pack_kernel, sz, chunks),
+        (shape((whole.all_rows + PATH_ROWS, HD), jnp.bfloat16),),
+        [vmem] * 3,
+        [wide, pltpu.VMEM((PATH_ROWS, HD), jnp.int32)],
+    )(*(jnp.swapaxes(array, 0, 1) for array in (queries, path_owner, path_slot)))
+    far_q = exchange(block, far)
+    near_q = exchange(block, near)
+    mate_keys, mate_values, mate_count = (
+        exchange(array, 1) for array in (page_keys, page_values, page_count)
+    )
+    counts = (page_count, mate_count)
+    own_pages = plain_call(
+        fetch_kernel,
+        (shape(page_keys.shape, page_keys.dtype),) * 2,
+        [hbm] * 2,
+        [pltpu.SemaphoreType.DMA((2,))],
+    )(after(page_keys, block), page_values)
+    all_pages = (*own_pages, mate_keys, mate_values)
+    far_q = after(far_q, *all_pages, mate_count)
+
+    def shared(size, chunk, is_exact, rows):
+        return plain_call(
+            functools.partial(shared_kernel, size, chunk, is_exact),
+            exact(size) if is_exact else sent(size),
+            [vmem] * 7,
+            scratch,
+        )(*counts, rows, *all_pages)
+
+    def merge(part, came):
+        return plain_call(functools.partial(merge_kernel, sz), sent(sz), [vmem] * 3)(*part, came)[0]
+
+    cross_q = exchange(far_q, near)
+    near_q = after(near_q, far_q)
+    far_part = shared(sz, 0, True, after(far_q, near_q))
+    cross_q = after(cross_q, *far_part)
+    cross_part = shared(sz, 0, False, cross_q)[0]
+    cross_back = exchange(cross_part, near)
+    near_part = shared(sz, 0, False, after(near_q, cross_part))[0]
+    cross_back = after(cross_back, near_part)
+    joined = merge(far_part, cross_back)
+    far_back = exchange(joined, far)
+    near_back = exchange(after(near_part, joined), near)
+    local = plain_call(
+        functools.partial(local_kernel, whole, 0),
+        exact(whole),
+        [vmem] * 2 + [smem] + [vmem] * 5 + [hbm] * 2 + [vmem] * 2,
+        [*scratch, fresh, fresh, leaves, leaves, pltpu.SemaphoreType.DMA((requests, 2))],
+    )(
+        *counts,
+        leaf_count,
+        after(block, joined),
+        *all_pages,
+        leaf_keys,
+        leaf_values,
+        jnp.swapaxes(new_keys, 0, 1),
+        jnp.swapaxes(new_values, 0, 1),
+    )
+    state = plain_call(functools.partial(join_kernel, whole), exact(whole), [vmem] * 3)(
+        *local, after(near_back, *local)
+    )
+    (out,) = plain_call(
+        functools.partial(final_kernel, whole, sz),
+        (shape((steps, requests, width), jnp.bfloat16),),
+        [vmem] * 3,
+        [wide],
+    )(*state, far_back)
+    return jnp.swapaxes(out, 0, 1)
+
+
 def solution(mesh):
+    on_line = mesh.shape["sub"] == 1 and mesh.shape["page"] == 4 * CORES
     return jax.shard_map(
-        shards,
+        line_shards if on_line else shards,
         mesh=mesh,
         in_specs=(
             P(("groups", "page", "sub"), None, "head"),

time: 295 us -> 67.4 us (0.23)
  waiting for transfers between devices: 131 us -> 27.4 us
  local copies, waits for them, and re-layouts: 93.2 us -> 4.8 us
  blocking collectives: 19.7 us -> 0 us
  Pallas kernels: 0 us -> 16.8 us
  matrix products: 16 us -> 0 us
  other arithmetic: 16 us -> 0 us
    all_to_all x3 -> x0, waiting for transfers between devices: 131 us -> none  [the longest x1 71.6 us: shards(): lax.all_to_all(outgoing, 'page', split_axis=0, concat_axis=0, tiled=True)]
    gather x32 -> x0, local copies, waits for them, and re-layouts: 57 us -> none  [the longest x3 18.3 us: shards(): jnp.take(queries, item_of_slot // level_count, axis=0)]
    ppermute x0 -> x9, waiting for transfers between devices: none -> 27.4 us  [exchange(): return lax.ppermute(array, 'page', [(at, at ^ hop) for at in range(owners)])]
    all_to_all x2 -> x0, blocking collectives: 19.7 us -> none  [the longest x1 9.87 us: shards(): lax.all_to_all(states[2], 'page', split_axis=0, concat_axis=0, tiled=True)]
    ppermute x0 -> x9, starting transfers between devices: none -> 18.1 us  [exchange(): return lax.ppermute(array, 'page', [(at, at ^ hop) for at in range(owners)])]
    pallas_call x0 -> x9, Pallas kernels: none -> 16.8 us  [the longest x1 7.17 us: line_shards(): plain_call(functools.partial(local_kernel, whole, 0), exact(whole), [vmem...]
    all_to_all x3 -> x0, starting transfers between devices: 16.1 us -> none  [the longest x1 6.33 us: shards(): lax.all_to_all(page_ids, 'page', split_axis=0, concat_axis=0, tiled=True)]
    dot_general x20 -> x0, matrix products: 16 us -> none  [the longest x8 5.98 us: page_states(): jnp.einsum('nskgd,ntkd->nskgt', query_five, key_heads, preferred_element_...]
  transfers between devices with their start and end apart: 3 -> 9, of which waited for: 2 -> 6; matrix products, arithmetic and copies ran while one was open for 12% -> 0% of each run, Pallas kernels for 0% -> 18%
where the time goes in v3:
time: 67.4 us; the launch traced here: 67.2 us
  waiting for transfers between devices  27.4 us (41%)
  starting transfers between devices  18.1 us (27%)
  Pallas kernels  16.8 us (25%)
  local copies, waits for them, and re-layouts  4.8 us (7%)
    ppermute x9, waiting for transfers between devices, exchange(): return lax.ppermute(array, 'page', [(at, at ^ hop) for at in range(owners)])  27.4 us
    ppermute x9, starting transfers between devices, exchange(): return lax.ppermute(array, 'page', [(at, at ^ hop) for at in range(owners)])  18.1 us
    pallas_call x1, Pallas kernels, line_shards(): plain_call(functools.partial(local_kernel, whole, 0), exact(whole), [vmem...  7.17 us
    pallas_call x3, Pallas kernels, shared(): plain_call(functools.partial(shared_kernel, size, chunk, is_exact), exact...  6.48 us
    unnamed x22, local copies, waits for them, and re-layouts  4.8 us
    pallas_call x1, Pallas kernels, line_shards(): plain_call(functools.partial(final_kernel, whole, sz), (shape((steps, req...  1.53 us
  transfers between devices with their start and end apart: 9, of which 6 were waited for; matrix products, arithmetic and copies ran while one was open for 0% of the time, Pallas kernels for 18%

profile of v3, /device:TPU:0, one launch (start us, length us, event | category | flops | bytes accessed | tf_op | source)
XLA Modules:
  0.0 67.2 jit_solution(16107140369850767635)
XLA Ops:
  0.0 0.5 collective-permute-start.2
  0.5 0.1 collective-permute-start.3
  0.5 0.7 %copy-done.9 = s32[8,3]{0,1:T(4,128)S(1)} copy-done((s32[8,3]{0,1:T(4,128)S(1)}, s32[8,3]{0,1:T(4,128)}, u32[]{:S(2)}) %copy-start.9) | copy-done | bytes 120
  1.2 0.0 copy-done.8
  1.2 1.0 %copy-done.4 = bf16[8,3,8192]{2,0,1:T(8,128)(2,1)S(1)} copy-done((bf16[8,3,8192]{2,0,1:T(8,128)(2,1)S(1)}, bf16[8,3,8192]{2,0,1:T(8,128)(2,1)}, u32[]{:S(2)}) %copy-start.4) | copy-done | bytes 393240
  2.2 0.2 shard_map.109.q_ref
  2.4 5.1 %collective-permute-start.1 = (bf16[1552,128]{1,0:T(8,128)(2,1)S(1)}, bf16[1552,128]{1,0:T(8,128)(2,1)S(1)}, u32[]{:S(2)}, u32[]{:S(2)}) collective-permute-start(bf16[1552,128]{1,0:T(8,128)(2,1)S(1)} %shard_map.109.q_ref), channel_id=1, source_target_pairs={{0,12},{2,14},{4,8},{6,10},{8,4},{10,6},{12,0},{14,2},{1,13},{3,15... | collective-permute-start | bytes 1191944 | tf_op jit(solution)/shard_map/ppermute | solution.py:550
  7.5 0.0 copy-start
  7.5 1.2 %copy-done = bf16[8,128,512]{2,1,0:T(8,128)(2,1)S(1)} copy-done((bf16[8,128,512]{2,1,0:T(8,128)(2,1)S(1)}, bf16[8,128,512]{2,1,0:T(8,128)(2,1)}, u32[]{:S(2)}) %copy-start) | copy-done | bytes 1048600
  8.7 1.2 %copy-done.1 = bf16[8,128,512]{2,1,0:T(8,128)(2,1)S(1)} copy-done((bf16[8,128,512]{2,1,0:T(8,128)(2,1)S(1)}, bf16[8,128,512]{2,1,0:T(8,128)(2,1)}, u32[]{:S(2)}) %copy-start.1) | copy-done | bytes 1048600
  10.0 0.2 shard_map.110
  10.1 7.5 %collective-permute-done.1.q_ref = bf16[1552,128]{1,0:T(8,128)(2,1)S(1)} collective-permute-done((bf16[1552,128]{1,0:T(8,128)(2,1)S(1)}, bf16[1552,128]{1,0:T(8,128)(2,1)S(1)}, u32[]{:S(2)}, u32[]{:S(2)}) %collective-permute-start.1) | collective-permute-done | bytes 397344 | tf_op jit(solution)/shard_map/ppermute | solution.py:550
  17.6 7.5 %collective-permute-start.5 = (bf16[1552,128]{1,0:T(8,128)(2,1)S(1)}, bf16[1552,128]{1,0:T(8,128)(2,1)S(1)}, u32[]{:S(2)}, u32[]{:S(2)}) collective-permute-start(bf16[1552,128]{1,0:T(8,128)(2,1)S(1)} %collective-permute-done.1.q_ref), channel_id=1, source_target_pairs={{0,4},{2,6},{4,0},{6,2},{8,12},{10,14},{12,8},{14,10},{1,5},{3,7},... | collective-permute-start | bytes 1191944 | tf_op jit(solution)/shard_map/ppermute | solution.py:550
  25.1 0.5 collective-permute-done.4.q_ref
  25.6 2.1 %shard_map.111 = (f32[1536,128]{1,0:T(8,128)S(1)}, f32[48,128]{1,0:T(8,128)S(1)}) custom-call(s32[8]{0:T(128)S(1)} %copy-done.7, s32[8]{0:T(128)S(1)} %collective-permute-done.count1_ref, bf16[1552,128]{1,0:T(8,128)(2,1)S(1)} %collective-permute-done.1.q_ref, bf16[8,128,512]{2,1,0:T(8,128)(2,1)S(1)} %get-tuple-element.24.k0, ...), custom_call_target="tpu_custom_call" | custom-call | tf_op jit(solution)/shard_map/pallas_call | solution.py:599
  27.7 6.3 %collective-permute-done.5.q_ref = bf16[1552,128]{1,0:T(8,128)(2,1)S(1)} collective-permute-done((bf16[1552,128]{1,0:T(8,128)(2,1)S(1)}, bf16[1552,128]{1,0:T(8,128)(2,1)S(1)}, u32[]{:S(2)}, u32[]{:S(2)}) %collective-permute-start.5) | collective-permute-done | bytes 397344 | tf_op jit(solution)/shard_map/ppermute | solution.py:550
  34.0 2.2 %shard_map.112 = bf16[1584,128]{1,0:T(8,128)(2,1)S(1)} custom-call(s32[8]{0:T(128)S(1)} %copy-done.7, s32[8]{0:T(128)S(1)} %collective-permute-done.count1_ref, bf16[1552,128]{1,0:T(8,128)(2,1)S(1)} %collective-permute-done.5.q_ref, bf16[8,128,512]{2,1,0:T(8,128)(2,1)S(1)} %get-tuple-element.24.k0, bf16[8,128,512]{2,1,0:T(8,128)(2,1)S(1)} %get-tuple-element.25.v0, ...), custom_call_target="tpu_custom_call" | custom-call | tf_op jit(solution)/shard_map/pallas_call | solution.py:599
  36.2 1.8 %collective-permute-start.6 = (bf16[1584,128]{1,0:T(8,128)(2,1)S(1)}, bf16[1584,128]{1,0:T(8,128)(2,1)S(1)}, u32[]{:S(2)}, u32[]{:S(2)}) collective-permute-start(bf16[1584,128]{1,0:T(8,128)(2,1)S(1)} %shard_map.112), channel_id=1, source_target_pairs={{0,4},{2,6},{4,0},{6,2},{8,12},{10,14},{12,8},{14,10},{1,5},{3,7},... | collective-permute-start | bytes 1216520 | tf_op jit(solution)/shard_map/ppermute | solution.py:550
  37.9 2.2 %shard_map.113 = bf16[1584,128]{1,0:T(8,128)(2,1)S(1)} custom-call(s32[8]{0:T(128)S(1)} %copy-done.7, s32[8]{0:T(128)S(1)} %collective-permute-done.count1_ref, bf16[1552,128]{1,0:T(8,128)(2,1)S(1)} %collective-permute-done.4.q_ref, bf16[8,128,512]{2,1,0:T(8,128)(2,1)S(1)} %get-tuple-element.24.k0, bf16[8,128,512]{2,1,0:T(8,128)(2,1)S(1)} %get-tuple-element.25.v0, ...), custom_call_target="tpu_custom_call" | custom-call | tf_op jit(solution)/shard_map/pallas_call | solution.py:599
  40.1 0.0 copy-start.2
  40.1 0.0 copy-start.5
  40.1 0.0 copy-start.6
  40.1 6.3 %collective-permute-done.6.came_ref = bf16[1584,128]{1,0:T(8,128)(2,1)S(1)} collective-permute-done((bf16[1584,128]{1,0:T(8,128)(2,1)S(1)}, bf16[1584,128]{1,0:T(8,128)(2,1)S(1)}, u32[]{:S(2)}, u32[]{:S(2)}) %collective-permute-start.6) | collective-permute-done | bytes 405536 | tf_op jit(solution)/shard_map/ppermute | solution.py:550
  46.4 0.6 shard_map.114
  47.0 1.4 %collective-permute-start.7 = (bf16[1584,128]{1,0:T(8,128)(2,1)S(1)}, bf16[1584,128]{1,0:T(8,128)(2,1)S(1)}, u32[]{:S(2)}, u32[]{:S(2)}) collective-permute-start(bf16[1584,128]{1,0:T(8,128)(2,1)S(1)} %shard_map.113), channel_id=1, source_target_pairs={{0,4},{2,6},{4,0},{6,2},{8,12},{10,14},{12,8},{14,10},{1,5},{3,7},... | collective-permute-start | bytes 1216520 | tf_op jit(solution)/shard_map/ppermute | solution.py:550
  48.4 1.8 %collective-permute-start.8 = (bf16[1584,128]{1,0:T(8,128)(2,1)S(1)}, bf16[1584,128]{1,0:T(8,128)(2,1)S(1)}, u32[]{:S(2)}, u32[]{:S(2)}) collective-permute-start(bf16[1584,128]{1,0:T(8,128)(2,1)S(1)} %shard_map.114), channel_id=1, source_target_pairs={{0,12},{2,14},{4,8},{6,10},{8,4},{10,6},{12,0},{14,2},{1,13},{3,15... | collective-permute-start | bytes 1216520 | tf_op jit(solution)/shard_map/ppermute | solution.py:550
  50.3 0.6 copy-done.10
  50.9 7.2 %shard_map.115 = (f32[1536,128]{1,0:T(8,128)S(1)}, f32[48,128]{1,0:T(8,128)S(1)}) custom-call(s32[8]{0:T(128)S(1)} %copy-done.7, s32[8]{0:T(128)S(1)} %collective-permute-done.count1_ref, s32[8]{0:T(128)S(1)} %copy-done.10, bf16[1552,128]{1,0:T(8,128)(2,1)S(1)} %shard_map.109.q_ref, bf16[8,128,512]{2,1,0:T(8,128)(2,1)S(1)} %get-tuple-element.24.k0, ...), custom_call_target="tpu_custom_call" | custom-call | tf_op jit(solution)/shard_map/pallas_call | solution.py:620
  58.1 1.4 %collective-permute-done.7.came_ref = bf16[1584,128]{1,0:T(8,128)(2,1)S(1)} collective-permute-done((bf16[1584,128]{1,0:T(8,128)(2,1)S(1)}, bf16[1584,128]{1,0:T(8,128)(2,1)S(1)}, u32[]{:S(2)}, u32[]{:S(2)}) %collective-permute-start.7) | collective-permute-done | bytes 405536 | tf_op jit(solution)/shard_map/ppermute | solution.py:550
  59.5 0.6 shard_map.116
  60.1 5.5 %collective-permute-done.8.refs_0_ = bf16[1584,128]{1,0:T(8,128)(2,1)S(1)} collective-permute-done((bf16[1584,128]{1,0:T(8,128)(2,1)S(1)}, bf16[1584,128]{1,0:T(8,128)(2,1)S(1)}, u32[]{:S(2)}, u32[]{:S(2)}) %collective-permute-start.8) | collective-permute-done | bytes 405536 | tf_op jit(solution)/shard_map/ppermute | solution.py:550
  65.6 1.5 %shard_map.117 = bf16[3,8,8192]{2,1,0:T(8,128)(2,1)} custom-call(f32[1536,128]{1,0:T(8,128)S(1)} %get-tuple-element.39.num_ref, f32[48,128]{1,0:T(8,128)S(1)} %get-tuple-element.40.stat_ref, bf16[1584,128]{1,0:T(8,128)(2,1)S(1)} %collective-permute-done.8.refs_0_), custom_call_target="tpu_custom_call" | custom-call | tf_op jit(solution)/shard_map/pallas_call | solution.py:638
  (17 shorter events, 0.0 us)
Async XLA Ops:
  0.0 17.6 %collective-permute-start.2 = (bf16[8,128,512]{2,1,0:T(8,128)(2,1)}, bf16[8,128,512]{2,1,0:T(8,128)(2,1)S(1)}, u32[]{:S(2)}, u32[]{:S(2)}) collective-permute-start(bf16[8,128,512]{2,1,0:T(8,128)(2,1)} %k_any), channel_id=1, source_target_pairs={{0,2},{2,0},{4,6},{6,4},{8,10},{10,8},{12,14},{14,12},{1,3},{3,1},... | collective-permute-start | bytes 3145736 | tf_op jit(solution)/shard_map/ppermute | solution.py:550
  0.5 17.2 %collective-permute-start.3 = (bf16[8,128,512]{2,1,0:T(8,128)(2,1)}, bf16[8,128,512]{2,1,0:T(8,128)(2,1)S(1)}, u32[]{:S(2)}, u32[]{:S(2)}) collective-permute-start(bf16[8,128,512]{2,1,0:T(8,128)(2,1)} %v_any.1), channel_id=1, source_target_pairs={{0,2},{2,0},{4,6},{6,4},{8,10},{10,8},{12,14},{14,12},{1,3},{3,1},... | collective-permute-start | bytes 3145736 | tf_op jit(solution)/shard_map/ppermute | solution.py:550
  0.5 0.7 %copy-start.9 = (s32[8,3]{0,1:T(4,128)S(1)}, s32[8,3]{0,1:T(4,128)}, u32[]{:S(2)}) copy-start(s32[8,3]{0,1:T(4,128)} %param.21) | copy-start | bytes 292
  0.5 0.7 %copy-start.8 = (s32[8,3]{0,1:T(4,128)S(1)}, s32[8,3]{0,1:T(4,128)}, u32[]{:S(2)}) copy-start(s32[8,3]{0,1:T(4,128)} %param.20) | copy-start | bytes 292
  1.2 1.0 %copy-start.4 = (bf16[8,3,8192]{2,0,1:T(8,128)(2,1)S(1)}, bf16[8,3,8192]{2,0,1:T(8,128)(2,1)}, u32[]{:S(2)}) copy-start(bf16[8,3,8192]{2,0,1:T(8,128)(2,1)} %param.11) | copy-start | bytes 1179652
  2.2 5.3 %copy-start.7 = (s32[8]{0:T(128)S(1)}, s32[8]{0:T(128)}, u32[]{:S(2)}) copy-start(s32[8]{0:T(128)} %count0_ref.7) | copy-start | bytes 100
  2.4 15.2 %collective-permute-start.1 = (bf16[1552,128]{1,0:T(8,128)(2,1)S(1)}, bf16[1552,128]{1,0:T(8,128)(2,1)S(1)}, u32[]{:S(2)}, u32[]{:S(2)}) collective-permute-start(bf16[1552,128]{1,0:T(8,128)(2,1)S(1)} %shard_map.109.q_ref), channel_id=1, source_target_pairs={{0,12},{2,14},{4,8},{6,10},{8,4},{10,6},{12,0},{14,2},{1,13},{3,15... | collective-permute-start | bytes 1191944 | tf_op jit(solution)/shard_map/ppermute | solution.py:550
  7.5 18.1 %collective-permute-start.4 = (bf16[1552,128]{1,0:T(8,128)(2,1)S(1)}, bf16[1552,128]{1,0:T(8,128)(2,1)S(1)}, u32[]{:S(2)}, u32[]{:S(2)}) collective-permute-start(bf16[1552,128]{1,0:T(8,128)(2,1)S(1)} %shard_map.109.q_ref), channel_id=1, source_target_pairs={{0,4},{2,6},{4,0},{6,2},{8,12},{10,14},{12,8},{14,10},{1,5},{3,7},... | collective-permute-start | bytes 1191944 | tf_op jit(solution)/shard_map/ppermute | solution.py:550
  7.5 2.6 %collective-permute-start = (s32[8]{0:T(128)S(1)}, s32[8]{0:T(128)S(1)}, u32[]{:S(2)}, u32[]{:S(2)}) collective-permute-start(s32[8]{0:T(128)S(1)} %copy-done.7), channel_id=1, source_target_pairs={{0,2},{2,0},{4,6},{6,4},{8,10},{10,8},{12,14},{14,12},{1,3},{3,1},... | collective-permute-start | bytes 104 | tf_op jit(solution)/shard_map/ppermute | solution.py:550
  7.5 1.2 %copy-start = (bf16[8,128,512]{2,1,0:T(8,128)(2,1)S(1)}, bf16[8,128,512]{2,1,0:T(8,128)(2,1)}, u32[]{:S(2)}) copy-start(bf16[8,128,512]{2,1,0:T(8,128)(2,1)} %k_any) | copy-start | bytes 3145732
  8.7 1.2 %copy-start.1 = (bf16[8,128,512]{2,1,0:T(8,128)(2,1)S(1)}, bf16[8,128,512]{2,1,0:T(8,128)(2,1)}, u32[]{:S(2)}) copy-start(bf16[8,128,512]{2,1,0:T(8,128)(2,1)} %v_any.1) | copy-start | bytes 3145732
  17.6 16.4 %collective-permute-start.5 = (bf16[1552,128]{1,0:T(8,128)(2,1)S(1)}, bf16[1552,128]{1,0:T(8,128)(2,1)S(1)}, u32[]{:S(2)}, u32[]{:S(2)}) collective-permute-start(bf16[1552,128]{1,0:T(8,128)(2,1)S(1)} %collective-permute-done.1.q_ref), channel_id=1, source_target_pairs={{0,4},{2,6},{4,0},{6,2},{8,12},{10,14},{12,8},{14,10},{1,5},{3,7},... | collective-permute-start | bytes 1191944 | tf_op jit(solution)/shard_map/ppermute | solution.py:550
  36.2 10.2 %collective-permute-start.6 = (bf16[1584,128]{1,0:T(8,128)(2,1)S(1)}, bf16[1584,128]{1,0:T(8,128)(2,1)S(1)}, u32[]{:S(2)}, u32[]{:S(2)}) collective-permute-start(bf16[1584,128]{1,0:T(8,128)(2,1)S(1)} %shard_map.112), channel_id=1, source_target_pairs={{0,4},{2,6},{4,0},{6,2},{8,12},{10,14},{12,8},{14,10},{1,5},{3,7},... | collective-permute-start | bytes 1216520 | tf_op jit(solution)/shard_map/ppermute | solution.py:550
  37.9 12.4 %copy-start.3 = (bf16[8,128,512]{2,1,0:T(8,128)(2,1)S(1)}, bf16[8,128,512]{2,1,0:T(8,128)(2,1)}, u32[]{:S(2)}) copy-start(bf16[8,128,512]{2,1,0:T(8,128)(2,1)} %leaf_v_any.1) | copy-start | bytes 3145732
  40.1 10.2 %copy-start.2 = (bf16[8,128,512]{2,1,0:T(8,128)(2,1)S(1)}, bf16[8,128,512]{2,1,0:T(8,128)(2,1)}, u32[]{:S(2)}) copy-start(bf16[8,128,512]{2,1,0:T(8,128)(2,1)} %leaf_k_any.1) | copy-start | bytes 3145732
  40.1 10.2 %copy-start.5 = (bf16[8,3,512]{2,0,1:T(8,128)(2,1)S(1)}, bf16[8,3,512]{2,0,1:T(8,128)(2,1)}, u32[]{:S(2)}) copy-start(bf16[8,3,512]{2,0,1:T(8,128)(2,1)} %param.18) | copy-start | bytes 73732
  40.1 10.2 %copy-start.6 = (bf16[8,3,512]{2,0,1:T(8,128)(2,1)S(1)}, bf16[8,3,512]{2,0,1:T(8,128)(2,1)}, u32[]{:S(2)}) copy-start(bf16[8,3,512]{2,0,1:T(8,128)(2,1)} %param.19) | copy-start | bytes 73732
  47.0 12.5 %collective-permute-start.7 = (bf16[1584,128]{1,0:T(8,128)(2,1)S(1)}, bf16[1584,128]{1,0:T(8,128)(2,1)S(1)}, u32[]{:S(2)}, u32[]{:S(2)}) collective-permute-start(bf16[1584,128]{1,0:T(8,128)(2,1)S(1)} %shard_map.113), channel_id=1, source_target_pairs={{0,4},{2,6},{4,0},{6,2},{8,12},{10,14},{12,8},{14,10},{1,5},{3,7},... | collective-permute-start | bytes 1216520 | tf_op jit(solution)/shard_map/ppermute | solution.py:550
  48.4 17.2 %collective-permute-start.8 = (bf16[1584,128]{1,0:T(8,128)(2,1)S(1)}, bf16[1584,128]{1,0:T(8,128)(2,1)S(1)}, u32[]{:S(2)}, u32[]{:S(2)}) collective-permute-start(bf16[1584,128]{1,0:T(8,128)(2,1)S(1)} %shard_map.114), channel_id=1, source_target_pairs={{0,12},{2,14},{4,8},{6,10},{8,4},{10,6},{12,0},{14,2},{1,13},{3,15... | collective-permute-start | bytes 1216520 | tf_op jit(solution)/shard_map/ppermute | solution.py:550
  50.3 0.7 copy-start.10

commit v4 on v3

--- a/solution.py
+++ b/solution.py
@@ -193,7 +193,6 @@
 
 NEG = -(2.0**127)
 CORES = 2
-PATH_ROWS = 16
 
 
 def pair_sums(tile):
@@ -243,54 +242,60 @@
             first = tile_at * self.per_tile
             yield tile_at, first, min(self.requests, first + self.per_tile)
 
-    def read_table(self, q_ref, counts, table_words, table_ref, sem):
-        words = q_ref[self.all_rows : self.all_rows + PATH_ROWS, :]
-        table_words[:PATH_ROWS, :] = words.astype(jnp.float32).astype(jnp.int32)
-        for at, count_ref in enumerate(counts):
-            table_words[PATH_ROWS + at : PATH_ROWS + at + 1, : self.pages] = count_ref[...].reshape(1, self.pages)
-        copy = pltpu.make_async_copy(table_words, table_ref, sem)
-        copy.start()
-        return copy
+    def spread(self, q_ref, wide):
+        for step in range(self.steps):
+            for head in range(self.step_rows):
+                at = (step * self.step_rows + head) * self.requests
+                wide[at : at + self.requests, :] = q_ref[
+                    step, :, head * HD : (head + 1) * HD
+                ].astype(jnp.float32)
+
+    def pick(self, wide, request, kv_head):
+        parts = []
+        for step in range(self.steps):
+            at = (step * self.step_rows + kv_head * self.group) * self.requests
+            parts.append(wide[pl.ds(at + request, self.group, stride=self.requests), :])
+        return jnp.concatenate(parts, axis=0).astype(jnp.bfloat16)
 
     def span(self, request, kv_head):
         at = (request * self.kv + kv_head) * self.rows
         return pl.ds(at if isinstance(at, int) else pl.multiple_of(at, 16), self.rows)
 
-    def find(self, table_ref, owner, which, request):
+    def find(self, table_ref, count_ref, owner, request):
         slot, used = jnp.int32(0), jnp.int32(0)
         for level in range(self.levels):
-            hit = table_ref[level, request] == owner
-            slot = jnp.where(hit, table_ref[self.levels + level, request], slot)
+            index = table_ref[level, request]
+            hit = index // self.pages == owner
+            slot = jnp.where(hit, index % self.pages, slot)
             used = jnp.where(hit, 1, used)
-        return slot, used * table_ref[PATH_ROWS + which, slot]
+        return slot, used * count_ref[slot]
 
 
 def shared_kernel(
-    sz, chunk, exact, count0_ref, count1_ref, q_ref, k0, v0, k1, v1, *rest
+    sz, chunk, exact, table_ref, count0_ref, count1_ref, q_ref, k0, v0, k1, v1, *rest
 ):
-    *outs, table_words, table_ref, sem = rest
+    *outs, wide = rest
     num_ref = outs[0]
     me = lax.axis_index("page")
     mate = jnp.bitwise_xor(me, 1)
     lane_ids = lax.broadcasted_iota(jnp.int32, (sz.rows, HD), 1)
     token_ids = lax.broadcasted_iota(jnp.int32, (sz.rows, sz.page_tok), 1)
     heads = range(sz.kv)
-    copy = sz.read_table(q_ref, (count0_ref, count1_ref), table_words, table_ref, sem)
-    copy.wait()
+    sz.spread(q_ref, wide)
     for tile_at, first, last in sz.tiles():
         tile = jnp.zeros((sz.rows, HD), jnp.float32)
         for start in range(first, last, 4):
             items = []
             for request in range(start, min(last, start + 4)):
-                slot0, count0 = sz.find(table_ref, me, 0, chunk * sz.requests + request)
-                slot1, count1 = sz.find(table_ref, mate, 1, chunk * sz.requests + request)
+                slot0, count0 = sz.find(table_ref, count0_ref, me, request)
+                slot1, count1 = sz.find(table_ref, count1_ref, mate, request)
                 allowed = jnp.concatenate([token_ids < count0, token_ids < count1], axis=1)
                 items += [(request, head, slot0, slot1, allowed) for head in heads]
             scores = []
             for request, head, slot0, slot1, allowed in items:
                 cols = slice(head * HD, (head + 1) * HD)
                 keys = jnp.concatenate([k0[slot0, :, cols], k1[slot1, :, cols]], 0)
-                s = dot_nt(q_ref[sz.span(request, head), :], keys)
+                s = dot_nt(sz.pick(wide, request, head), keys)
                 scores.append(jnp.where(allowed, s, NEG))
             point = [sum(two_pieces(jnp.max(s, axis=1, keepdims=True))) for s in scores]
             weights = [jnp.exp2((s - p) * sz.factor) for s, p in zip(scores, point)]
@@ -319,6 +324,7 @@
 def local_kernel(
     sz,
     chunk,
+    table_ref,
     count0_ref,
     count1_ref,
     leaf_count_ref,
@@ -333,9 +339,7 @@
     new_v,
     num_ref,
     stat_ref,
-    table_words,
-    table_ref,
-    sem,
+    wide,
     fresh_k,
     fresh_v,
     leaf_k,
@@ -362,8 +366,7 @@
     fresh_request = fresh_ids % device_requests
     heads = range(sz.kv)
     cols = [slice(head * HD, (head + 1) * HD) for head in heads]
-    copy = sz.read_table(q_ref, (count0_ref, count1_ref), table_words, table_ref, sem)
-    copy.wait()
+    sz.spread(q_ref, wide)
     for new_ref, full in ((new_k, fresh_k), (new_v, fresh_v)):
         rows = [new_ref[step].astype(jnp.float32) for step in range(sz.steps)]
         filler = fresh - sz.steps * device_requests
@@ -376,8 +379,8 @@
             items = []
             for request in range(start, min(last, start + 2)):
                 row = chunk * sz.requests + request
-                slot0, count0 = sz.find(table_ref, me, 0, row)
-                slot1, count1 = sz.find(table_ref, mate, 1, row)
+                slot0, count0 = sz.find(table_ref, count0_ref, me, row)
+                slot1, count1 = sz.find(table_ref, count1_ref, mate, row)
                 allowed = (
                     token_ids < count0,
                     token_ids < count1,
@@ -393,7 +396,7 @@
             for request, head, places, allowed in items:
                 keys = [keys[at, :, cols[head]] for keys, _, at in places]
                 keys = jnp.concatenate(keys + [fresh_k[:, cols[head]]], 0)
-                s = dot_nt(q_ref[sz.span(request, head), :], keys)
+                s = dot_nt(sz.pick(wide, request, head), keys)
                 scores.append(jnp.where(allowed, s, NEG))
             top = [jnp.max(s, axis=1, keepdims=True) for s in scores]
             weights = [jnp.exp2((s - t) * sz.factor) for s, t in zip(scores, top)]
@@ -495,33 +498,6 @@
         copy.wait()
 
 
-def pack_kernel(sz, chunks, q_ref, owner_ref, slot_ref, *refs):
-    *outs, wide, words = refs
-    all_requests = chunks * sz.requests
-    words[...] = jnp.zeros(words.shape, words.dtype)
-    words[: sz.levels, :all_requests] = owner_ref[...]
-    words[sz.levels : 2 * sz.levels, :all_requests] = slot_ref[...]
-    paths = words[...].astype(jnp.float32).astype(jnp.bfloat16)
-    for out in outs:
-        out[sz.all_rows : sz.all_rows + PATH_ROWS, :] = paths
-    for step in range(sz.steps):
-        for head in range(sz.step_rows):
-            at = (step * sz.step_rows + head) * all_requests
-            wide[at : at + all_requests, :] = q_ref[
-                step, :, head * HD : (head + 1) * HD
-            ].astype(jnp.float32)
-    for chunk, out in enumerate(outs):
-        for request in range(sz.requests):
-            for head in range(sz.kv):
-                parts = []
-                for step in range(sz.steps):
-                    at = (step * sz.step_rows + head * sz.group) * all_requests
-                    at = at + chunk * sz.requests + request
-                    parts.append(wide[pl.ds(at, sz.group, stride=all_requests), :])
-                rows = jnp.concatenate(parts, axis=0).astype(out.dtype)
-                out[sz.span(request, head), :] = rows
-
-
 def line_shards(
     queries,
     page_keys,
@@ -555,11 +531,6 @@
     near, far = CORES, owners - CORES
     smem, vmem, hbm = pltpu.SMEM, pltpu.VMEM, pl.ANY
     shape = jax.ShapeDtypeStruct
-    scratch = (
-        pltpu.VMEM((PATH_ROWS + 8, HD), jnp.int32),
-        pltpu.SMEM((PATH_ROWS + 8, HD), jnp.int32),
-        pltpu.SemaphoreType.DMA,
-    )
     wide = pltpu.VMEM((whole.all_rows, HD), jnp.float32)
     fresh_rows = -(-requests * steps // page_tok) * page_tok
     fresh = pltpu.VMEM((fresh_rows, kv * HD), jnp.bfloat16)
@@ -574,12 +545,8 @@
             shape((size.stat_rows, HD), jnp.float32),
         )
 
-    (block,) = plain_call(
-        functools.partial(pack_kernel, sz, chunks),
-        (shape((whole.all_rows + PATH_ROWS, HD), jnp.bfloat16),),
-        [vmem] * 3,
-        [wide, pltpu.VMEM((PATH_ROWS, HD), jnp.int32)],
-    )(*(jnp.swapaxes(array, 0, 1) for array in (queries, path_owner, path_slot)))
+    block = jnp.swapaxes(queries, 0, 1)
+    table = jnp.swapaxes(path_owner * pages + path_slot, 0, 1)
     far_q = exchange(block, far)
     near_q = exchange(block, near)
     mate_keys, mate_values, mate_count = (
@@ -591,28 +558,31 @@
         (shape(page_keys.shape, page_keys.dtype),) * 2,
         [hbm] * 2,
         [pltpu.SemaphoreType.DMA((2,))],
-    )(after(page_keys, block), page_values)
+    )(after(page_keys, mate_keys, mate_values, mate_count), page_values)
     all_pages = (*own_pages, mate_keys, mate_values)
-    far_q = after(far_q, *all_pages, mate_count)
-
-    def shared(size, chunk, is_exact, rows):
+    near_table, far_table, cross_table = (exchange(table, hop) for hop in (near, far, near ^ far))
+    far_q, near_table, far_table, cross_table = lax.optimization_barrier(
+        (far_q, near_table, far_table, cross_table, *all_pages, mate_count)
+    )[:4]
+
+    def shared(size, chunk, is_exact, paths, rows):
         return plain_call(
             functools.partial(shared_kernel, size, chunk, is_exact),
             exact(size) if is_exact else sent(size),
-            [vmem] * 7,
-            scratch,
-        )(*counts, rows, *all_pages)
+            [smem] * 3 + [vmem] * 5,
+            [wide],
+        )(paths, *counts, rows, *all_pages)
 
     def merge(part, came):
         return plain_call(functools.partial(merge_kernel, sz), sent(sz), [vmem] * 3)(*part, came)[0]
 
     cross_q = exchange(far_q, near)
     near_q = after(near_q, far_q)
-    far_part = shared(sz, 0, True, after(far_q, near_q))
+    far_part = shared(sz, 0, True, far_table, after(far_q, near_q))
     cross_q = after(cross_q, *far_part)
-    cross_part = shared(sz, 0, False, cross_q)[0]
+    cross_part = shared(sz, 0, False, cross_table, cross_q)[0]
     cross_back = exchange(cross_part, near)
-    near_part = shared(sz, 0, False, after(near_q, cross_part))[0]
+    near_part = shared(sz, 0, False, near_table, after(near_q, cross_part))[0]
     cross_back = after(cross_back, near_part)
     joined = merge(far_part, cross_back)
     far_back = exchange(joined, far)
@@ -620,9 +590,10 @@
     local = plain_call(
         functools.partial(local_kernel, whole, 0),
         exact(whole),
-        [vmem] * 2 + [smem] + [vmem] * 5 + [hbm] * 2 + [vmem] * 2,
-        [*scratch, fresh, fresh, leaves, leaves, pltpu.SemaphoreType.DMA((requests, 2))],
+        [smem] * 4 + [vmem] * 5 + [hbm] * 2 + [vmem] * 2,
+        [wide, fresh, fresh, leaves, leaves, pltpu.SemaphoreType.DMA((requests, 2))],
     )(
+        table,
         *counts,
         leaf_count,
         after(block, joined),

time: 67.4 us -> 65.6 us (0.973)
  waiting for transfers between devices: 27.4 us -> 30.7 us
  starting transfers between devices: 18.1 us -> 15.2 us
  local copies, waits for them, and re-layouts: 4.8 us -> 3.1 us
  Pallas kernels: 16.8 us -> 15.6 us
  other arithmetic: 0 us -> 0.7 us
    ppermute x9 -> x12, waiting for transfers between devices: 27.4 us -> 30.7 us  [exchange(): return lax.ppermute(array, 'page', [(at, at ^ hop) for at in range(owners)])]
    ppermute x9 -> x12, starting transfers between devices: 18.1 us -> 15.2 us  [exchange(): return lax.ppermute(array, 'page', [(at, at ^ hop) for at in range(owners)])]
    unnamed x22 -> x18, local copies, waits for them, and re-layouts: 4.8 us -> 3.1 us
    pallas_call x2 -> x1, Pallas kernels: 7.34 us -> 6.58 us  [line_shards(): plain_call(functools.partial(local_kernel, whole, 0), exact(whole), [smem...]
    transpose x0 -> x1, other arithmetic: none -> 0.7 us  [line_shards(): table = jnp.swapaxes(path_owner * pages + path_slot, 0, 1)]
  transfers between devices with their start and end apart: 9 -> 12, of which waited for: 6 -> 9; matrix products, arithmetic and copies ran while one was open for 0% -> 1% of each run, Pallas kernels for 18% -> 17%
where the time goes in v4:
time: 65.6 us; the launch traced here: 65.4 us
  waiting for transfers between devices  30.7 us (47%)
  Pallas kernels  15.6 us (24%)
  starting transfers between devices  15.2 us (23%)
  local copies, waits for them, and re-layouts  3.1 us (5%)
  other arithmetic  0.7 us (1%)
    ppermute x12, waiting for transfers between devices, exchange(): return lax.ppermute(array, 'page', [(at, at ^ hop) for at in range(owners)])  30.7 us
    ppermute x12, starting transfers between devices, exchange(): return lax.ppermute(array, 'page', [(at, at ^ hop) for at in range(owners)])  15.2 us
    pallas_call x1, Pallas kernels, line_shards(): plain_call(functools.partial(local_kernel, whole, 0), exact(whole), [smem...  6.58 us
    pallas_call x3, Pallas kernels, shared(): plain_call(functools.partial(shared_kernel, size, chunk, is_exact), exact...  6.03 us
    unnamed x18, local copies, waits for them, and re-layouts  3.1 us
    pallas_call x1, Pallas kernels, line_shards(): plain_call(functools.partial(final_kernel, whole, sz), (shape((steps, req...  1.53 us
  transfers between devices with their start and end apart: 12, of which 9 were waited for; matrix products, arithmetic and copies ran while one was open for 1% of the time, Pallas kernels for 17%

profile of v4, /device:TPU:0, one launch (start us, length us, event | category | flops | bytes accessed | tf_op | source)
XLA Modules:
  0.0 65.4 jit_solution(9733022776140246240)
XLA Ops:
  0.0 0.5 collective-permute-start.5
  0.5 0.1 collective-permute-start.6
  0.5 5.0 %collective-permute-start.1 = (bf16[3,8,8192]{2,1,0:T(8,128)(2,1)}, bf16[3,8,8192]{2,1,0:T(8,128)(2,1)S(1)}, u32[]{:S(2)}, u32[]{:S(2)}) collective-permute-start(bf16[3,8,8192]{2,1,0:T(8,128)(2,1)} %bitcast.6), channel_id=1, source_target_pairs={{0,12},{2,14},{4,8},{6,10},{8,4},{10,6},{12,0},{14,2},{1,13},{3,15... | collective-permute-start | bytes 1179656 | tf_op jit(solution)/shard_map/ppermute | solution.py:526
  5.6 0.7 %add_bitcast_fusion.table_ref = s32[3,8]{1,0:T(4,128)S(1)} fusion(s32[8,3]{0,1:T(4,128)} %param.21, s32[8,3]{0,1:T(4,128)} %param.20), kind=kLoop, calls=%fused_computation | loop fusion | flops 48 | bytes 288 | tf_op jit(solution)/shard_map/transpose | solution.py:549
  6.3 0.4 collective-permute-done.count1_ref
  6.7 1.0 %collective-permute-start.3 = (s32[3,8]{1,0:T(4,128)S(1)}, s32[3,8]{1,0:T(4,128)S(1)}, u32[]{:S(2)}, u32[]{:S(2)}) collective-permute-start(s32[3,8]{1,0:T(4,128)S(1)} %add_bitcast_fusion.table_ref), channel_id=1, source_target_pairs={{0,12},{2,14},{4,8},{6,10},{8,4},{10,6},{12,0},{14,2},{1,13},{3,15... | collective-permute-start | bytes 296 | tf_op jit(solution)/shard_map/ppermute | solution.py:526
  7.7 2.1 %collective-permute-start.4 = (s32[3,8]{1,0:T(4,128)S(1)}, s32[3,8]{1,0:T(4,128)S(1)}, u32[]{:S(2)}, u32[]{:S(2)}) collective-permute-start(s32[3,8]{1,0:T(4,128)S(1)} %add_bitcast_fusion.table_ref), channel_id=1, source_target_pairs={{0,8},{2,10},{4,12},{6,14},{8,0},{10,2},{12,4},{14,6},{1,9},{3,11}... | collective-permute-start | bytes 296 | tf_op jit(solution)/shard_map/ppermute | solution.py:526
  9.8 1.3 %collective-permute-start.7 = (bf16[3,8,8192]{2,1,0:T(8,128)(2,1)}, bf16[3,8,8192]{2,1,0:T(8,128)(2,1)S(1)}, u32[]{:S(2)}, u32[]{:S(2)}) collective-permute-start(bf16[3,8,8192]{2,1,0:T(8,128)(2,1)} %bitcast.7), channel_id=1, source_target_pairs={{0,4},{2,6},{4,0},{6,2},{8,12},{10,14},{12,8},{14,10},{1,5},{3,7},... | collective-permute-start | bytes 1179656 | tf_op jit(solution)/shard_map/ppermute | solution.py:526
  11.1 1.2 %copy-done = bf16[8,128,512]{2,1,0:T(8,128)(2,1)S(1)} copy-done((bf16[8,128,512]{2,1,0:T(8,128)(2,1)S(1)}, bf16[8,128,512]{2,1,0:T(8,128)(2,1)}, u32[]{:S(2)}) %copy-start) | copy-done | bytes 1048600
  12.3 1.2 %copy-done.1 = bf16[8,128,512]{2,1,0:T(8,128)(2,1)S(1)} copy-done((bf16[8,128,512]{2,1,0:T(8,128)(2,1)S(1)}, bf16[8,128,512]{2,1,0:T(8,128)(2,1)}, u32[]{:S(2)}) %copy-start.1) | copy-done | bytes 1048600
  13.5 0.2 shard_map.109
  13.7 1.8 %collective-permute-done.2.table_ref = s32[3,8]{1,0:T(4,128)S(1)} collective-permute-done((s32[3,8]{1,0:T(4,128)S(1)}, s32[3,8]{1,0:T(4,128)S(1)}, u32[]{:S(2)}, u32[]{:S(2)}) %collective-permute-start.2) | collective-permute-done | bytes 128 | tf_op jit(solution)/shard_map/ppermute | solution.py:526
  15.5 0.4 collective-permute-done.3.table_ref
  15.9 7.1 %collective-permute-done.4.table_ref = s32[3,8]{1,0:T(4,128)S(1)} collective-permute-done((s32[3,8]{1,0:T(4,128)S(1)}, s32[3,8]{1,0:T(4,128)S(1)}, u32[]{:S(2)}, u32[]{:S(2)}) %collective-permute-start.4) | collective-permute-done | bytes 128 | tf_op jit(solution)/shard_map/ppermute | solution.py:526
  23.0 0.4 collective-permute-start.8
  23.4 0.4 collective-permute-done.7.q_ref
  23.8 2.0 %shard_map.110 = (f32[1536,128]{1,0:T(8,128)S(1)}, f32[48,128]{1,0:T(8,128)S(1)}) custom-call(s32[3,8]{1,0:T(4,128)S(1)} %collective-permute-done.3.table_ref, s32[8]{0:T(128)S(1)} %copy-done.7, s32[8]{0:T(128)S(1)} %collective-permute-done.count1_ref, bf16[3,8,8192]{2,1,0:T(8,128)(2,1)S(1)} %collective-permute-done.1.q_ref, ...), custom_call_target="tpu_custom_call" | custom-call | tf_op jit(solution)/shard_map/pallas_call | solution.py:569
  25.8 7.1 %collective-permute-done.8.q_ref = bf16[3,8,8192]{2,1,0:T(8,128)(2,1)S(1)} collective-permute-done((bf16[3,8,8192]{2,1,0:T(8,128)(2,1)S(1)}, bf16[3,8,8192]{2,1,0:T(8,128)(2,1)S(1)}, u32[]{:S(2)}, u32[]{:S(2)}) %collective-permute-start.8) | collective-permute-done | bytes 393248 | tf_op jit(solution)/shard_map/ppermute | solution.py:526
  32.8 2.0 %shard_map.111 = bf16[1584,128]{1,0:T(8,128)(2,1)S(1)} custom-call(s32[3,8]{1,0:T(4,128)S(1)} %collective-permute-done.4.table_ref, s32[8]{0:T(128)S(1)} %copy-done.7, s32[8]{0:T(128)S(1)} %collective-permute-done.count1_ref, bf16[3,8,8192]{2,1,0:T(8,128)(2,1)S(1)} %collective-permute-done.8.q_ref, bf16[8,128,512]{2,1,0:T(8,128)(2,1)S(1)} %get-tuple-element.27.k0, ...), custom_call_target="tpu_custom_call" | custom-call | tf_op jit(solution)/shard_map/pallas_call | solution.py:569
  34.9 1.2 %collective-permute-start.9 = (bf16[1584,128]{1,0:T(8,128)(2,1)S(1)}, bf16[1584,128]{1,0:T(8,128)(2,1)S(1)}, u32[]{:S(2)}, u32[]{:S(2)}) collective-permute-start(bf16[1584,128]{1,0:T(8,128)(2,1)S(1)} %shard_map.111), channel_id=1, source_target_pairs={{0,4},{2,6},{4,0},{6,2},{8,12},{10,14},{12,8},{14,10},{1,5},{3,7},... | collective-permute-start | bytes 1216520 | tf_op jit(solution)/shard_map/ppermute | solution.py:526
  36.0 2.0 %shard_map.112 = bf16[1584,128]{1,0:T(8,128)(2,1)S(1)} custom-call(s32[3,8]{1,0:T(4,128)S(1)} %collective-permute-done.2.table_ref, s32[8]{0:T(128)S(1)} %copy-done.7, s32[8]{0:T(128)S(1)} %collective-permute-done.count1_ref, bf16[3,8,8192]{2,1,0:T(8,128)(2,1)S(1)} %collective-permute-done.7.q_ref, bf16[8,128,512]{2,1,0:T(8,128)(2,1)S(1)} %get-tuple-element.27.k0, ...), custom_call_target="tpu_custom_call" | custom-call | tf_op jit(solution)/shard_map/pallas_call | solution.py:569
  38.1 0.0 copy-start.5
  38.1 6.0 %collective-permute-done.9.came_ref = bf16[1584,128]{1,0:T(8,128)(2,1)S(1)} collective-permute-done((bf16[1584,128]{1,0:T(8,128)(2,1)S(1)}, bf16[1584,128]{1,0:T(8,128)(2,1)S(1)}, u32[]{:S(2)}, u32[]{:S(2)}) %collective-permute-start.9) | collective-permute-done | bytes 405536 | tf_op jit(solution)/shard_map/ppermute | solution.py:526
  44.1 0.6 shard_map.113
  44.8 1.8 %collective-permute-start.10 = (bf16[1584,128]{1,0:T(8,128)(2,1)S(1)}, bf16[1584,128]{1,0:T(8,128)(2,1)S(1)}, u32[]{:S(2)}, u32[]{:S(2)}) collective-permute-start(bf16[1584,128]{1,0:T(8,128)(2,1)S(1)} %shard_map.112), channel_id=1, source_target_pairs={{0,4},{2,6},{4,0},{6,2},{8,12},{10,14},{12,8},{14,10},{1,5},{3,7},... | collective-permute-start | bytes 1216520 | tf_op jit(solution)/shard_map/ppermute | solution.py:526
  46.6 1.9 %collective-permute-start.11 = (bf16[1584,128]{1,0:T(8,128)(2,1)S(1)}, bf16[1584,128]{1,0:T(8,128)(2,1)S(1)}, u32[]{:S(2)}, u32[]{:S(2)}) collective-permute-start(bf16[1584,128]{1,0:T(8,128)(2,1)S(1)} %shard_map.113), channel_id=1, source_target_pairs={{0,12},{2,14},{4,8},{6,10},{8,4},{10,6},{12,0},{14,2},{1,13},{3,15... | collective-permute-start | bytes 1216520 | tf_op jit(solution)/shard_map/ppermute | solution.py:526
  48.5 0.6 copy-done.8
  49.1 6.6 %shard_map.114 = (f32[1536,128]{1,0:T(8,128)S(1)}, f32[48,128]{1,0:T(8,128)S(1)}) custom-call(s32[3,8]{1,0:T(4,128)S(1)} %add_bitcast_fusion.table_ref, s32[8]{0:T(128)S(1)} %copy-done.7, s32[8]{0:T(128)S(1)} %collective-permute-done.count1_ref, s32[8]{0:T(128)S(1)} %copy-done.8, bf16[3,8,8192]{2,1,0:T(8,128)(2,1)S(1)} %bitcast.8, ...), custom_call_target="tpu_custom_call" | custom-call | tf_op jit(solution)/shard_map/pallas_call | solution.py:590
  55.7 0.7 %collective-permute-done.10.came_ref = bf16[1584,128]{1,0:T(8,128)(2,1)S(1)} collective-permute-done((bf16[1584,128]{1,0:T(8,128)(2,1)S(1)}, bf16[1584,128]{1,0:T(8,128)(2,1)S(1)}, u32[]{:S(2)}, u32[]{:S(2)}) %collective-permute-start.10) | collective-permute-done | bytes 405536 | tf_op jit(solution)/shard_map/ppermute | solution.py:526
  56.4 0.6 shard_map.115
  57.0 6.8 %collective-permute-done.11.refs_0_ = bf16[1584,128]{1,0:T(8,128)(2,1)S(1)} collective-permute-done((bf16[1584,128]{1,0:T(8,128)(2,1)S(1)}, bf16[1584,128]{1,0:T(8,128)(2,1)S(1)}, u32[]{:S(2)}, u32[]{:S(2)}) %collective-permute-start.11) | collective-permute-done | bytes 405536 | tf_op jit(solution)/shard_map/ppermute | solution.py:526
  63.9 1.5 %shard_map.116 = bf16[3,8,8192]{2,1,0:T(8,128)(2,1)} custom-call(f32[1536,128]{1,0:T(8,128)S(1)} %get-tuple-element.45.num_ref, f32[48,128]{1,0:T(8,128)S(1)} %get-tuple-element.46.stat_ref, bf16[1584,128]{1,0:T(8,128)(2,1)S(1)} %collective-permute-done.11.refs_0_), custom_call_target="tpu_custom_call" | custom-call | tf_op jit(solution)/shard_map/pallas_call | solution.py:609
  (19 shorter events, 0.0 us)
Async XLA Ops:
  0.0 5.6 %copy-start.7 = (s32[8]{0:T(128)S(1)}, s32[8]{0:T(128)}, u32[]{:S(2)}) copy-start(s32[8]{0:T(128)} %count0_ref.7) | copy-start | bytes 100
  0.0 7.7 %collective-permute-start.5 = (bf16[8,128,512]{2,1,0:T(8,128)(2,1)}, bf16[8,128,512]{2,1,0:T(8,128)(2,1)S(1)}, u32[]{:S(2)}, u32[]{:S(2)}) collective-permute-start(bf16[8,128,512]{2,1,0:T(8,128)(2,1)} %k_any), channel_id=1, source_target_pairs={{0,2},{2,0},{4,6},{6,4},{8,10},{10,8},{12,14},{14,12},{1,3},{3,1},... | collective-permute-start | bytes 3145736 | tf_op jit(solution)/shard_map/ppermute | solution.py:526
  0.5 9.3 %collective-permute-start.6 = (bf16[8,128,512]{2,1,0:T(8,128)(2,1)}, bf16[8,128,512]{2,1,0:T(8,128)(2,1)S(1)}, u32[]{:S(2)}, u32[]{:S(2)}) collective-permute-start(bf16[8,128,512]{2,1,0:T(8,128)(2,1)} %v_any.1), channel_id=1, source_target_pairs={{0,2},{2,0},{4,6},{6,4},{8,10},{10,8},{12,14},{14,12},{1,3},{3,1},... | collective-permute-start | bytes 3145736 | tf_op jit(solution)/shard_map/ppermute | solution.py:526
  0.5 22.5 %collective-permute-start.1 = (bf16[3,8,8192]{2,1,0:T(8,128)(2,1)}, bf16[3,8,8192]{2,1,0:T(8,128)(2,1)S(1)}, u32[]{:S(2)}, u32[]{:S(2)}) collective-permute-start(bf16[3,8,8192]{2,1,0:T(8,128)(2,1)} %bitcast.6), channel_id=1, source_target_pairs={{0,12},{2,14},{4,8},{6,10},{8,4},{10,6},{12,0},{14,2},{1,13},{3,15... | collective-permute-start | bytes 1179656 | tf_op jit(solution)/shard_map/ppermute | solution.py:526
  5.6 1.1 %collective-permute-start = (s32[8]{0:T(128)S(1)}, s32[8]{0:T(128)S(1)}, u32[]{:S(2)}, u32[]{:S(2)}) collective-permute-start(s32[8]{0:T(128)S(1)} %copy-done.7), channel_id=1, source_target_pairs={{0,2},{2,0},{4,6},{6,4},{8,10},{10,8},{12,14},{14,12},{1,3},{3,1},... | collective-permute-start | bytes 104 | tf_op jit(solution)/shard_map/ppermute | solution.py:526
  6.3 9.2 %collective-permute-start.2 = (s32[3,8]{1,0:T(4,128)S(1)}, s32[3,8]{1,0:T(4,128)S(1)}, u32[]{:S(2)}, u32[]{:S(2)}) collective-permute-start(s32[3,8]{1,0:T(4,128)S(1)} %add_bitcast_fusion.table_ref), channel_id=1, source_target_pairs={{0,4},{2,6},{4,0},{6,2},{8,12},{10,14},{12,8},{14,10},{1,5},{3,7},... | collective-permute-start | bytes 296 | tf_op jit(solution)/shard_map/ppermute | solution.py:526
  6.7 9.2 %collective-permute-start.3 = (s32[3,8]{1,0:T(4,128)S(1)}, s32[3,8]{1,0:T(4,128)S(1)}, u32[]{:S(2)}, u32[]{:S(2)}) collective-permute-start(s32[3,8]{1,0:T(4,128)S(1)} %add_bitcast_fusion.table_ref), channel_id=1, source_target_pairs={{0,12},{2,14},{4,8},{6,10},{8,4},{10,6},{12,0},{14,2},{1,13},{3,15... | collective-permute-start | bytes 296 | tf_op jit(solution)/shard_map/ppermute | solution.py:526
  7.7 15.3 %collective-permute-start.4 = (s32[3,8]{1,0:T(4,128)S(1)}, s32[3,8]{1,0:T(4,128)S(1)}, u32[]{:S(2)}, u32[]{:S(2)}) collective-permute-start(s32[3,8]{1,0:T(4,128)S(1)} %add_bitcast_fusion.table_ref), channel_id=1, source_target_pairs={{0,8},{2,10},{4,12},{6,14},{8,0},{10,2},{12,4},{14,6},{1,9},{3,11}... | collective-permute-start | bytes 296 | tf_op jit(solution)/shard_map/ppermute | solution.py:526
  9.8 14.0 %collective-permute-start.7 = (bf16[3,8,8192]{2,1,0:T(8,128)(2,1)}, bf16[3,8,8192]{2,1,0:T(8,128)(2,1)S(1)}, u32[]{:S(2)}, u32[]{:S(2)}) collective-permute-start(bf16[3,8,8192]{2,1,0:T(8,128)(2,1)} %bitcast.7), channel_id=1, source_target_pairs={{0,4},{2,6},{4,0},{6,2},{8,12},{10,14},{12,8},{14,10},{1,5},{3,7},... | collective-permute-start | bytes 1179656 | tf_op jit(solution)/shard_map/ppermute | solution.py:526
  11.1 1.2 %copy-start = (bf16[8,128,512]{2,1,0:T(8,128)(2,1)S(1)}, bf16[8,128,512]{2,1,0:T(8,128)(2,1)}, u32[]{:S(2)}) copy-start(bf16[8,128,512]{2,1,0:T(8,128)(2,1)} %k_any) | copy-start | bytes 3145732
  12.3 1.2 %copy-start.1 = (bf16[8,128,512]{2,1,0:T(8,128)(2,1)S(1)}, bf16[8,128,512]{2,1,0:T(8,128)(2,1)}, u32[]{:S(2)}) copy-start(bf16[8,128,512]{2,1,0:T(8,128)(2,1)} %v_any.1) | copy-start | bytes 3145732
  23.0 9.9 %collective-permute-start.8 = (bf16[3,8,8192]{2,1,0:T(8,128)(2,1)S(1)}, bf16[3,8,8192]{2,1,0:T(8,128)(2,1)S(1)}, u32[]{:S(2)}, u32[]{:S(2)}) collective-permute-start(bf16[3,8,8192]{2,1,0:T(8,128)(2,1)S(1)} %collective-permute-done.1.q_ref), channel_id=1, source_target_pairs={{0,4},{2,6},{4,0},{6,2},{8,12},{10,14},{12,8},{14,10},{1,5},{3,7},... | collective-permute-start | bytes 1179656 | tf_op jit(solution)/shard_map/ppermute | solution.py:526
  34.9 9.3 %collective-permute-start.9 = (bf16[1584,128]{1,0:T(8,128)(2,1)S(1)}, bf16[1584,128]{1,0:T(8,128)(2,1)S(1)}, u32[]{:S(2)}, u32[]{:S(2)}) collective-permute-start(bf16[1584,128]{1,0:T(8,128)(2,1)S(1)} %shard_map.111), channel_id=1, source_target_pairs={{0,4},{2,6},{4,0},{6,2},{8,12},{10,14},{12,8},{14,10},{1,5},{3,7},... | collective-permute-start | bytes 1216520 | tf_op jit(solution)/shard_map/ppermute | solution.py:526
  36.0 12.4 %copy-start.3 = (bf16[8,128,512]{2,1,0:T(8,128)(2,1)S(1)}, bf16[8,128,512]{2,1,0:T(8,128)(2,1)}, u32[]{:S(2)}) copy-start(bf16[8,128,512]{2,1,0:T(8,128)(2,1)} %leaf_v_any.1) | copy-start | bytes 3145732
  38.0 10.4 %copy-start.2 = (bf16[8,128,512]{2,1,0:T(8,128)(2,1)S(1)}, bf16[8,128,512]{2,1,0:T(8,128)(2,1)}, u32[]{:S(2)}) copy-start(bf16[8,128,512]{2,1,0:T(8,128)(2,1)} %leaf_k_any.1) | copy-start | bytes 3145732
  38.1 10.4 %copy-start.4 = (bf16[8,3,8192]{2,0,1:T(8,128)(2,1)S(1)}, bf16[8,3,8192]{2,0,1:T(8,128)(2,1)}, u32[]{:S(2)}) copy-start(bf16[8,3,8192]{2,0,1:T(8,128)(2,1)} %param.11) | copy-start | bytes 1179652
  38.1 10.4 %copy-start.5 = (bf16[8,3,512]{2,0,1:T(8,128)(2,1)S(1)}, bf16[8,3,512]{2,0,1:T(8,128)(2,1)}, u32[]{:S(2)}) copy-start(bf16[8,3,512]{2,0,1:T(8,128)(2,1)} %param.18) | copy-start | bytes 73732
  38.1 10.4 %copy-start.6 = (bf16[8,3,512]{2,0,1:T(8,128)(2,1)S(1)}, bf16[8,3,512]{2,0,1:T(8,128)(2,1)}, u32[]{:S(2)}) copy-start(bf16[8,3,512]{2,0,1:T(8,128)(2,1)} %param.19) | copy-start | bytes 73732
  44.8 11.6 %collective-permute-start.10 = (bf16[1584,128]{1,0:T(8,128)(2,1)S(1)}, bf16[1584,128]{1,0:T(8,128)(2,1)S(1)}, u32[]{:S(2)}, u32[]{:S(2)}) collective-permute-start(bf16[1584,128]{1,0:T(8,128)(2,1)S(1)} %shard_map.112), channel_id=1, source_target_pairs={{0,4},{2,6},{4,0},{6,2},{8,12},{10,14},{12,8},{14,10},{1,5},{3,7},... | collective-permute-start | bytes 1216520 | tf_op jit(solution)/shard_map/ppermute | solution.py:526
  46.6 17.3 %collective-permute-start.11 = (bf16[1584,128]{1,0:T(8,128)(2,1)S(1)}, bf16[1584,128]{1,0:T(8,128)(2,1)S(1)}, u32[]{:S(2)}, u32[]{:S(2)}) collective-permute-start(bf16[1584,128]{1,0:T(8,128)(2,1)S(1)} %shard_map.113), channel_id=1, source_target_pairs={{0,12},{2,14},{4,8},{6,10},{8,4},{10,6},{12,0},{14,2},{1,13},{3,15... | collective-permute-start | bytes 1216520 | tf_op jit(solution)/shard_map/ppermute | solution.py:526
  48.4 0.7 %copy-start.8 = (s32[8]{0:T(128)S(1)}, s32[8]{0:T(128)}, u32[]{:S(2)}) copy-start(s32[8]{0:T(128)} %leaf_count_ref.1) | copy-start | bytes 100

commit v5 on v4

--- a/solution.py
+++ b/solution.py
@@ -531,7 +531,7 @@
     near, far = CORES, owners - CORES
     smem, vmem, hbm = pltpu.SMEM, pltpu.VMEM, pl.ANY
     shape = jax.ShapeDtypeStruct
-    wide = pltpu.VMEM((whole.all_rows, HD), jnp.float32)
+    wide = pltpu.VMEM((whole.all_rows + requests, HD), jnp.float32)
     fresh_rows = -(-requests * steps // page_tok) * page_tok
     fresh = pltpu.VMEM((fresh_rows, kv * HD), jnp.bfloat16)
     leaves = pltpu.VMEM((requests, page_tok, kv * HD), jnp.bfloat16)

time: 65.6 us -> 65.6 us (level)
  no operation moved by 1% of the time
where the time goes in v5:
time: 65.6 us; the launch traced here: 65.4 us
  waiting for transfers between devices  30.7 us (47%)
  Pallas kernels  15.6 us (24%)
  starting transfers between devices  15.2 us (23%)
  local copies, waits for them, and re-layouts  3.1 us (5%)
  other arithmetic  0.7 us (1%)
    ppermute x12, waiting for transfers between devices, exchange(): return lax.ppermute(array, 'page', [(at, at ^ hop) for at in range(owners)])  30.7 us
    ppermute x12, starting transfers between devices, exchange(): return lax.ppermute(array, 'page', [(at, at ^ hop) for at in range(owners)])  15.2 us
    pallas_call x1, Pallas kernels, line_shards(): plain_call(functools.partial(local_kernel, whole, 0), exact(whole), [smem...  6.58 us
    pallas_call x3, Pallas kernels, shared(): plain_call(functools.partial(shared_kernel, size, chunk, is_exact), exact...  6.04 us
    unnamed x18, local copies, waits for them, and re-layouts  3.1 us
    pallas_call x1, Pallas kernels, line_shards(): plain_call(functools.partial(final_kernel, whole, sz), (shape((steps, req...  1.53 us
  transfers between devices with their start and end apart: 12, of which 9 were waited for; matrix products, arithmetic and copies ran while one was open for 1% of the time, Pallas kernels for 17%

profile of v5, /device:TPU:0, one launch (start us, length us, event | category | flops | bytes accessed | tf_op | source)
XLA Modules:
  0.0 65.4 jit_solution(7817080163916719371)
XLA Ops:
  0.0 0.5 collective-permute-start.5
  0.5 0.1 collective-permute-start.6
  0.5 5.0 %collective-permute-start.1 = (bf16[3,8,8192]{2,1,0:T(8,128)(2,1)}, bf16[3,8,8192]{2,1,0:T(8,128)(2,1)S(1)}, u32[]{:S(2)}, u32[]{:S(2)}) collective-permute-start(bf16[3,8,8192]{2,1,0:T(8,128)(2,1)} %bitcast.6), channel_id=1, source_target_pairs={{0,12},{2,14},{4,8},{6,10},{8,4},{10,6},{12,0},{14,2},{1,13},{3,15... | collective-permute-start | bytes 1179656 | tf_op jit(solution)/shard_map/ppermute | solution.py:526
  5.6 0.7 %add_bitcast_fusion.table_ref = s32[3,8]{1,0:T(4,128)S(1)} fusion(s32[8,3]{0,1:T(4,128)} %param.21, s32[8,3]{0,1:T(4,128)} %param.20), kind=kLoop, calls=%fused_computation | loop fusion | flops 48 | bytes 288 | tf_op jit(solution)/shard_map/transpose | solution.py:549
  6.3 0.4 collective-permute-done.count1_ref
  6.7 1.0 %collective-permute-start.3 = (s32[3,8]{1,0:T(4,128)S(1)}, s32[3,8]{1,0:T(4,128)S(1)}, u32[]{:S(2)}, u32[]{:S(2)}) collective-permute-start(s32[3,8]{1,0:T(4,128)S(1)} %add_bitcast_fusion.table_ref), channel_id=1, source_target_pairs={{0,12},{2,14},{4,8},{6,10},{8,4},{10,6},{12,0},{14,2},{1,13},{3,15... | collective-permute-start | bytes 296 | tf_op jit(solution)/shard_map/ppermute | solution.py:526
  7.7 2.1 %collective-permute-start.4 = (s32[3,8]{1,0:T(4,128)S(1)}, s32[3,8]{1,0:T(4,128)S(1)}, u32[]{:S(2)}, u32[]{:S(2)}) collective-permute-start(s32[3,8]{1,0:T(4,128)S(1)} %add_bitcast_fusion.table_ref), channel_id=1, source_target_pairs={{0,8},{2,10},{4,12},{6,14},{8,0},{10,2},{12,4},{14,6},{1,9},{3,11}... | collective-permute-start | bytes 296 | tf_op jit(solution)/shard_map/ppermute | solution.py:526
  9.8 1.3 %collective-permute-start.7 = (bf16[3,8,8192]{2,1,0:T(8,128)(2,1)}, bf16[3,8,8192]{2,1,0:T(8,128)(2,1)S(1)}, u32[]{:S(2)}, u32[]{:S(2)}) collective-permute-start(bf16[3,8,8192]{2,1,0:T(8,128)(2,1)} %bitcast.7), channel_id=1, source_target_pairs={{0,4},{2,6},{4,0},{6,2},{8,12},{10,14},{12,8},{14,10},{1,5},{3,7},... | collective-permute-start | bytes 1179656 | tf_op jit(solution)/shard_map/ppermute | solution.py:526
  11.1 1.2 %copy-done = bf16[8,128,512]{2,1,0:T(8,128)(2,1)S(1)} copy-done((bf16[8,128,512]{2,1,0:T(8,128)(2,1)S(1)}, bf16[8,128,512]{2,1,0:T(8,128)(2,1)}, u32[]{:S(2)}) %copy-start) | copy-done | bytes 1048600
  12.3 1.2 %copy-done.1 = bf16[8,128,512]{2,1,0:T(8,128)(2,1)S(1)} copy-done((bf16[8,128,512]{2,1,0:T(8,128)(2,1)S(1)}, bf16[8,128,512]{2,1,0:T(8,128)(2,1)}, u32[]{:S(2)}) %copy-start.1) | copy-done | bytes 1048600
  13.5 0.2 shard_map.109
  13.7 1.8 %collective-permute-done.2.table_ref = s32[3,8]{1,0:T(4,128)S(1)} collective-permute-done((s32[3,8]{1,0:T(4,128)S(1)}, s32[3,8]{1,0:T(4,128)S(1)}, u32[]{:S(2)}, u32[]{:S(2)}) %collective-permute-start.2) | collective-permute-done | bytes 128 | tf_op jit(solution)/shard_map/ppermute | solution.py:526
  15.5 0.4 collective-permute-done.3.table_ref
  15.9 7.1 %collective-permute-done.4.table_ref = s32[3,8]{1,0:T(4,128)S(1)} collective-permute-done((s32[3,8]{1,0:T(4,128)S(1)}, s32[3,8]{1,0:T(4,128)S(1)}, u32[]{:S(2)}, u32[]{:S(2)}) %collective-permute-start.4) | collective-permute-done | bytes 128 | tf_op jit(solution)/shard_map/ppermute | solution.py:526
  23.0 0.4 collective-permute-start.8
  23.4 0.4 collective-permute-done.7.q_ref
  23.8 2.0 %shard_map.110 = (f32[1536,128]{1,0:T(8,128)S(1)}, f32[48,128]{1,0:T(8,128)S(1)}) custom-call(s32[3,8]{1,0:T(4,128)S(1)} %collective-permute-done.3.table_ref, s32[8]{0:T(128)S(1)} %copy-done.7, s32[8]{0:T(128)S(1)} %collective-permute-done.count1_ref, bf16[3,8,8192]{2,1,0:T(8,128)(2,1)S(1)} %collective-permute-done.1.q_ref, ...), custom_call_target="tpu_custom_call" | custom-call | tf_op jit(solution)/shard_map/pallas_call | solution.py:569
  25.8 7.1 %collective-permute-done.8.q_ref = bf16[3,8,8192]{2,1,0:T(8,128)(2,1)S(1)} collective-permute-done((bf16[3,8,8192]{2,1,0:T(8,128)(2,1)S(1)}, bf16[3,8,8192]{2,1,0:T(8,128)(2,1)S(1)}, u32[]{:S(2)}, u32[]{:S(2)}) %collective-permute-start.8) | collective-permute-done | bytes 393248 | tf_op jit(solution)/shard_map/ppermute | solution.py:526
  32.8 2.0 %shard_map.111 = bf16[1584,128]{1,0:T(8,128)(2,1)S(1)} custom-call(s32[3,8]{1,0:T(4,128)S(1)} %collective-permute-done.4.table_ref, s32[8]{0:T(128)S(1)} %copy-done.7, s32[8]{0:T(128)S(1)} %collective-permute-done.count1_ref, bf16[3,8,8192]{2,1,0:T(8,128)(2,1)S(1)} %collective-permute-done.8.q_ref, bf16[8,128,512]{2,1,0:T(8,128)(2,1)S(1)} %get-tuple-element.27.k0, ...), custom_call_target="tpu_custom_call" | custom-call | tf_op jit(solution)/shard_map/pallas_call | solution.py:569
  34.9 1.2 %collective-permute-start.9 = (bf16[1584,128]{1,0:T(8,128)(2,1)S(1)}, bf16[1584,128]{1,0:T(8,128)(2,1)S(1)}, u32[]{:S(2)}, u32[]{:S(2)}) collective-permute-start(bf16[1584,128]{1,0:T(8,128)(2,1)S(1)} %shard_map.111), channel_id=1, source_target_pairs={{0,4},{2,6},{4,0},{6,2},{8,12},{10,14},{12,8},{14,10},{1,5},{3,7},... | collective-permute-start | bytes 1216520 | tf_op jit(solution)/shard_map/ppermute | solution.py:526
  36.0 2.0 %shard_map.112 = bf16[1584,128]{1,0:T(8,128)(2,1)S(1)} custom-call(s32[3,8]{1,0:T(4,128)S(1)} %collective-permute-done.2.table_ref, s32[8]{0:T(128)S(1)} %copy-done.7, s32[8]{0:T(128)S(1)} %collective-permute-done.count1_ref, bf16[3,8,8192]{2,1,0:T(8,128)(2,1)S(1)} %collective-permute-done.7.q_ref, bf16[8,128,512]{2,1,0:T(8,128)(2,1)S(1)} %get-tuple-element.27.k0, ...), custom_call_target="tpu_custom_call" | custom-call | tf_op jit(solution)/shard_map/pallas_call | solution.py:569
  38.1 0.0 copy-start.6
  38.1 6.0 %collective-permute-done.9.came_ref = bf16[1584,128]{1,0:T(8,128)(2,1)S(1)} collective-permute-done((bf16[1584,128]{1,0:T(8,128)(2,1)S(1)}, bf16[1584,128]{1,0:T(8,128)(2,1)S(1)}, u32[]{:S(2)}, u32[]{:S(2)}) %collective-permute-start.9) | collective-permute-done | bytes 405536 | tf_op jit(solution)/shard_map/ppermute | solution.py:526
  44.1 0.6 shard_map.113
  44.8 1.8 %collective-permute-start.10 = (bf16[1584,128]{1,0:T(8,128)(2,1)S(1)}, bf16[1584,128]{1,0:T(8,128)(2,1)S(1)}, u32[]{:S(2)}, u32[]{:S(2)}) collective-permute-start(bf16[1584,128]{1,0:T(8,128)(2,1)S(1)} %shard_map.112), channel_id=1, source_target_pairs={{0,4},{2,6},{4,0},{6,2},{8,12},{10,14},{12,8},{14,10},{1,5},{3,7},... | collective-permute-start | bytes 1216520 | tf_op jit(solution)/shard_map/ppermute | solution.py:526
  46.6 1.9 %collective-permute-start.11 = (bf16[1584,128]{1,0:T(8,128)(2,1)S(1)}, bf16[1584,128]{1,0:T(8,128)(2,1)S(1)}, u32[]{:S(2)}, u32[]{:S(2)}) collective-permute-start(bf16[1584,128]{1,0:T(8,128)(2,1)S(1)} %shard_map.113), channel_id=1, source_target_pairs={{0,12},{2,14},{4,8},{6,10},{8,4},{10,6},{12,0},{14,2},{1,13},{3,15... | collective-permute-start | bytes 1216520 | tf_op jit(solution)/shard_map/ppermute | solution.py:526
  48.5 0.6 copy-done.8
  49.1 6.6 %shard_map.114 = (f32[1536,128]{1,0:T(8,128)S(1)}, f32[48,128]{1,0:T(8,128)S(1)}) custom-call(s32[3,8]{1,0:T(4,128)S(1)} %add_bitcast_fusion.table_ref, s32[8]{0:T(128)S(1)} %copy-done.7, s32[8]{0:T(128)S(1)} %collective-permute-done.count1_ref, s32[8]{0:T(128)S(1)} %copy-done.8, bf16[3,8,8192]{2,1,0:T(8,128)(2,1)S(1)} %bitcast.8, ...), custom_call_target="tpu_custom_call" | custom-call | tf_op jit(solution)/shard_map/pallas_call | solution.py:590
  55.7 0.7 %collective-permute-done.10.came_ref = bf16[1584,128]{1,0:T(8,128)(2,1)S(1)} collective-permute-done((bf16[1584,128]{1,0:T(8,128)(2,1)S(1)}, bf16[1584,128]{1,0:T(8,128)(2,1)S(1)}, u32[]{:S(2)}, u32[]{:S(2)}) %collective-permute-start.10) | collective-permute-done | bytes 405536 | tf_op jit(solution)/shard_map/ppermute | solution.py:526
  56.4 0.6 shard_map.115
  57.0 6.8 %collective-permute-done.11.refs_0_ = bf16[1584,128]{1,0:T(8,128)(2,1)S(1)} collective-permute-done((bf16[1584,128]{1,0:T(8,128)(2,1)S(1)}, bf16[1584,128]{1,0:T(8,128)(2,1)S(1)}, u32[]{:S(2)}, u32[]{:S(2)}) %collective-permute-start.11) | collective-permute-done | bytes 405536 | tf_op jit(solution)/shard_map/ppermute | solution.py:526
  63.9 1.5 %shard_map.116 = bf16[3,8,8192]{2,1,0:T(8,128)(2,1)} custom-call(f32[1536,128]{1,0:T(8,128)S(1)} %get-tuple-element.45.num_ref, f32[48,128]{1,0:T(8,128)S(1)} %get-tuple-element.46.stat_ref, bf16[1584,128]{1,0:T(8,128)(2,1)S(1)} %collective-permute-done.11.refs_0_), custom_call_target="tpu_custom_call" | custom-call | tf_op jit(solution)/shard_map/pallas_call | solution.py:609
  (19 shorter events, 0.0 us)
Async XLA Ops:
  0.0 5.6 %copy-start.7 = (s32[8]{0:T(128)S(1)}, s32[8]{0:T(128)}, u32[]{:S(2)}) copy-start(s32[8]{0:T(128)} %count0_ref.7) | copy-start | bytes 100
  0.0 7.7 %collective-permute-start.5 = (bf16[8,128,512]{2,1,0:T(8,128)(2,1)}, bf16[8,128,512]{2,1,0:T(8,128)(2,1)S(1)}, u32[]{:S(2)}, u32[]{:S(2)}) collective-permute-start(bf16[8,128,512]{2,1,0:T(8,128)(2,1)} %k_any), channel_id=1, source_target_pairs={{0,2},{2,0},{4,6},{6,4},{8,10},{10,8},{12,14},{14,12},{1,3},{3,1},... | collective-permute-start | bytes 3145736 | tf_op jit(solution)/shard_map/ppermute | solution.py:526
  0.5 9.3 %collective-permute-start.6 = (bf16[8,128,512]{2,1,0:T(8,128)(2,1)}, bf16[8,128,512]{2,1,0:T(8,128)(2,1)S(1)}, u32[]{:S(2)}, u32[]{:S(2)}) collective-permute-start(bf16[8,128,512]{2,1,0:T(8,128)(2,1)} %v_any.1), channel_id=1, source_target_pairs={{0,2},{2,0},{4,6},{6,4},{8,10},{10,8},{12,14},{14,12},{1,3},{3,1},... | collective-permute-start | bytes 3145736 | tf_op jit(solution)/shard_map/ppermute | solution.py:526
  0.5 22.5 %collective-permute-start.1 = (bf16[3,8,8192]{2,1,0:T(8,128)(2,1)}, bf16[3,8,8192]{2,1,0:T(8,128)(2,1)S(1)}, u32[]{:S(2)}, u32[]{:S(2)}) collective-permute-start(bf16[3,8,8192]{2,1,0:T(8,128)(2,1)} %bitcast.6), channel_id=1, source_target_pairs={{0,12},{2,14},{4,8},{6,10},{8,4},{10,6},{12,0},{14,2},{1,13},{3,15... | collective-permute-start | bytes 1179656 | tf_op jit(solution)/shard_map/ppermute | solution.py:526
  5.6 1.1 %collective-permute-start = (s32[8]{0:T(128)S(1)}, s32[8]{0:T(128)S(1)}, u32[]{:S(2)}, u32[]{:S(2)}) collective-permute-start(s32[8]{0:T(128)S(1)} %copy-done.7), channel_id=1, source_target_pairs={{0,2},{2,0},{4,6},{6,4},{8,10},{10,8},{12,14},{14,12},{1,3},{3,1},... | collective-permute-start | bytes 104 | tf_op jit(solution)/shard_map/ppermute | solution.py:526
  6.3 9.2 %collective-permute-start.2 = (s32[3,8]{1,0:T(4,128)S(1)}, s32[3,8]{1,0:T(4,128)S(1)}, u32[]{:S(2)}, u32[]{:S(2)}) collective-permute-start(s32[3,8]{1,0:T(4,128)S(1)} %add_bitcast_fusion.table_ref), channel_id=1, source_target_pairs={{0,4},{2,6},{4,0},{6,2},{8,12},{10,14},{12,8},{14,10},{1,5},{3,7},... | collective-permute-start | bytes 296 | tf_op jit(solution)/shard_map/ppermute | solution.py:526
  6.7 9.2 %collective-permute-start.3 = (s32[3,8]{1,0:T(4,128)S(1)}, s32[3,8]{1,0:T(4,128)S(1)}, u32[]{:S(2)}, u32[]{:S(2)}) collective-permute-start(s32[3,8]{1,0:T(4,128)S(1)} %add_bitcast_fusion.table_ref), channel_id=1, source_target_pairs={{0,12},{2,14},{4,8},{6,10},{8,4},{10,6},{12,0},{14,2},{1,13},{3,15... | collective-permute-start | bytes 296 | tf_op jit(solution)/shard_map/ppermute | solution.py:526
  7.7 15.3 %collective-permute-start.4 = (s32[3,8]{1,0:T(4,128)S(1)}, s32[3,8]{1,0:T(4,128)S(1)}, u32[]{:S(2)}, u32[]{:S(2)}) collective-permute-start(s32[3,8]{1,0:T(4,128)S(1)} %add_bitcast_fusion.table_ref), channel_id=1, source_target_pairs={{0,8},{2,10},{4,12},{6,14},{8,0},{10,2},{12,4},{14,6},{1,9},{3,11}... | collective-permute-start | bytes 296 | tf_op jit(solution)/shard_map/ppermute | solution.py:526
  9.8 14.0 %collective-permute-start.7 = (bf16[3,8,8192]{2,1,0:T(8,128)(2,1)}, bf16[3,8,8192]{2,1,0:T(8,128)(2,1)S(1)}, u32[]{:S(2)}, u32[]{:S(2)}) collective-permute-start(bf16[3,8,8192]{2,1,0:T(8,128)(2,1)} %bitcast.7), channel_id=1, source_target_pairs={{0,4},{2,6},{4,0},{6,2},{8,12},{10,14},{12,8},{14,10},{1,5},{3,7},... | collective-permute-start | bytes 1179656 | tf_op jit(solution)/shard_map/ppermute | solution.py:526
  11.1 1.2 %copy-start = (bf16[8,128,512]{2,1,0:T(8,128)(2,1)S(1)}, bf16[8,128,512]{2,1,0:T(8,128)(2,1)}, u32[]{:S(2)}) copy-start(bf16[8,128,512]{2,1,0:T(8,128)(2,1)} %k_any) | copy-start | bytes 3145732
  12.3 1.2 %copy-start.1 = (bf16[8,128,512]{2,1,0:T(8,128)(2,1)S(1)}, bf16[8,128,512]{2,1,0:T(8,128)(2,1)}, u32[]{:S(2)}) copy-start(bf16[8,128,512]{2,1,0:T(8,128)(2,1)} %v_any.1) | copy-start | bytes 3145732
  23.0 9.9 %collective-permute-start.8 = (bf16[3,8,8192]{2,1,0:T(8,128)(2,1)S(1)}, bf16[3,8,8192]{2,1,0:T(8,128)(2,1)S(1)}, u32[]{:S(2)}, u32[]{:S(2)}) collective-permute-start(bf16[3,8,8192]{2,1,0:T(8,128)(2,1)S(1)} %collective-permute-done.1.q_ref), channel_id=1, source_target_pairs={{0,4},{2,6},{4,0},{6,2},{8,12},{10,14},{12,8},{14,10},{1,5},{3,7},... | collective-permute-start | bytes 1179656 | tf_op jit(solution)/shard_map/ppermute | solution.py:526
  34.9 9.3 %collective-permute-start.9 = (bf16[1584,128]{1,0:T(8,128)(2,1)S(1)}, bf16[1584,128]{1,0:T(8,128)(2,1)S(1)}, u32[]{:S(2)}, u32[]{:S(2)}) collective-permute-start(bf16[1584,128]{1,0:T(8,128)(2,1)S(1)} %shard_map.111), channel_id=1, source_target_pairs={{0,4},{2,6},{4,0},{6,2},{8,12},{10,14},{12,8},{14,10},{1,5},{3,7},... | collective-permute-start | bytes 1216520 | tf_op jit(solution)/shard_map/ppermute | solution.py:526
  36.0 12.4 %copy-start.3 = (bf16[8,128,512]{2,1,0:T(8,128)(2,1)S(1)}, bf16[8,128,512]{2,1,0:T(8,128)(2,1)}, u32[]{:S(2)}) copy-start(bf16[8,128,512]{2,1,0:T(8,128)(2,1)} %leaf_v_any.1) | copy-start | bytes 3145732
  38.0 10.4 %copy-start.2 = (bf16[8,128,512]{2,1,0:T(8,128)(2,1)S(1)}, bf16[8,128,512]{2,1,0:T(8,128)(2,1)}, u32[]{:S(2)}) copy-start(bf16[8,128,512]{2,1,0:T(8,128)(2,1)} %leaf_k_any.1) | copy-start | bytes 3145732
  38.1 10.4 %copy-start.4 = (bf16[8,3,8192]{2,0,1:T(8,128)(2,1)S(1)}, bf16[8,3,8192]{2,0,1:T(8,128)(2,1)}, u32[]{:S(2)}) copy-start(bf16[8,3,8192]{2,0,1:T(8,128)(2,1)} %param.11) | copy-start | bytes 1179652
  38.1 10.4 %copy-start.5 = (bf16[8,3,512]{2,0,1:T(8,128)(2,1)S(1)}, bf16[8,3,512]{2,0,1:T(8,128)(2,1)}, u32[]{:S(2)}) copy-start(bf16[8,3,512]{2,0,1:T(8,128)(2,1)} %param.18) | copy-start | bytes 73732
  38.1 10.4 %copy-start.6 = (bf16[8,3,512]{2,0,1:T(8,128)(2,1)S(1)}, bf16[8,3,512]{2,0,1:T(8,128)(2,1)}, u32[]{:S(2)}) copy-start(bf16[8,3,512]{2,0,1:T(8,128)(2,1)} %param.19) | copy-start | bytes 73732
  44.8 11.6 %collective-permute-start.10 = (bf16[1584,128]{1,0:T(8,128)(2,1)S(1)}, bf16[1584,128]{1,0:T(8,128)(2,1)S(1)}, u32[]{:S(2)}, u32[]{:S(2)}) collective-permute-start(bf16[1584,128]{1,0:T(8,128)(2,1)S(1)} %shard_map.112), channel_id=1, source_target_pairs={{0,4},{2,6},{4,0},{6,2},{8,12},{10,14},{12,8},{14,10},{1,5},{3,7},... | collective-permute-start | bytes 1216520 | tf_op jit(solution)/shard_map/ppermute | solution.py:526
  46.6 17.3 %collective-permute-start.11 = (bf16[1584,128]{1,0:T(8,128)(2,1)S(1)}, bf16[1584,128]{1,0:T(8,128)(2,1)S(1)}, u32[]{:S(2)}, u32[]{:S(2)}) collective-permute-start(bf16[1584,128]{1,0:T(8,128)(2,1)S(1)} %shard_map.113), channel_id=1, source_target_pairs={{0,12},{2,14},{4,8},{6,10},{8,4},{10,6},{12,0},{14,2},{1,13},{3,15... | collective-permute-start | bytes 1216520 | tf_op jit(solution)/shard_map/ppermute | solution.py:526
  48.5 0.7 %copy-start.8 = (s32[8]{0:T(128)S(1)}, s32[8]{0:T(128)}, u32[]{:S(2)}) copy-start(s32[8]{0:T(128)} %leaf_count_ref.1) | copy-start | bytes 100

commit v6 on v5

--- a/solution.py
+++ b/solution.py
@@ -284,9 +284,9 @@
     sz.spread(q_ref, wide)
     for tile_at, first, last in sz.tiles():
         tile = jnp.zeros((sz.rows, HD), jnp.float32)
-        for start in range(first, last, 4):
+        for start in range(first, last, 8):
             items = []
-            for request in range(start, min(last, start + 4)):
+            for request in range(start, min(last, start + 8)):
                 slot0, count0 = sz.find(table_ref, count0_ref, me, request)
                 slot1, count1 = sz.find(table_ref, count1_ref, mate, request)
                 allowed = jnp.concatenate([token_ids < count0, token_ids < count1], axis=1)

time: 65.6 us -> 65.5 us (level)
  no operation moved by 1% of the time
where the time goes in v6:
time: 65.5 us; the launch traced here: 65.3 us
  waiting for transfers between devices  30.9 us (47%)
  starting transfers between devices  15.3 us (23%)
  Pallas kernels  15.1 us (23%)
  local copies, waits for them, and re-layouts  3.11 us (5%)
  other arithmetic  0.7 us (1%)
    ppermute x12, waiting for transfers between devices, exchange(): return lax.ppermute(array, 'page', [(at, at ^ hop) for at in range(owners)])  30.9 us
    ppermute x12, starting transfers between devices, exchange(): return lax.ppermute(array, 'page', [(at, at ^ hop) for at in range(owners)])  15.3 us
    pallas_call x1, Pallas kernels, line_shards(): plain_call(functools.partial(local_kernel, whole, 0), exact(whole), [smem...  6.58 us
    pallas_call x3, Pallas kernels, shared(): plain_call(functools.partial(shared_kernel, size, chunk, is_exact), exact...  5.61 us
    unnamed x18, local copies, waits for them, and re-layouts  3.11 us
    pallas_call x1, Pallas kernels, line_shards(): plain_call(functools.partial(final_kernel, whole, sz), (shape((steps, req...  1.53 us
  transfers between devices with their start and end apart: 12, of which 9 were waited for; matrix products, arithmetic and copies ran while one was open for 1% of the time, Pallas kernels for 17%

profile of v6, /device:TPU:0, one launch (start us, length us, event | category | flops | bytes accessed | tf_op | source)
XLA Modules:
  0.0 65.3 jit_solution(11986221930741531981)
XLA Ops:
  0.0 0.5 collective-permute-start.5
  0.5 0.1 collective-permute-start.6
  0.5 5.0 %collective-permute-start.1 = (bf16[3,8,8192]{2,1,0:T(8,128)(2,1)}, bf16[3,8,8192]{2,1,0:T(8,128)(2,1)S(1)}, u32[]{:S(2)}, u32[]{:S(2)}) collective-permute-start(bf16[3,8,8192]{2,1,0:T(8,128)(2,1)} %bitcast.6), channel_id=1, source_target_pairs={{0,12},{2,14},{4,8},{6,10},{8,4},{10,6},{12,0},{14,2},{1,13},{3,15... | collective-permute-start | bytes 1179656 | tf_op jit(solution)/shard_map/ppermute | solution.py:526
  5.6 0.7 %add_bitcast_fusion.table_ref = s32[3,8]{1,0:T(4,128)S(1)} fusion(s32[8,3]{0,1:T(4,128)} %param.21, s32[8,3]{0,1:T(4,128)} %param.20), kind=kLoop, calls=%fused_computation | loop fusion | flops 48 | bytes 288 | tf_op jit(solution)/shard_map/transpose | solution.py:549
  6.3 0.4 collective-permute-done.count1_ref
  6.7 1.0 %collective-permute-start.3 = (s32[3,8]{1,0:T(4,128)S(1)}, s32[3,8]{1,0:T(4,128)S(1)}, u32[]{:S(2)}, u32[]{:S(2)}) collective-permute-start(s32[3,8]{1,0:T(4,128)S(1)} %add_bitcast_fusion.table_ref), channel_id=1, source_target_pairs={{0,12},{2,14},{4,8},{6,10},{8,4},{10,6},{12,0},{14,2},{1,13},{3,15... | collective-permute-start | bytes 296 | tf_op jit(solution)/shard_map/ppermute | solution.py:526
  7.7 2.1 %collective-permute-start.4 = (s32[3,8]{1,0:T(4,128)S(1)}, s32[3,8]{1,0:T(4,128)S(1)}, u32[]{:S(2)}, u32[]{:S(2)}) collective-permute-start(s32[3,8]{1,0:T(4,128)S(1)} %add_bitcast_fusion.table_ref), channel_id=1, source_target_pairs={{0,8},{2,10},{4,12},{6,14},{8,0},{10,2},{12,4},{14,6},{1,9},{3,11}... | collective-permute-start | bytes 296 | tf_op jit(solution)/shard_map/ppermute | solution.py:526
  9.8 1.3 %collective-permute-start.7 = (bf16[3,8,8192]{2,1,0:T(8,128)(2,1)}, bf16[3,8,8192]{2,1,0:T(8,128)(2,1)S(1)}, u32[]{:S(2)}, u32[]{:S(2)}) collective-permute-start(bf16[3,8,8192]{2,1,0:T(8,128)(2,1)} %bitcast.7), channel_id=1, source_target_pairs={{0,4},{2,6},{4,0},{6,2},{8,12},{10,14},{12,8},{14,10},{1,5},{3,7},... | collective-permute-start | bytes 1179656 | tf_op jit(solution)/shard_map/ppermute | solution.py:526
  11.1 1.2 %copy-done = bf16[8,128,512]{2,1,0:T(8,128)(2,1)S(1)} copy-done((bf16[8,128,512]{2,1,0:T(8,128)(2,1)S(1)}, bf16[8,128,512]{2,1,0:T(8,128)(2,1)}, u32[]{:S(2)}) %copy-start) | copy-done | bytes 1048600
  12.3 1.2 %copy-done.1 = bf16[8,128,512]{2,1,0:T(8,128)(2,1)S(1)} copy-done((bf16[8,128,512]{2,1,0:T(8,128)(2,1)S(1)}, bf16[8,128,512]{2,1,0:T(8,128)(2,1)}, u32[]{:S(2)}) %copy-start.1) | copy-done | bytes 1048600
  13.5 0.2 shard_map.109
  13.7 1.8 %collective-permute-done.2.table_ref = s32[3,8]{1,0:T(4,128)S(1)} collective-permute-done((s32[3,8]{1,0:T(4,128)S(1)}, s32[3,8]{1,0:T(4,128)S(1)}, u32[]{:S(2)}, u32[]{:S(2)}) %collective-permute-start.2) | collective-permute-done | bytes 128 | tf_op jit(solution)/shard_map/ppermute | solution.py:526
  15.5 0.4 collective-permute-done.3.table_ref
  15.9 7.1 %collective-permute-done.4.table_ref = s32[3,8]{1,0:T(4,128)S(1)} collective-permute-done((s32[3,8]{1,0:T(4,128)S(1)}, s32[3,8]{1,0:T(4,128)S(1)}, u32[]{:S(2)}, u32[]{:S(2)}) %collective-permute-start.4) | collective-permute-done | bytes 128 | tf_op jit(solution)/shard_map/ppermute | solution.py:526
  23.0 0.4 collective-permute-start.8
  23.4 0.4 collective-permute-done.7.q_ref
  23.8 1.9 %shard_map.110 = (f32[1536,128]{1,0:T(8,128)S(1)}, f32[48,128]{1,0:T(8,128)S(1)}) custom-call(s32[3,8]{1,0:T(4,128)S(1)} %collective-permute-done.3.table_ref, s32[8]{0:T(128)S(1)} %copy-done.7, s32[8]{0:T(128)S(1)} %collective-permute-done.count1_ref, bf16[3,8,8192]{2,1,0:T(8,128)(2,1)S(1)} %collective-permute-done.1.q_ref, ...), custom_call_target="tpu_custom_call" | custom-call | tf_op jit(solution)/shard_map/pallas_call | solution.py:569
  25.7 7.2 %collective-permute-done.8.q_ref = bf16[3,8,8192]{2,1,0:T(8,128)(2,1)S(1)} collective-permute-done((bf16[3,8,8192]{2,1,0:T(8,128)(2,1)S(1)}, bf16[3,8,8192]{2,1,0:T(8,128)(2,1)S(1)}, u32[]{:S(2)}, u32[]{:S(2)}) %collective-permute-start.8) | collective-permute-done | bytes 393248 | tf_op jit(solution)/shard_map/ppermute | solution.py:526
  32.8 1.9 %shard_map.111 = bf16[1584,128]{1,0:T(8,128)(2,1)S(1)} custom-call(s32[3,8]{1,0:T(4,128)S(1)} %collective-permute-done.4.table_ref, s32[8]{0:T(128)S(1)} %copy-done.7, s32[8]{0:T(128)S(1)} %collective-permute-done.count1_ref, bf16[3,8,8192]{2,1,0:T(8,128)(2,1)S(1)} %collective-permute-done.8.q_ref, bf16[8,128,512]{2,1,0:T(8,128)(2,1)S(1)} %get-tuple-element.27.k0, ...), custom_call_target="tpu_custom_call" | custom-call | tf_op jit(solution)/shard_map/pallas_call | solution.py:569
  34.7 1.2 %collective-permute-start.9 = (bf16[1584,128]{1,0:T(8,128)(2,1)S(1)}, bf16[1584,128]{1,0:T(8,128)(2,1)S(1)}, u32[]{:S(2)}, u32[]{:S(2)}) collective-permute-start(bf16[1584,128]{1,0:T(8,128)(2,1)S(1)} %shard_map.111), channel_id=1, source_target_pairs={{0,4},{2,6},{4,0},{6,2},{8,12},{10,14},{12,8},{14,10},{1,5},{3,7},... | collective-permute-start | bytes 1216520 | tf_op jit(solution)/shard_map/ppermute | solution.py:526
  35.9 1.9 %shard_map.112 = bf16[1584,128]{1,0:T(8,128)(2,1)S(1)} custom-call(s32[3,8]{1,0:T(4,128)S(1)} %collective-permute-done.2.table_ref, s32[8]{0:T(128)S(1)} %copy-done.7, s32[8]{0:T(128)S(1)} %collective-permute-done.count1_ref, bf16[3,8,8192]{2,1,0:T(8,128)(2,1)S(1)} %collective-permute-done.7.q_ref, bf16[8,128,512]{2,1,0:T(8,128)(2,1)S(1)} %get-tuple-element.27.k0, ...), custom_call_target="tpu_custom_call" | custom-call | tf_op jit(solution)/shard_map/pallas_call | solution.py:569
  37.8 0.0 copy-start.2
  37.8 6.2 %collective-permute-done.9.came_ref = bf16[1584,128]{1,0:T(8,128)(2,1)S(1)} collective-permute-done((bf16[1584,128]{1,0:T(8,128)(2,1)S(1)}, bf16[1584,128]{1,0:T(8,128)(2,1)S(1)}, u32[]{:S(2)}, u32[]{:S(2)}) %collective-permute-start.9) | collective-permute-done | bytes 405536 | tf_op jit(solution)/shard_map/ppermute | solution.py:526
  44.0 0.6 shard_map.113
  44.6 1.8 %collective-permute-start.10 = (bf16[1584,128]{1,0:T(8,128)(2,1)S(1)}, bf16[1584,128]{1,0:T(8,128)(2,1)S(1)}, u32[]{:S(2)}, u32[]{:S(2)}) collective-permute-start(bf16[1584,128]{1,0:T(8,128)(2,1)S(1)} %shard_map.112), channel_id=1, source_target_pairs={{0,4},{2,6},{4,0},{6,2},{8,12},{10,14},{12,8},{14,10},{1,5},{3,7},... | collective-permute-start | bytes 1216520 | tf_op jit(solution)/shard_map/ppermute | solution.py:526
  46.4 1.9 %collective-permute-start.11 = (bf16[1584,128]{1,0:T(8,128)(2,1)S(1)}, bf16[1584,128]{1,0:T(8,128)(2,1)S(1)}, u32[]{:S(2)}, u32[]{:S(2)}) collective-permute-start(bf16[1584,128]{1,0:T(8,128)(2,1)S(1)} %shard_map.113), channel_id=1, source_target_pairs={{0,12},{2,14},{4,8},{6,10},{8,4},{10,6},{12,0},{14,2},{1,13},{3,15... | collective-permute-start | bytes 1216520 | tf_op jit(solution)/shard_map/ppermute | solution.py:526
  48.3 0.6 copy-done.8
  49.0 6.6 %shard_map.114 = (f32[1536,128]{1,0:T(8,128)S(1)}, f32[48,128]{1,0:T(8,128)S(1)}) custom-call(s32[3,8]{1,0:T(4,128)S(1)} %add_bitcast_fusion.table_ref, s32[8]{0:T(128)S(1)} %copy-done.7, s32[8]{0:T(128)S(1)} %collective-permute-done.count1_ref, s32[8]{0:T(128)S(1)} %copy-done.8, bf16[3,8,8192]{2,1,0:T(8,128)(2,1)S(1)} %bitcast.8, ...), custom_call_target="tpu_custom_call" | custom-call | tf_op jit(solution)/shard_map/pallas_call | solution.py:590
  55.6 0.7 %collective-permute-done.10.came_ref = bf16[1584,128]{1,0:T(8,128)(2,1)S(1)} collective-permute-done((bf16[1584,128]{1,0:T(8,128)(2,1)S(1)}, bf16[1584,128]{1,0:T(8,128)(2,1)S(1)}, u32[]{:S(2)}, u32[]{:S(2)}) %collective-permute-start.10) | collective-permute-done | bytes 405536 | tf_op jit(solution)/shard_map/ppermute | solution.py:526
  56.3 0.6 shard_map.115
  56.9 6.8 %collective-permute-done.11.refs_0_ = bf16[1584,128]{1,0:T(8,128)(2,1)S(1)} collective-permute-done((bf16[1584,128]{1,0:T(8,128)(2,1)S(1)}, bf16[1584,128]{1,0:T(8,128)(2,1)S(1)}, u32[]{:S(2)}, u32[]{:S(2)}) %collective-permute-start.11) | collective-permute-done | bytes 405536 | tf_op jit(solution)/shard_map/ppermute | solution.py:526
  63.7 1.5 %shard_map.116 = bf16[3,8,8192]{2,1,0:T(8,128)(2,1)} custom-call(f32[1536,128]{1,0:T(8,128)S(1)} %get-tuple-element.45.num_ref, f32[48,128]{1,0:T(8,128)S(1)} %get-tuple-element.46.stat_ref, bf16[1584,128]{1,0:T(8,128)(2,1)S(1)} %collective-permute-done.11.refs_0_), custom_call_target="tpu_custom_call" | custom-call | tf_op jit(solution)/shard_map/pallas_call | solution.py:609
  (19 shorter events, 0.0 us)
Async XLA Ops:
  0.0 5.6 %copy-start.7 = (s32[8]{0:T(128)S(1)}, s32[8]{0:T(128)}, u32[]{:S(2)}) copy-start(s32[8]{0:T(128)} %count0_ref.7) | copy-start | bytes 100
  0.0 7.7 %collective-permute-start.5 = (bf16[8,128,512]{2,1,0:T(8,128)(2,1)}, bf16[8,128,512]{2,1,0:T(8,128)(2,1)S(1)}, u32[]{:S(2)}, u32[]{:S(2)}) collective-permute-start(bf16[8,128,512]{2,1,0:T(8,128)(2,1)} %k_any), channel_id=1, source_target_pairs={{0,2},{2,0},{4,6},{6,4},{8,10},{10,8},{12,14},{14,12},{1,3},{3,1},... | collective-permute-start | bytes 3145736 | tf_op jit(solution)/shard_map/ppermute | solution.py:526
  0.5 9.3 %collective-permute-start.6 = (bf16[8,128,512]{2,1,0:T(8,128)(2,1)}, bf16[8,128,512]{2,1,0:T(8,128)(2,1)S(1)}, u32[]{:S(2)}, u32[]{:S(2)}) collective-permute-start(bf16[8,128,512]{2,1,0:T(8,128)(2,1)} %v_any.1), channel_id=1, source_target_pairs={{0,2},{2,0},{4,6},{6,4},{8,10},{10,8},{12,14},{14,12},{1,3},{3,1},... | collective-permute-start | bytes 3145736 | tf_op jit(solution)/shard_map/ppermute | solution.py:526
  0.5 22.5 %collective-permute-start.1 = (bf16[3,8,8192]{2,1,0:T(8,128)(2,1)}, bf16[3,8,8192]{2,1,0:T(8,128)(2,1)S(1)}, u32[]{:S(2)}, u32[]{:S(2)}) collective-permute-start(bf16[3,8,8192]{2,1,0:T(8,128)(2,1)} %bitcast.6), channel_id=1, source_target_pairs={{0,12},{2,14},{4,8},{6,10},{8,4},{10,6},{12,0},{14,2},{1,13},{3,15... | collective-permute-start | bytes 1179656 | tf_op jit(solution)/shard_map/ppermute | solution.py:526
  5.6 1.1 %collective-permute-start = (s32[8]{0:T(128)S(1)}, s32[8]{0:T(128)S(1)}, u32[]{:S(2)}, u32[]{:S(2)}) collective-permute-start(s32[8]{0:T(128)S(1)} %copy-done.7), channel_id=1, source_target_pairs={{0,2},{2,0},{4,6},{6,4},{8,10},{10,8},{12,14},{14,12},{1,3},{3,1},... | collective-permute-start | bytes 104 | tf_op jit(solution)/shard_map/ppermute | solution.py:526
  6.3 9.2 %collective-permute-start.2 = (s32[3,8]{1,0:T(4,128)S(1)}, s32[3,8]{1,0:T(4,128)S(1)}, u32[]{:S(2)}, u32[]{:S(2)}) collective-permute-start(s32[3,8]{1,0:T(4,128)S(1)} %add_bitcast_fusion.table_ref), channel_id=1, source_target_pairs={{0,4},{2,6},{4,0},{6,2},{8,12},{10,14},{12,8},{14,10},{1,5},{3,7},... | collective-permute-start | bytes 296 | tf_op jit(solution)/shard_map/ppermute | solution.py:526
  6.7 9.2 %collective-permute-start.3 = (s32[3,8]{1,0:T(4,128)S(1)}, s32[3,8]{1,0:T(4,128)S(1)}, u32[]{:S(2)}, u32[]{:S(2)}) collective-permute-start(s32[3,8]{1,0:T(4,128)S(1)} %add_bitcast_fusion.table_ref), channel_id=1, source_target_pairs={{0,12},{2,14},{4,8},{6,10},{8,4},{10,6},{12,0},{14,2},{1,13},{3,15... | collective-permute-start | bytes 296 | tf_op jit(solution)/shard_map/ppermute | solution.py:526
  7.7 15.3 %collective-permute-start.4 = (s32[3,8]{1,0:T(4,128)S(1)}, s32[3,8]{1,0:T(4,128)S(1)}, u32[]{:S(2)}, u32[]{:S(2)}) collective-permute-start(s32[3,8]{1,0:T(4,128)S(1)} %add_bitcast_fusion.table_ref), channel_id=1, source_target_pairs={{0,8},{2,10},{4,12},{6,14},{8,0},{10,2},{12,4},{14,6},{1,9},{3,11}... | collective-permute-start | bytes 296 | tf_op jit(solution)/shard_map/ppermute | solution.py:526
  9.8 14.0 %collective-permute-start.7 = (bf16[3,8,8192]{2,1,0:T(8,128)(2,1)}, bf16[3,8,8192]{2,1,0:T(8,128)(2,1)S(1)}, u32[]{:S(2)}, u32[]{:S(2)}) collective-permute-start(bf16[3,8,8192]{2,1,0:T(8,128)(2,1)} %bitcast.7), channel_id=1, source_target_pairs={{0,4},{2,6},{4,0},{6,2},{8,12},{10,14},{12,8},{14,10},{1,5},{3,7},... | collective-permute-start | bytes 1179656 | tf_op jit(solution)/shard_map/ppermute | solution.py:526
  11.1 1.2 %copy-start = (bf16[8,128,512]{2,1,0:T(8,128)(2,1)S(1)}, bf16[8,128,512]{2,1,0:T(8,128)(2,1)}, u32[]{:S(2)}) copy-start(bf16[8,128,512]{2,1,0:T(8,128)(2,1)} %k_any) | copy-start | bytes 3145732
  12.3 1.2 %copy-start.1 = (bf16[8,128,512]{2,1,0:T(8,128)(2,1)S(1)}, bf16[8,128,512]{2,1,0:T(8,128)(2,1)}, u32[]{:S(2)}) copy-start(bf16[8,128,512]{2,1,0:T(8,128)(2,1)} %v_any.1) | copy-start | bytes 3145732
  23.0 9.9 %collective-permute-start.8 = (bf16[3,8,8192]{2,1,0:T(8,128)(2,1)S(1)}, bf16[3,8,8192]{2,1,0:T(8,128)(2,1)S(1)}, u32[]{:S(2)}, u32[]{:S(2)}) collective-permute-start(bf16[3,8,8192]{2,1,0:T(8,128)(2,1)S(1)} %collective-permute-done.1.q_ref), channel_id=1, source_target_pairs={{0,4},{2,6},{4,0},{6,2},{8,12},{10,14},{12,8},{14,10},{1,5},{3,7},... | collective-permute-start | bytes 1179656 | tf_op jit(solution)/shard_map/ppermute | solution.py:526
  34.7 9.3 %collective-permute-start.9 = (bf16[1584,128]{1,0:T(8,128)(2,1)S(1)}, bf16[1584,128]{1,0:T(8,128)(2,1)S(1)}, u32[]{:S(2)}, u32[]{:S(2)}) collective-permute-start(bf16[1584,128]{1,0:T(8,128)(2,1)S(1)} %shard_map.111), channel_id=1, source_target_pairs={{0,4},{2,6},{4,0},{6,2},{8,12},{10,14},{12,8},{14,10},{1,5},{3,7},... | collective-permute-start | bytes 1216520 | tf_op jit(solution)/shard_map/ppermute | solution.py:526
  35.9 12.4 %copy-start.3 = (bf16[8,128,512]{2,1,0:T(8,128)(2,1)S(1)}, bf16[8,128,512]{2,1,0:T(8,128)(2,1)}, u32[]{:S(2)}) copy-start(bf16[8,128,512]{2,1,0:T(8,128)(2,1)} %leaf_v_any.1) | copy-start | bytes 3145732
  37.8 10.6 %copy-start.2 = (bf16[8,128,512]{2,1,0:T(8,128)(2,1)S(1)}, bf16[8,128,512]{2,1,0:T(8,128)(2,1)}, u32[]{:S(2)}) copy-start(bf16[8,128,512]{2,1,0:T(8,128)(2,1)} %leaf_k_any.1) | copy-start | bytes 3145732
  37.8 10.6 %copy-start.4 = (bf16[8,3,8192]{2,0,1:T(8,128)(2,1)S(1)}, bf16[8,3,8192]{2,0,1:T(8,128)(2,1)}, u32[]{:S(2)}) copy-start(bf16[8,3,8192]{2,0,1:T(8,128)(2,1)} %param.11) | copy-start | bytes 1179652
  37.8 10.6 %copy-start.5 = (bf16[8,3,512]{2,0,1:T(8,128)(2,1)S(1)}, bf16[8,3,512]{2,0,1:T(8,128)(2,1)}, u32[]{:S(2)}) copy-start(bf16[8,3,512]{2,0,1:T(8,128)(2,1)} %param.18) | copy-start | bytes 73732
  37.8 10.5 %copy-start.6 = (bf16[8,3,512]{2,0,1:T(8,128)(2,1)S(1)}, bf16[8,3,512]{2,0,1:T(8,128)(2,1)}, u32[]{:S(2)}) copy-start(bf16[8,3,512]{2,0,1:T(8,128)(2,1)} %param.19) | copy-start | bytes 73732
  44.6 11.6 %collective-permute-start.10 = (bf16[1584,128]{1,0:T(8,128)(2,1)S(1)}, bf16[1584,128]{1,0:T(8,128)(2,1)S(1)}, u32[]{:S(2)}, u32[]{:S(2)}) collective-permute-start(bf16[1584,128]{1,0:T(8,128)(2,1)S(1)} %shard_map.112), channel_id=1, source_target_pairs={{0,4},{2,6},{4,0},{6,2},{8,12},{10,14},{12,8},{14,10},{1,5},{3,7},... | collective-permute-start | bytes 1216520 | tf_op jit(solution)/shard_map/ppermute | solution.py:526
  46.4 17.3 %collective-permute-start.11 = (bf16[1584,128]{1,0:T(8,128)(2,1)S(1)}, bf16[1584,128]{1,0:T(8,128)(2,1)S(1)}, u32[]{:S(2)}, u32[]{:S(2)}) collective-permute-start(bf16[1584,128]{1,0:T(8,128)(2,1)S(1)} %shard_map.113), channel_id=1, source_target_pairs={{0,12},{2,14},{4,8},{6,10},{8,4},{10,6},{12,0},{14,2},{1,13},{3,15... | collective-permute-start | bytes 1216520 | tf_op jit(solution)/shard_map/ppermute | solution.py:526
  48.3 0.7 %copy-start.8 = (s32[8]{0:T(128)S(1)}, s32[8]{0:T(128)}, u32[]{:S(2)}) copy-start(s32[8]{0:T(128)} %leaf_count_ref.1) | copy-start | bytes 100
